TPU v7x, 32 devices: a whole 2x2x4 slice. The times are simulated.
32 devices in a mesh: dp: 8 (over z, x), tensor: 4 (over y, core).
Axes of the slice: x: 2, y: 2, z: 4, core: 2. Of those that a mesh axis runs over, the one named last changes fastest.
Arguments:
- inputs: bfloat16 [8192, 2048], P('dp'), may hold values from -6 to 6
- segments: int32 [8, 1024], P('dp'), may hold values from 0 to 3, never falling along the last dimension, each value on 1 to 512 neighbouring positions
- decay_order: int32 [8], P('tensor'), may hold values from 0 to 7, each once
- ln1_gain: float32 [2048], replicated, may hold values from 0.1 to 1.9
- ln1_bias: float32 [2048], replicated, may hold values from -1.5 to 1.5
- w_query: bfloat16 [2048, 2048], P(None, 'tensor'), may hold values from -0.125 to 0.125
- w_key: bfloat16 [2048, 2048], P(None, 'tensor'), may hold values from -0.125 to 0.125
- w_value: bfloat16 [2048, 4096], P(None, 'tensor'), may hold values from -0.125 to 0.125
- w_swish: bfloat16 [2048, 4096], P(None, 'tensor'), may hold values from -0.125 to 0.125
- w_out: bfloat16 [4096, 2048], P('tensor'), may hold values from -0.1875 to 0.1875
- ln2_gain: float32 [2048], replicated, may hold values from 0.1 to 1.9
- ln2_bias: float32 [2048], replicated, may hold values from -1.5 to 1.5
- w_gate: bfloat16 [2048, 4096], P(None, 'tensor'), may hold values from -0.125 to 0.125
- w_up: bfloat16 [2048, 4096], P(None, 'tensor'), may hold values from -0.125 to 0.125
- w_down: bfloat16 [4096, 2048], P('tensor'), may hold values from -0.1875 to 0.1875
- cotangent: bfloat16 [8192, 2048], P('dp'), may hold values from -6 to 6
Outputs:
- output: bfloat16 [8192, 2048], P('dp')
- grad_inputs: float32 [8192, 2048], P('dp')
- grad_ln1_gain: float32 [2048], P('dp')
- grad_ln1_bias: float32 [2048], P('dp')
- grad_query: float32 [2048, 2048], P('dp', 'tensor')
- grad_key: float32 [2048, 2048], P('dp', 'tensor')
- grad_value: float32 [2048, 4096], P('dp', 'tensor')
- grad_swish: float32 [2048, 4096], P('dp', 'tensor')
- grad_out: float32 [4096, 2048], P('tensor', 'dp')
- grad_ln2_gain: float32 [2048], P('dp')
- grad_ln2_bias: float32 [2048], P('dp')
- grad_gate: float32 [2048, 4096], P('dp', 'tensor')
- grad_up: float32 [2048, 4096], P('dp', 'tensor')
- grad_down: float32 [4096, 2048], P('tensor', 'dp')
Inputs may be any that keep to these rules, and one draw needn't show every extreme that they name: `segments`: along each sequence the document number never falls; each document has 1 to 512 tokens. `decay_order`: every head has its own number.
All inputs are finite; a program needn't handle non-finite values.
Results may differ from a plain program's by a relative error of at most 0.017.
Values sent between devices are 32-bit elements; how exact they have to be, the bound alone decides.
A program may use at most 320 MiB of HBM per device.

v0:
```python
import jax
import jax.numpy as jnp
from jax import lax
from jax.sharding import PartitionSpec as P

KEY = 256
VALUE = 512
SEQ_LEN = 1024


def layer_norm(values, scales, shifts):
    average = jnp.mean(values, axis=-1, keepdims=True)
    centred = values - average
    spread = jnp.mean(centred * centred, axis=-1, keepdims=True)
    return centred * lax.rsqrt(spread + 1e-05) * scales + shifts


def head_norm(values):
    average = jnp.mean(values, axis=-1, keepdims=True)
    centred = values - average
    spread = jnp.mean(centred * centred, axis=-1, keepdims=True)
    return centred * lax.rsqrt(spread + 1.0)


def gate_apply(retained, switch):
    row_count = retained.shape[0]
    normed = head_norm(retained).reshape(row_count, -1)
    return normed * jax.nn.silu(switch)


def gelu_product(gate_proj, up_proj):
    return jax.nn.gelu(gate_proj) * up_proj


def rotate(values, cosines, sines, sign):
    full_width = values.shape[-1]
    parity = lax.broadcasted_iota(jnp.int32, (1, full_width), 1) % 2 == 0
    partner = jnp.where(parity, -jnp.roll(values, -1, axis=-1), jnp.roll(values, 1, axis=-1))
    return values * cosines + sign * partner * sines


def angle_tables(length, heads_here):
    half_width = KEY // 2
    column = jnp.arange(KEY, dtype=jnp.int32) // 2
    frequency = jnp.power(10000.0, -column.astype(jnp.float32) / (half_width - 1))
    position = jnp.arange(length, dtype=jnp.int32).astype(jnp.float32)
    angles = position[:, None] * frequency[None, :]
    return (jnp.tile(jnp.cos(angles), (1, heads_here)), jnp.tile(jnp.sin(angles), (1, heads_here)))


def decay_mask(seq_segments, decay_order, length):
    exponent = (decay_order + 5).astype(jnp.float32)
    log_keep = jnp.log1p(-jnp.exp2(-exponent))
    row_index = lax.broadcasted_iota(jnp.int32, (length, length), 0)
    col_index = lax.broadcasted_iota(jnp.int32, (length, length), 1)
    offset_gap = jnp.maximum(row_index - col_index, 0).astype(jnp.float32)
    decays = jnp.exp(offset_gap[None] * log_keep[:, None, None])
    same_doc = (seq_segments[:, :, None] == seq_segments[:, None, :]) & (row_index >= col_index)[
        None
    ]
    return jnp.where(same_doc[:, None], decays[None], jnp.zeros_like(decays[None]))


def product_tn(left, right):
    return lax.dot_general(
        left, right, (((0,), (0,)), ((), ())), preferred_element_type=jnp.float32
    )


def product_nt(left, right):
    return lax.dot_general(
        left, right, (((1,), (1,)), ((), ())), preferred_element_type=jnp.float32
    )


def product_nn(left, right):
    return jnp.dot(left, right, preferred_element_type=jnp.float32)


def on_device(
    inputs,
    segments,
    decay_order,
    ln1_gain,
    ln1_bias,
    w_query,
    w_key,
    w_value,
    w_swish,
    w_out,
    ln2_gain,
    ln2_bias,
    w_gate,
    w_up,
    w_down,
    cotangent,
):
    row_count = inputs.shape[0]
    seqs_here = row_count // SEQ_LEN
    heads_here = decay_order.shape[0]
    key_width = w_query.shape[1]
    value_width = w_value.shape[1]
    key_scale = float(KEY) ** (-0.5)
    cos_base, sin_base = angle_tables(SEQ_LEN, heads_here)
    cosines = jnp.tile(cos_base, (seqs_here, 1))
    sines = jnp.tile(sin_base, (seqs_here, 1))
    weights_mask = decay_mask(segments, decay_order, SEQ_LEN)
    residual_in = inputs.astype(jnp.float32)
    normed_one = layer_norm(residual_in, ln1_gain, ln1_bias).astype(jnp.bfloat16)
    query_proj = product_nn(normed_one, w_query)
    key_proj = product_nn(normed_one, w_key)
    switch = product_nn(normed_one, w_swish)
    value_low = product_nn(normed_one, w_value).astype(jnp.bfloat16)
    query_rot = rotate(query_proj, cosines, sines, 1.0).astype(jnp.bfloat16)
    key_rot = (rotate(key_proj, cosines, sines, 1.0) * key_scale).astype(jnp.bfloat16)
    query_four = query_rot.reshape(seqs_here, SEQ_LEN, heads_here, KEY)
    key_four = key_rot.reshape(seqs_here, SEQ_LEN, heads_here, KEY)
    value_four = value_low.reshape(seqs_here, SEQ_LEN, heads_here, VALUE)
    scores = jnp.einsum("snhk,smhk->shnm", query_four, key_four, preferred_element_type=jnp.float32)
    weighted = (scores * weights_mask).astype(jnp.bfloat16)
    retained = jnp.einsum(
        "shnm,smhv->snhv", weighted, value_four, preferred_element_type=jnp.float32
    )
    retained = retained.reshape(row_count, heads_here, VALUE)
    gated, gate_pull = jax.vjp(gate_apply, retained, switch)
    gated_low = gated.astype(jnp.bfloat16)
    branch = lax.psum(product_nn(gated_low, w_out), "tensor")
    middle = residual_in + branch
    normed_two = layer_norm(middle, ln2_gain, ln2_bias).astype(jnp.bfloat16)
    gate_proj = product_nn(normed_two, w_gate)
    up_proj = product_nn(normed_two, w_up)
    hidden, hidden_pull = jax.vjp(gelu_product, gate_proj, up_proj)
    hidden_low = hidden.astype(jnp.bfloat16)
    feed_out = lax.psum(product_nn(hidden_low, w_down), "tensor")
    output = (middle + feed_out).astype(jnp.bfloat16)
    grad_down = product_tn(hidden_low, cotangent)
    grad_hidden = product_nt(cotangent, w_down)
    grad_gate_proj, grad_up_proj = hidden_pull(grad_hidden)
    gate_back = grad_gate_proj.astype(jnp.bfloat16)
    up_back = grad_up_proj.astype(jnp.bfloat16)
    grad_gate = product_tn(normed_two, gate_back)
    grad_up = product_tn(normed_two, up_back)
    grad_normed_two = lax.psum(product_nt(gate_back, w_gate) + product_nt(up_back, w_up), "tensor")
    second_value, second_pull = jax.vjp(layer_norm, middle, ln2_gain, ln2_bias)
    grad_mid_norm, grad_ln2_gain, grad_ln2_bias = second_pull(grad_normed_two)
    grad_middle = cotangent.astype(jnp.float32) + grad_mid_norm
    branch_back = grad_middle.astype(jnp.bfloat16)
    grad_out = product_tn(gated_low, branch_back)
    grad_gated = product_nt(branch_back, w_out)
    grad_retained, grad_switch = gate_pull(grad_gated)
    retained_back = grad_retained.astype(jnp.bfloat16).reshape(
        seqs_here, SEQ_LEN, heads_here, VALUE
    )
    switch_back = grad_switch.astype(jnp.bfloat16)
    grad_weighted = jnp.einsum(
        "snhv,smhv->shnm", retained_back, value_four, preferred_element_type=jnp.float32
    )
    scores_back = (grad_weighted * weights_mask).astype(jnp.bfloat16)
    value_back = jnp.einsum(
        "shnm,snhv->smhv", weighted, retained_back, preferred_element_type=jnp.float32
    )
    value_back = value_back.reshape(row_count, value_width).astype(jnp.bfloat16)
    query_rot_back = jnp.einsum(
        "shnm,smhk->snhk", scores_back, key_four, preferred_element_type=jnp.float32
    )
    key_rot_back = jnp.einsum(
        "shnm,snhk->smhk", scores_back, query_four, preferred_element_type=jnp.float32
    )
    query_back = rotate(query_rot_back.reshape(row_count, key_width), cosines, sines, -1.0).astype(
        jnp.bfloat16
    )
    key_back = (
        rotate(key_rot_back.reshape(row_count, key_width), cosines, sines, -1.0) * key_scale
    ).astype(jnp.bfloat16)
    grad_query = product_tn(normed_one, query_back)
    grad_key = product_tn(normed_one, key_back)
    grad_value = product_tn(normed_one, value_back)
    grad_swish = product_tn(normed_one, switch_back)
    partial_one = product_nt(query_back, w_query) + product_nt(key_back, w_key)
    partial_one = partial_one + product_nt(value_back, w_value) + product_nt(switch_back, w_swish)
    grad_normed_one = lax.psum(partial_one, "tensor")
    first_value, first_pull = jax.vjp(layer_norm, residual_in, ln1_gain, ln1_bias)
    grad_in_norm, grad_ln1_gain, grad_ln1_bias = first_pull(grad_normed_one)
    grad_inputs = grad_middle + grad_in_norm
    summed = (
        lax.psum_scatter(grad_ln1_gain, "dp", scatter_dimension=0, tiled=True),
        lax.psum_scatter(grad_ln1_bias, "dp", scatter_dimension=0, tiled=True),
        lax.psum_scatter(grad_query, "dp", scatter_dimension=0, tiled=True),
        lax.psum_scatter(grad_key, "dp", scatter_dimension=0, tiled=True),
        lax.psum_scatter(grad_value, "dp", scatter_dimension=0, tiled=True),
        lax.psum_scatter(grad_swish, "dp", scatter_dimension=0, tiled=True),
        lax.psum_scatter(grad_out, "dp", scatter_dimension=1, tiled=True),
        lax.psum_scatter(grad_ln2_gain, "dp", scatter_dimension=0, tiled=True),
        lax.psum_scatter(grad_ln2_bias, "dp", scatter_dimension=0, tiled=True),
        lax.psum_scatter(grad_gate, "dp", scatter_dimension=0, tiled=True),
        lax.psum_scatter(grad_up, "dp", scatter_dimension=0, tiled=True),
        lax.psum_scatter(grad_down, "dp", scatter_dimension=1, tiled=True),
    )
    return (
        output,
        grad_inputs,
        summed[0],
        summed[1],
        summed[2],
        summed[3],
        summed[4],
        summed[5],
        summed[6],
        summed[7],
        summed[8],
        summed[9],
        summed[10],
        summed[11],
    )


def solution(mesh):
    return jax.shard_map(
        on_device,
        mesh=mesh,
        in_specs=(
            P("dp", None),
            P("dp", None),
            P("tensor"),
            P(),
            P(),
            P(None, "tensor"),
            P(None, "tensor"),
            P(None, "tensor"),
            P(None, "tensor"),
            P("tensor", None),
            P(),
            P(),
            P(None, "tensor"),
            P(None, "tensor"),
            P("tensor", None),
            P("dp", None),
        ),
        out_specs=(
            P("dp", None),
            P("dp", None),
            P("dp"),
            P("dp"),
            P("dp", "tensor"),
            P("dp", "tensor"),
            P("dp", "tensor"),
            P("dp", "tensor"),
            P("tensor", "dp"),
            P("dp"),
            P("dp"),
            P("dp", "tensor"),
            P("dp", "tensor"),
            P("tensor", "dp"),
        ),
        check_vma=False,
    )
```

profile of v0, /device:TPU:0, one launch (start us, length us, event | category | flops | bytes accessed | tf_op | source)
XLA Modules:
  0.0 1909.8 jit_solution(12793942768969955812)
XLA Ops:
  21.6 8.9 convolution_convert_fusion.1
  49.1 7.4 multiply_convert_fusion.4
  56.5 8.6 fusion.73
  65.2 155.7 %all-reduce.10.cloned.1.call-done = f32[1024,2048]{1,0:T(8,128)} async-done(((f32[1024,2048]{1,0:T(8,128)}), f32[1024,2048]{1,0:T(8,128)}) %all-reduce.10.cloned.1.call-update) | async-done | bytes 8388624 | tf_op jit(solution)/shard_map/psum | solution.py:127
  242.7 11.1 multiply_convert_fusion.2
  253.8 6.9 fusion.77
  267.7 10.7 fusion.76
  278.4 142.5 %all-reduce.12.cloned.1.call-done = f32[1024,2048]{1,0:T(8,128)} async-done(((f32[1024,2048]{1,0:T(8,128)}), f32[1024,2048]{1,0:T(8,128)}) %all-reduce.12.cloned.1.call-update) | async-done | bytes 8388624 | tf_op jit(solution)/shard_map/psum | solution.py:143
  420.9 8.1 multiply_reduce_fusion
  429.1 7.0 fusion.61
  436.1 7.7 fusion.11
  443.8 11.0 fusion.24
  486.2 7.2 fusion.82
  500.2 12.1 add_add_fusion.3
  529.5 9.0 fusion.89
  540.1 9.2 fusion.88
  550.9 8.9 fusion.90
  561.4 9.1 fusion.87
  572.1 9.1 fusion.85
  582.8 9.1 fusion.86
  593.8 207.6 %all-reduce.14.cloned.1.call-done = (f32[1024,2048]{1,0:T(8,128)}, f32[1024,2048]{1,0:T(8,128)}) async-done(((f32[1024,2048]{1,0:T(8,128)}, f32[1024,2048]{1,0:T(8,128)}), (f32[1024,2048]{1,0:T(8,128)}, f32[1024,2048]{1,0:T(8,128)})) %all-reduce.14.cloned.1.call-update) | async-done | bytes 16777232 | tf_op jit(solution)/shard_map/psum | solution.py:134
  813.7 39.1 %all-reduce.4 = (f32[2048]{0:T(1024)S(1)}, f32[2048]{0:T(1024)S(1)}, f32[2048]{0:T(1024)S(1)}, f32[2048]{0:T(1024)S(1)}) all-reduce(f32[2048]{0:T(1024)S(1)} %get-tuple-element.16, f32[2048]{0:T(1024)S(1)} %get-tuple-element.19, f32[2048]{0:T(1024)S(1)} %copy-done.46, ...), channel_id=2, replica_groups=mesh['dp'=8,'tensor'=4] {'dp'}, use_global_device_ids=true, to_apply=%region_17.18.clone | all-reduce | flops 8192 | bytes 65536
  855.4 9.7 add_convert_fusion
  865.0 11.5 add_add_fusion.2
  876.5 18.1 reduce-scatter.11.cloned.1.call-done
  894.6 92.3 %reduce-scatter.9.cloned.1.call-done = f32[256,512]{1,0:T(8,128)} async-done(((f32[2048,512]{1,0:T(8,128)}), f32[256,512]{1,0:T(8,128)}) %reduce-scatter.9.cloned.1.call-update) | async-done | bytes 524304 | tf_op jit(solution)/shard_map/reduce_scatter | solution.py:188
  986.9 152.9 %reduce-scatter.21.cloned.1.call-done = f32[256,1024]{1,0:T(8,128)} async-done(((f32[2048,1024]{1,0:T(8,128)}), f32[256,1024]{1,0:T(8,128)}) %reduce-scatter.21.cloned.1.call-update) | async-done | bytes 1048592 | tf_op jit(solution)/shard_map/reduce_scatter | solution.py:196
  1139.8 152.7 %reduce-scatter.19.cloned.1.call-done = f32[256,1024]{1,0:T(8,128)} async-done(((f32[2048,1024]{1,0:T(8,128)}), f32[256,1024]{1,0:T(8,128)}) %reduce-scatter.19.cloned.1.call-update) | async-done | bytes 1048592 | tf_op jit(solution)/shard_map/reduce_scatter | solution.py:195
  1292.4 152.6 %reduce-scatter.23.cloned.1.call-done = f32[1024,256]{1,0:T(8,128)} async-done(((f32[1024,2048]{1,0:T(8,128)}), f32[1024,256]{1,0:T(8,128)}) %reduce-scatter.23.cloned.1.call-update) | async-done | bytes 1048592 | tf_op jit(solution)/shard_map/reduce_scatter | solution.py:197
  1445.1 153.1 %reduce-scatter.17.cloned.1.call-done = f32[1024,256]{1,0:T(8,128)} async-done(((f32[1024,2048]{1,0:T(8,128)}), f32[1024,256]{1,0:T(8,128)}) %reduce-scatter.17.cloned.1.call-update) | async-done | bytes 1048592 | tf_op jit(solution)/shard_map/reduce_scatter | solution.py:192
  1598.2 152.1 %reduce-scatter.13.cloned.1.call-done = f32[256,1024]{1,0:T(8,128)} async-done(((f32[2048,1024]{1,0:T(8,128)}), f32[256,1024]{1,0:T(8,128)}) %reduce-scatter.13.cloned.1.call-update) | async-done | bytes 1048592 | tf_op jit(solution)/shard_map/reduce_scatter | solution.py:190
  1750.3 152.7 %reduce-scatter.15.cloned.1.call-done = f32[256,1024]{1,0:T(8,128)} async-done(((f32[2048,1024]{1,0:T(8,128)}), f32[256,1024]{1,0:T(8,128)}) %reduce-scatter.15.cloned.1.call-update) | async-done | bytes 1048592 | tf_op jit(solution)/shard_map/reduce_scatter | solution.py:191
  (213 shorter events, 140.4 us)
Async XLA Ops:
  7.2 10.2 copy-start
  7.2 213.7 %all-reduce.10.cloned.1.call-start = ((), (), s32[]{:S(2)}) async-start(), calls=%async_computation.8 | async-start | bytes 16777216 | tf_op jit(solution)/shard_map/psum | solution.py:127
  14.9 31.0 %copy-start.12 = (bf16[1024,2048]{1,0:T(8,128)(2,1)}, bf16[1024,2048]{1,0:T(8,128)(2,1)S(1)}, u32[]{:S(2)}) copy-start(bf16[1024,2048]{1,0:T(8,128)(2,1)S(1)} %fusion.7) | copy-start | bytes 12582916
  21.5 14.4 copy-start.34
  35.9 7.0 copy-start.59
  45.4 11.1 copy-start.6
  49.1 7.4 copy-start.15
  65.1 355.7 %all-reduce.12.cloned.1.call-start = ((), (), s32[]{:S(2)}) async-start(), calls=%async_computation.9 | async-start | bytes 16777216 | tf_op jit(solution)/shard_map/psum | solution.py:143
  267.7 533.8 %all-reduce.14.cloned.1.call-start = ((), (), s32[]{:S(2)}) async-start(), calls=%async_computation.18 | async-start | bytes 33554432 | tf_op jit(solution)/shard_map/psum | solution.py:134
  420.9 8.2 copy-start.10
  436.1 7.8 copy-start.42
  436.1 7.8 copy-start.7
  436.1 7.7 copy-start.9
  454.9 30.8 %copy-start.28 = (bf16[1024,1024]{0,1:T(8,128)(2,1)}, bf16[1024,1024]{0,1:T(8,128)(2,1)S(1)}, u32[]{:S(2)}) copy-start(bf16[1024,1024]{0,1:T(8,128)(2,1)S(1)} %get-tuple-element.62) | copy-start | bytes 6291460
  474.2 19.1 %copy-start.57 = (bf16[2,512,1024]{2,1,0:T(8,128)(2,1)}, bf16[2,512,1024]{2,1,0:T(8,128)(2,1)S(1)}, u32[]{:S(2)}) copy-start(bf16[2,512,1024]{2,1,0:T(8,128)(2,1)S(1)} %convolution_convert_fusion) | copy-start | bytes 6291460
  483.2 17.0 copy-start.20
  486.2 7.2 copy-start.55
  512.3 382.2 %reduce-scatter.11.cloned.1.call-start = ((), (), s32[]{:S(2)}) async-start(), calls=%async_computation.11 | async-start | bytes 4718592 | tf_op jit(solution)/shard_map/reduce_scatter | solution.py:189
  520.1 466.8 %reduce-scatter.9.cloned.1.call-start = ((), (), s32[]{:S(2)}) async-start(), calls=%async_computation.10 | async-start | bytes 4718592 | tf_op jit(solution)/shard_map/reduce_scatter | solution.py:188
  527.9 611.9 %reduce-scatter.21.cloned.1.call-start = ((), (), s32[]{:S(2)}) async-start(), calls=%async_computation.16 | async-start | bytes 9437184 | tf_op jit(solution)/shard_map/reduce_scatter | solution.py:196
  538.5 753.9 %reduce-scatter.19.cloned.1.call-start = ((), (), s32[]{:S(2)}) async-start(), calls=%async_computation.15 | async-start | bytes 9437184 | tf_op jit(solution)/shard_map/reduce_scatter | solution.py:195
  549.3 895.8 %reduce-scatter.23.cloned.1.call-start = ((), (), s32[]{:S(2)}) async-start(), calls=%async_computation.17 | async-start | bytes 9437184 | tf_op jit(solution)/shard_map/reduce_scatter | solution.py:197
  559.8 1038.4 %reduce-scatter.17.cloned.1.call-start = ((), (), s32[]{:S(2)}) async-start(), calls=%async_computation.14 | async-start | bytes 9437184 | tf_op jit(solution)/shard_map/reduce_scatter | solution.py:192
  570.5 1179.8 %reduce-scatter.13.cloned.1.call-start = ((), (), s32[]{:S(2)}) async-start(), calls=%async_computation.12 | async-start | bytes 9437184 | tf_op jit(solution)/shard_map/reduce_scatter | solution.py:190
  581.3 1321.7 %reduce-scatter.15.cloned.1.call-start = ((), (), s32[]{:S(2)}) async-start(), calls=%async_computation.13 | async-start | bytes 9437184 | tf_op jit(solution)/shard_map/reduce_scatter | solution.py:191
  591.9 209.5 %copy-start.36 = (f32[1024]{0:T(1024)S(1)}, f32[1024]{0:T(1024)}, u32[]{:S(2)}) copy-start(f32[1024]{0:T(1024)} %copy-done.35) | copy-start | bytes 12292
  591.9 209.5 %copy-start.38 = (f32[2048]{0:T(1024)S(1)}, f32[2048]{0:T(1024)}, u32[]{:S(2)}) copy-start(f32[2048]{0:T(1024)} %param.19) | copy-start | bytes 24580
  801.5 8.3 copy-start.8
  801.5 8.3 copy-start.41
  855.3 9.7 copy-start.5
  855.3 9.7 copy-start.43
  865.0 1038.0 %copy-start.1 = (bf16[2048,512]{1,0:T(8,128)(2,1)S(1)}, bf16[2048,512]{1,0:T(8,128)(2,1)}, u32[]{:S(2)}) copy-start(bf16[2048,512]{1,0:T(8,128)(2,1)} %param.21) | copy-start | bytes 6291460
  (45 other events, 146.0 us)
Sparse Core Ops, SparseCore 0:
  65.3 155.5 all-reduce.9
  267.8 152.9 all-reduce.11
  512.4 288.9 all-reduce.13
  805.5 89.0 reduce-scatter.10
  899.1 87.8 reduce-scatter.8
  991.0 148.7 reduce-scatter.20
  1144.4 147.9 reduce-scatter.18
  1296.6 148.3 reduce-scatter.22
  1449.7 148.4 reduce-scatter.16
  1602.2 148.0 reduce-scatter.12
  1754.9 148.0 reduce-scatter.14
where the time goes:
time: 1920 us; the launch traced here: 1910 us
  waiting for transfers between devices  1530 us (80%)
  matrix products  204 us (11%)
  other arithmetic  87.4 us (5%)
  blocking collectives  39.1 us (2%)
  local copies, waits for them, and re-layouts  30.4 us (2%)
    psum x1, waiting for transfers between devices, on_device(): feed_out = lax.psum(product_nn(hidden_low, w_down), 'tensor')  208 us
    psum x1, waiting for transfers between devices, on_device(): branch = lax.psum(product_nn(gated_low, w_out), 'tensor')  156 us
    reduce_scatter x1, waiting for transfers between devices, on_device(): lax.psum_scatter(grad_out, 'dp', scatter_dimension=1, tiled=True)  153 us
    reduce_scatter x1, waiting for transfers between devices, on_device(): lax.psum_scatter(grad_up, 'dp', scatter_dimension=0, tiled=True)  153 us
    reduce_scatter x1, waiting for transfers between devices, on_device(): lax.psum_scatter(grad_swish, 'dp', scatter_dimension=0, tiled=True)  153 us
    reduce_scatter x1, waiting for transfers between devices, on_device(): lax.psum_scatter(grad_gate, 'dp', scatter_dimension=0, tiled=True)  153 us
    reduce_scatter x1, waiting for transfers between devices, on_device(): lax.psum_scatter(grad_down, 'dp', scatter_dimension=1, tiled=True)  153 us
    reduce_scatter x1, waiting for transfers between devices, on_device(): lax.psum_scatter(grad_value, 'dp', scatter_dimension=0, tiled=True)  152 us
  transfers between devices with their start and end apart: 11, of which 11 were waited for; matrix products, arithmetic and copies ran while one was open for 6% of the time, Pallas kernels for 0%

commit v1 on v0

v1 whole, which is shorter than its diff:
```python
import functools

import jax
import jax.numpy as jnp
from jax import lax
from jax.experimental import pallas as pl
from jax.experimental.pallas import tpu as pltpu
from jax.sharding import PartitionSpec as P

KEY = 256
VALUE = 512
SEQ_LEN = 1024
DOC_MOST = 512
BLOCK = 256
CHUNKS = SEQ_LEN // BLOCK
HALF = BLOCK // 2
BF16 = jnp.bfloat16
F32 = jnp.float32
MIB = 1 << 20


def product_tn(left, right):
    return lax.dot_general(left, right, (((0,), (0,)), ((), ())), preferred_element_type=F32)


def product_nt(left, right):
    return lax.dot_general(left, right, (((1,), (1,)), ((), ())), preferred_element_type=F32)


def product_nn(left, right):
    return jnp.dot(left, right, preferred_element_type=F32)


def angle_tables(length):
    half_width = KEY // 2
    column = jnp.arange(KEY, dtype=jnp.int32) // 2
    frequency = jnp.power(10000.0, -column.astype(F32) / (half_width - 1))
    position = jnp.arange(length, dtype=jnp.int32).astype(F32)
    angles = position[:, None] * frequency[None, :]
    return jnp.cos(angles), jnp.sin(angles)


def rotate(values, cosines, sines, sign):
    even = lax.broadcasted_iota(jnp.int32, values.shape, 1) % 2 == 0
    after = pltpu.roll(values, KEY - 1, 1)
    before = pltpu.roll(values, 1, 1)
    return values * cosines + sign * jnp.where(even, -after, before) * sines


def normal_rows(values, eps):
    average = jnp.mean(values, axis=-1, keepdims=True)
    centred = values - average
    spread = jnp.mean(centred * centred, axis=-1, keepdims=True)
    return centred, lax.rsqrt(spread + eps)


def decay_block(log_keep, seg_rows, seg_columns, row_start, column_start):
    rows = row_start + lax.broadcasted_iota(jnp.int32, (BLOCK, BLOCK), 0)
    columns = column_start + lax.broadcasted_iota(jnp.int32, (BLOCK, BLOCK), 1)
    gap = rows - columns
    keep = (seg_rows == seg_columns) & (gap >= 0)
    return jnp.where(keep, jnp.exp(jnp.maximum(gap, 0).astype(F32) * log_keep), 0.0)


def first_key_block(chunk):
    return max(0, chunk - (DOC_MOST + BLOCK - 2) // BLOCK)


class Line:
    def __init__(self):
        self.last = []
        self.shared = 0

    def call(
        self,
        kernel,
        outs,
        out_specs,
        ins,
        in_specs,
        grid=(1,),
        scalars=None,
        scratch=(),
        vmem=63,
        onto=(),
        paired=False,
    ):
        extra = [array for _, array in onto] + self.last
        scalar_count = 0 if scalars is None else 1
        in_count = len(ins)
        skipped = len(extra)

        def body(*refs):
            head, rest = refs[: scalar_count + in_count], refs[scalar_count + in_count + skipped :]
            kernel(*head, *rest)

        specs = list(in_specs) + [pl.BlockSpec(memory_space=pl.ANY)] * skipped
        arguments = ([] if scalars is None else [scalars]) + list(ins) + extra
        extras = {}
        if paired:
            extras = dict(collective_id=self.shared, has_side_effects=True)
            self.shared += 1
        result = pl.pallas_call(
            body,
            out_shape=tuple(outs),
            grid_spec=pltpu.PrefetchScalarGridSpec(
                num_scalar_prefetch=scalar_count,
                grid=grid,
                in_specs=specs,
                out_specs=tuple(out_specs),
                scratch_shapes=list(scratch),
            ),
            input_output_aliases={scalar_count + in_count + n: out for n, (out, _) in enumerate(onto)},
            compiler_params=pltpu.CompilerParams(
                vmem_limit_bytes=vmem * MIB,
                dimension_semantics=("arbitrary",) * len(grid),
                **extras,
            ),
            cost_estimate=pl.CostEstimate(flops=1, bytes_accessed=1, transcendentals=0),
        )(*arguments)
        self.last = [result[0]]
        return result


def my_core():
    return lax.rem(lax.axis_index("tensor"), 2)


def other_core():
    rank = lax.axis_index("tensor")
    return {"tensor": rank + 1 - 2 * lax.rem(rank, 2)}


def meet_other_core():
    barrier = pltpu.get_barrier_semaphore()
    pl.semaphore_signal(barrier, inc=1, device_id=other_core(), device_id_type=pl.DeviceIdType.MESH)
    pl.semaphore_wait(barrier, 1)


def to_other_core(source, target, sent, arrived):
    return pltpu.make_async_remote_copy(
        src_ref=source,
        dst_ref=target,
        send_sem=sent,
        recv_sem=arrived,
        device_id=other_core(),
        device_id_type=pl.DeviceIdType.MESH,
    )


def core_rows(mine, block):
    core = my_core() if mine else 1 - my_core()
    return pl.ds(pl.multiple_of(block * BLOCK + core * HALF, HALF), HALF)


def shape(dims, kind):
    return jax.ShapeDtypeStruct(dims, kind)


def const_spec(dims):
    return pl.BlockSpec(dims, lambda *_: (0,) * len(dims))


def once_spec(dims):
    return pl.BlockSpec(dims, lambda *_: (0,) * len(dims), pipeline_mode=pl.Buffered(1))


def row_spec(rows, columns, chunk):
    return pl.BlockSpec((rows, columns), lambda *_: (chunk, 0))


SMEM = pl.BlockSpec(memory_space=pltpu.SMEM)


def proj_kernel(x, gain, bias, cos, sin, wq, wk, wv, ws, a_out, q_out, k_out, v_out, s_out):
    centred, scale = normal_rows(x[...].astype(F32), 1e-05)
    normed = (centred * scale * gain[...] + bias[...]).astype(BF16)
    a_out[...] = normed
    query = product_nn(normed, wq[...])
    key = product_nn(normed, wk[...])
    for first in range(0, query.shape[1], KEY):
        part = slice(first, first + KEY)
        q_out[:, part] = rotate(query[:, part], cos[...], sin[...], 1.0).astype(BF16)
        turned = rotate(key[:, part], cos[...], sin[...], 1.0) * float(KEY) ** (-0.5)
        k_out[:, part] = turned.astype(BF16)
    v_out[...] = product_nn(normed, wv[...]).astype(BF16)
    s_out[...] = product_nn(normed, ws[...])


def projections(line, x, gain, bias, cos, sin, wq, wk, wv, ws):
    rows, width = x.shape

    def rowed(columns):
        return pl.BlockSpec((BLOCK, columns), lambda i: (i, 0))

    kw, vw = wq.shape[1], wv.shape[1]
    return line.call(
        proj_kernel,
        [
            shape((rows, width), BF16),
            shape((rows, kw), BF16),
            shape((rows, kw), BF16),
            shape((rows, vw), BF16),
            shape((rows, vw), F32),
        ],
        [rowed(width), rowed(kw), rowed(kw), rowed(vw), rowed(vw)],
        [x, gain, bias, cos, sin, wq, wk, wv, ws],
        [
            rowed(width),
            const_spec((1, width)),
            const_spec((1, width)),
            rowed(KEY),
            rowed(KEY),
            once_spec(wq.shape),
            once_spec(wk.shape),
            once_spec(wv.shape),
            once_spec(ws.shape),
        ],
        grid=(rows // BLOCK,),
    )


TILES = 4


def retain_kernel(chunk, q, k, v, switch, seg_col, seg_row, logs, w, chip, u_out, o_out, p_out, full, sent, got, s1, s2):
    meet_other_core()
    heads = q.shape[1] // KEY
    low = first_key_block(chunk)
    for head in range(heads):
        kpart, vpart = slice(head * KEY, (head + 1) * KEY), slice(head * VALUE, (head + 1) * VALUE)
        total = None
        for block in range(low, chunk + 1):
            rows = slice(block * BLOCK, (block + 1) * BLOCK)
            raw = product_nt(q[:, kpart], k[rows, kpart])
            mask = decay_block(logs[head], seg_col[...], seg_row[:, rows], chunk * BLOCK, block * BLOCK)
            weights = (raw * mask).astype(BF16)
            p_out[head, :, (block - low) * BLOCK : (block - low + 1) * BLOCK] = weights
            part = product_nn(weights, v[rows, vpart])
            total = part if total is None else total + part
        o_out[:, vpart] = total
        centred, scale = normal_rows(total, 1.0)
        gate = switch[:, vpart]
        u_out[:, vpart] = (centred * scale * (gate * jax.nn.sigmoid(gate))).astype(BF16)
    tile = w.shape[1] // TILES
    copies = []
    for j in range(TILES):
        columns = slice(j * tile, (j + 1) * tile)
        full[:, columns] = product_nn(u_out[...], w[:, columns])
        sent[j] = full[core_rows(False, 0), columns]
        copies.append(to_other_core(sent.at[j], got.at[j], s1.at[j], s2.at[j]))
        copies[-1].start()
    for j in range(TILES):
        columns = slice(j * tile, (j + 1) * tile)
        copies[j].wait()
        chip[:, columns] = full[core_rows(True, 0), columns] + got[j]


def retention(line, chunk, q, k, v, switch, seg_col, seg_row, logs, w):
    kw, vw, width = q.shape[1], v.shape[1], w.shape[1]
    heads = kw // KEY
    blocks = chunk + 1 - first_key_block(chunk)
    return line.call(
        functools.partial(retain_kernel, chunk),
        [
            shape((HALF, width), F32),
            shape((BLOCK, vw), BF16),
            shape((BLOCK, vw), F32),
            shape((heads, BLOCK, blocks * BLOCK), BF16),
        ],
        [
            const_spec((HALF, width)),
            const_spec((BLOCK, vw)),
            const_spec((BLOCK, vw)),
            const_spec((heads, BLOCK, blocks * BLOCK)),
        ],
        [q, k, v, switch, seg_col, seg_row, logs, w],
        [
            row_spec(BLOCK, kw, chunk),
            const_spec(k.shape),
            const_spec(v.shape),
            row_spec(BLOCK, vw, chunk),
            row_spec(BLOCK, 1, chunk),
            const_spec(seg_row.shape),
            SMEM,
            const_spec(w.shape),
        ],
        scratch=[
            pltpu.VMEM((BLOCK, width), F32),
            pltpu.VMEM((TILES, HALF, width // TILES), F32),
            pltpu.VMEM((TILES, HALF, width // TILES), F32),
            pltpu.SemaphoreType.DMA((TILES,)),
            pltpu.SemaphoreType.DMA((TILES,)),
        ],
        paired=True,
    )


def feed_kernel(a, c, wg, wu, wd, hid_out, dg_out, du_out):
    gate = product_nn(a[...], wg[...])
    up = product_nn(a[...], wu[...])
    back = product_nt(c[...], wd[...])
    factor = 0.7978845608028654
    bent = jnp.tanh(factor * (gate + 0.044715 * (gate * gate * gate)))
    half = 0.5 * (1.0 + bent)
    active = gate * half
    slope = half + 0.5 * gate * (1.0 - bent * bent) * (factor * (1.0 + 3 * 0.044715 * gate * gate))
    hid_out[...] = (active * up).astype(BF16)
    dg_out[...] = (back * up * slope).astype(BF16)
    du_out[...] = (back * active).astype(BF16)


def feed_forward(line, chunk, rows, a, c, wg, wu, wd, before):
    width, ff = wg.shape
    tile = min(256, ff)
    whole = a.shape[0]
    return line.call(
        feed_kernel,
        [shape((whole, ff), BF16)] * 3,
        [pl.BlockSpec((rows, tile), lambda i: (chunk, i))] * 3,
        [a, c, wg, wu, wd],
        [
            row_spec(rows, width, chunk),
            row_spec(rows, width, chunk),
            pl.BlockSpec((width, tile), lambda i: (0, i)),
            pl.BlockSpec((width, tile), lambda i: (0, i)),
            pl.BlockSpec((tile, width), lambda i: (i, 0)),
        ],
        grid=(ff // tile,),
        onto=() if before is None else tuple(enumerate(before)),
    )


def chip_kernel(count, transposed, steps, *refs):
    lefts, rights = refs[:count], refs[count : 2 * count]
    out, full, kept, sent, got, s1, s2 = refs[2 * count :]
    half = kept.shape[1]
    j = pl.program_id(0)

    @pl.when(j == 0)
    def _():
        meet_other_core()

    @pl.when(j < steps)
    def _():
        total = None
        for left, right in zip(lefts, rights):
            part = product_nt(left[...], right[...]) if transposed else product_nn(left[...], right[...])
            total = part if total is None else total + part
        full[...] = total
        for n in range(half // HALF):
            part = slice(n * HALF, (n + 1) * HALF)
            sent[j, part] = full[core_rows(False, n), :]
            kept[j, part] = full[core_rows(True, n), :]
        to_other_core(sent.at[j], got.at[j], s1.at[j], s2.at[j]).start()

    @pl.when(j > 0)
    def _():
        to_other_core(sent.at[j - 1], got.at[j - 1], s1.at[j - 1], s2.at[j - 1]).wait()
        out[...] = kept[j - 1] + got[j - 1]


def chip_sum(line, rows, lefts, rights, transposed, chunk):
    width = rights[0].shape[0] if transposed else rights[0].shape[1]
    tile = 512
    steps = width // tile
    half = rows // 2
    right_specs = [
        pl.BlockSpec((tile, right.shape[1]), lambda i: (jnp.minimum(i, steps - 1), 0))
        if transposed
        else pl.BlockSpec((right.shape[0], tile), lambda i: (0, jnp.minimum(i, steps - 1)))
        for right in rights
    ]
    left_specs = [row_spec(rows, left.shape[1], chunk) for left in lefts]
    return line.call(
        functools.partial(chip_kernel, len(lefts), transposed, steps),
        [shape((half, width), F32)],
        [pl.BlockSpec((half, tile), lambda i: (0, jnp.maximum(i, 1) - 1))],
        list(lefts) + list(rights),
        left_specs + right_specs,
        grid=(steps + 1,),
        scratch=[
            pltpu.VMEM((rows, tile), F32),
            pltpu.VMEM((steps, half, tile), F32),
            pltpu.VMEM((steps, half, tile), F32),
            pltpu.VMEM((steps, half, tile), F32),
            pltpu.SemaphoreType.DMA((steps,)),
            pltpu.SemaphoreType.DMA((steps,)),
        ],
        paired=True,
    )[0]


def across_chips(values, size):
    return lax.ppermute(values, "tensor", [(i, i ^ 2) for i in range(size)])


def shared_kernel(work, in_count, *refs):
    ins, out = refs[:in_count], refs[in_count]
    extras, (sent, got, s1, s2) = refs[in_count + 1 : -4], refs[-4:]
    meet_other_core()
    copies = []
    for n in range(sent.shape[0] // HALF):
        part = pl.ds(n * HALF, HALF)
        value = work(n, part, core_rows(True, n), *ins, *extras)
        sent[part, :] = value
        copies.append(to_other_core(sent.at[part], got.at[part], s1.at[n], s2.at[n]))
        copies[-1].start()
        out[core_rows(True, n), :] = value.astype(out.dtype)
    for n, copy in enumerate(copies):
        copy.wait()
        out[core_rows(False, n), :] = got[pl.ds(n * HALF, HALF), :].astype(out.dtype)


def shared_rows(line, work, chunk, rows, ins, in_specs, kind, total_rows, width, extras, before):
    half = rows // 2
    return line.call(
        functools.partial(shared_kernel, work, len(ins)),
        [shape((total_rows, width), kind)] + [shape(dims, F32) for dims in extras],
        [row_spec(rows, width, chunk)] + [const_spec(dims) for dims in extras],
        ins,
        in_specs,
        scratch=[
            pltpu.VMEM((half, width), F32),
            pltpu.VMEM((half, width), F32),
            pltpu.SemaphoreType.DMA((half // HALF,)),
            pltpu.SemaphoreType.DMA((half // HALF,)),
        ],
        onto=() if before is None else ((0, before),),
        paired=True,
    )


def norm_work(n, part, rows, chip, crossed, x, gain, bias, h_out):
    middle = x[rows, :].astype(F32) + (chip[part, :] + crossed[part, :])
    h_out[part, :] = middle
    centred, scale = normal_rows(middle, 1e-05)
    return (centred * scale * gain[...] + bias[...]).astype(BF16).astype(F32)


def second_norm(line, chunk, rows, chip, crossed, x, gain, bias, before):
    width = x.shape[1]
    half = rows // 2
    return shared_rows(
        line,
        norm_work,
        chunk,
        rows,
        [chip, crossed, x, gain, bias],
        [const_spec((half, width)), const_spec((half, width)), row_spec(rows, width, chunk)]
        + [const_spec((1, width))] * 2,
        BF16,
        x.shape[0],
        width,
        [(half, width)],
        before,
    )


def norm_back(n, back, centred, scale, gain, gain_out, bias_out):
    normed = centred * scale
    one, two = jnp.sum(back * normed, axis=0, keepdims=True), jnp.sum(back, axis=0, keepdims=True)
    gain_out[...] = one if n == 0 else gain_out[...] + one
    bias_out[...] = two if n == 0 else bias_out[...] + two
    scaled = back * gain[...]
    first = jnp.mean(scaled, axis=-1, keepdims=True)
    second = jnp.mean(scaled * normed, axis=-1, keepdims=True)
    return scale * (scaled - first - normed * second)


def mid_work(n, part, rows, chip, crossed, h, gain, c, dh_out, gain_out, bias_out):
    centred, scale = normal_rows(h[part, :], 1e-05)
    back = chip[part, :] + crossed[part, :]
    value = c[rows, :].astype(F32) + norm_back(n, back, centred, scale, gain, gain_out, bias_out)
    dh_out[part, :] = value
    return value


def second_norm_back(line, chunk, rows, chip, crossed, h, gain, c, before):
    width = c.shape[1]
    half = rows // 2
    return shared_rows(
        line,
        mid_work,
        chunk,
        rows,
        [chip, crossed, h, gain, c],
        [const_spec((half, width))] * 3 + [const_spec((1, width)), row_spec(rows, width, chunk)],
        BF16,
        c.shape[0],
        width,
        [(half, width), (1, width), (1, width)],
        before,
    )


def first_work(n, part, rows, chip, crossed, x, gain, dh, gain_out, bias_out):
    centred, scale = normal_rows(x[rows, :].astype(F32), 1e-05)
    back = chip[part, :] + crossed[part, :]
    return dh[part, :] + norm_back(n, back, centred, scale, gain, gain_out, bias_out)


def first_norm_back(line, chunk, rows, chip, crossed, x, gain, dh, before):
    width = x.shape[1]
    half = rows // 2
    return shared_rows(
        line,
        first_work,
        chunk,
        rows,
        [chip, crossed, x, gain, dh],
        [const_spec((half, width))] * 2
        + [row_spec(rows, width, chunk), const_spec((1, width)), const_spec((half, width))],
        F32,
        x.shape[0],
        width,
        [(1, width), (1, width)],
        before,
    )


def output_work(n, part, rows, chip, crossed, h):
    return h[part, :] + (chip[part, :] + crossed[part, :])


def output_rows(line, chunk, rows, chip, crossed, h, total_rows, before):
    width = h.shape[1]
    half = rows // 2
    return shared_rows(
        line,
        output_work,
        chunk,
        rows,
        [chip, crossed, h],
        [const_spec((half, width))] * 3,
        BF16,
        total_rows,
        width,
        [],
        before,
    )


def gate_kernel(dz, w, o, switch, do_out, ds_out):
    grad = product_nt(dz[...], w[...])
    centred, scale = normal_rows(o[...], 1.0)
    gate = switch[...]
    sig = jax.nn.sigmoid(gate)
    ds_out[...] = (grad * (centred * scale) * (sig * (1.0 + gate * (1.0 - sig)))).astype(BF16)
    dn = grad * (gate * sig)
    one = jnp.mean(dn, axis=-1, keepdims=True)
    two = jnp.mean(dn * centred, axis=-1, keepdims=True)
    do_out[...] = (scale * (dn - one) - (scale * scale * scale) * centred * two).astype(BF16)


def gate_back(line, dz, w, o, switch):
    rows, width = dz.shape
    vw = w.shape[0]
    part = 512
    tiled = pl.BlockSpec((part, VALUE), lambda h, i: (i, h))
    return line.call(
        gate_kernel,
        [shape((rows, vw), BF16)] * 2,
        [tiled] * 2,
        [dz, w, o, switch],
        [
            pl.BlockSpec((part, width), lambda h, i: (i, 0)),
            pl.BlockSpec((VALUE, width), lambda h, i: (h, 0)),
            tiled,
            tiled,
        ],
        grid=(vw // VALUE, rows // part),
    )


def retain_back_kernel(q, k, v, do, seg_col, seg_row, logs, cos, sin, *rest):
    weights = rest[:CHUNKS]
    dq_out, dk_out, dv_out, dq_sum, dk_sum, dv_sum = rest[CHUNKS:]
    head = pl.program_id(0)
    dk_sum[...] = jnp.zeros_like(dk_sum)
    dv_sum[...] = jnp.zeros_like(dv_sum)
    for chunk in range(CHUNKS):
        low = first_key_block(chunk)
        here = slice(chunk * BLOCK, (chunk + 1) * BLOCK)
        total = None
        for block in range(low, chunk + 1):
            rows = slice(block * BLOCK, (block + 1) * BLOCK)
            part = slice((block - low) * BLOCK, (block - low + 1) * BLOCK)
            mask = decay_block(logs[head], seg_col[here, :], seg_row[:, rows], chunk * BLOCK, block * BLOCK)
            scores = (product_nt(do[here, :], v[rows, :]) * mask).astype(BF16)
            dv_sum[rows, :] += product_tn(weights[chunk][0, :, part], do[here, :])
            dk_sum[rows, :] += product_tn(scores, q[here, :])
            term = product_nn(scores, k[rows, :])
            total = term if total is None else total + term
        dq_sum[here, :] = total
    dq_out[...] = rotate(dq_sum[...], cos[...], sin[...], -1.0).astype(BF16)
    dk_out[...] = (rotate(dk_sum[...], cos[...], sin[...], -1.0) * float(KEY) ** (-0.5)).astype(BF16)
    dv_out[...] = dv_sum[...].astype(BF16)


def retention_back(line, q, k, v, do, seg_col, seg_row, logs, cos, sin, weights):
    rows, kw = q.shape
    vw = v.shape[1]

    def headed(columns):
        return pl.BlockSpec((rows, columns), lambda h: (0, h))

    return line.call(
        retain_back_kernel,
        [shape((rows, kw), BF16), shape((rows, kw), BF16), shape((rows, vw), BF16)],
        [headed(KEY), headed(KEY), headed(VALUE)],
        [q, k, v, do, seg_col, seg_row, logs, cos, sin] + list(weights),
        [
            headed(KEY),
            headed(KEY),
            headed(VALUE),
            headed(VALUE),
            const_spec(seg_col.shape),
            const_spec(seg_row.shape),
            SMEM,
            const_spec(cos.shape),
            const_spec(sin.shape),
        ]
        + [pl.BlockSpec((1,) + part.shape[1:], lambda h: (h, 0, 0)) for part in weights],
        grid=(kw // KEY,),
        scratch=[pltpu.VMEM((rows, KEY), F32), pltpu.VMEM((rows, KEY), F32), pltpu.VMEM((rows, VALUE), F32)],
    )


def block_kernel(by_rows, extra, where, left, right, *refs):
    total = product_tn(left[...], right[...])
    for term in refs[:extra]:
        total = total + term[...].reshape(total.shape)
    out = refs[extra]
    out[...] = total.reshape(out.shape)


class Weight:
    def __init__(self, line, where, left, right, by_rows, dp):
        self.line, self.where, self.left, self.right, self.by_rows, self.dp = line, where, left, right, by_rows, dp
        self.groups = dp // 2
        split = left if by_rows else right
        self.width = split.shape[1] // dp
        self.block = (self.width, right.shape[1]) if by_rows else (left.shape[1], self.width)

    def blocks(self, position, count, own, received=None, travelling=None):
        groups, width = self.groups, self.width
        if width % 128:
            return self.plain_blocks(position, count, own, received, travelling)

        def column(j, where):
            outer = lax.rem(where[1] + 2 * groups - 1 - position - j, groups)
            return outer * 2 + (where[0] if own else 1 - where[0])

        rows = self.left.shape[0]
        moving = pl.BlockSpec((rows, width), lambda j, where: (0, column(j, where)))
        left = moving if self.by_rows else const_spec(self.left.shape)
        right = const_spec(self.right.shape) if self.by_rows else moving
        ins, specs = [self.left, self.right], [left, right]
        if received is not None:
            ins.append(received)
            specs.append(pl.BlockSpec((1,) + self.block, lambda j, where: (position + j, 0, 0)))
        if travelling is not None:
            ins.append(travelling)
            specs.append(const_spec(self.block))
        if received is None:
            out, out_spec = (count,) + self.block, pl.BlockSpec((1,) + self.block, lambda j, where: (j, 0, 0))
        else:
            out, out_spec = self.block, const_spec(self.block)
        return self.line.call(
            functools.partial(block_kernel, self.by_rows, len(ins) - 2),
            [shape(out, F32)],
            [out_spec],
            ins,
            specs,
            grid=(count,),
            scalars=self.where,
        )[0]

    def plain_blocks(self, position, count, own, received, travelling):
        where, groups, width = self.where, self.groups, self.width
        parts = []
        for j in range(position, position + count):
            outer = lax.rem(where[1] + 2 * groups - 1 - j, groups)
            column = (outer * 2 + (where[0] if own else 1 - where[0])) * width
            if self.by_rows:
                part = product_tn(lax.dynamic_slice_in_dim(self.left, column, width, 1), self.right)
            else:
                part = product_tn(self.left, lax.dynamic_slice_in_dim(self.right, column, width, 1))
            if received is not None:
                part = part + received[j]
            if travelling is not None:
                part = part + travelling
            parts.append(part)
        return parts[0] if received is not None else jnp.stack(parts)

    def steps(self):
        dp, groups = self.dp, self.groups
        sent = self.blocks(0, groups, False)
        received = lax.ppermute(sent, "dp", [(i, i ^ 1) for i in range(dp)])
        yield None
        travelling = None
        for position in range(groups):
            block = self.blocks(position, 1, True, received, travelling)
            if position < groups - 1:
                travelling = lax.ppermute(block, "dp", [(i, (i + 2) % dp) for i in range(dp)])
                yield None
            else:
                yield block


def on_device(
    dp,
    tensor,
    inputs,
    segments,
    decay_order,
    ln1_gain,
    ln1_bias,
    w_query,
    w_key,
    w_value,
    w_swish,
    w_out,
    ln2_gain,
    ln2_bias,
    w_gate,
    w_up,
    w_down,
    cotangent,
):
    line = Line()
    place = lax.axis_index("dp")
    where = jnp.stack([lax.rem(place, 2), lax.div(place, 2)]).astype(jnp.int32)
    cos, sin = angle_tables(SEQ_LEN)
    logs = jnp.log1p(-jnp.exp2(-(decay_order + 5).astype(F32)))
    seg_row = segments.reshape(1, SEQ_LEN)
    seg_col = segments.reshape(SEQ_LEN, 1)
    gain1, bias1, gain2, bias2 = (v.reshape(1, -1) for v in (ln1_gain, ln1_bias, ln2_gain, ln2_bias))
    rows_here = inputs.shape[0]

    normed, query, key, value, switch = projections(
        line, inputs, gain1, bias1, cos, sin, w_query, w_key, w_value, w_swish
    )
    every = range(CHUNKS)
    firsts, gated, retained, weights = [], [], [], []
    for chunk in every:
        chip, u, o, p = retention(line, chunk, query, key, value, switch, seg_col, seg_row, logs, w_out)
        firsts.append((chip, across_chips(chip, tensor)))
        gated.append(u)
        retained.append(o)
        weights.append(p)
    middle, normed2, inner = [], None, None
    for chunk in every:
        normed2, h = second_norm(line, chunk, BLOCK, *firsts[chunk], inputs, gain2, bias2, normed2)
        inner = feed_forward(line, chunk, BLOCK, normed2, cotangent, w_gate, w_up, w_down, inner)
        middle.append(h)
    hidden, back_gate, back_up = inner
    gated, retained = jnp.concatenate(gated, axis=0), jnp.concatenate(retained, axis=0)
    results = {}

    def gradient(name, left, right, by_rows):
        for step in Weight(line, where, left, right, by_rows, dp).steps():
            if step is not None:
                results[name] = step
            yield

    rows = 2 * BLOCK
    pair = range(2)
    joined = [jnp.concatenate([middle[2 * i], middle[2 * i + 1]], axis=0) for i in pair]

    def summed(lefts, rights, transposed, chunk):
        chip = chip_sum(line, rows, lefts, rights, transposed, chunk)
        return chip, across_chips(chip, tensor)

    down = gradient("down", hidden, cotangent, False)
    gate = gradient("gate", normed2, back_gate, True)
    up = gradient("up", normed2, back_up, True)
    next(down)
    seconds = [summed([back_gate, back_up], [w_gate, w_up], True, i) for i in pair]
    next(gate)
    next(up)
    dz, dh, ln2g, ln2b = None, [], [], []

    def middle_step(i):
        out, own, one, two = second_norm_back(line, i, rows, *seconds[i], joined[i], gain2, cotangent, dz)
        dh.append(own)
        ln2g.append(one)
        ln2b.append(two)
        return out

    dz = middle_step(0)
    next(down)
    dz = middle_step(1)
    do, ds = gate_back(line, dz, w_out, retained, switch)
    next(down)
    dq, dk, dv = retention_back(line, query, key, value, do, seg_col, seg_row, logs, cos, sin, weights)
    next(down)
    thirds = [
        summed([dq, dk, dv, ds], [w_query, w_key, w_value, w_swish], True, i) for i in pair
    ]
    out = gradient("out", gated, dz, False)
    next(down)
    next(out)
    next(gate)
    swish = gradient("swish", normed, ds, True)
    vgrad = gradient("value", normed, dv, True)
    qgrad = gradient("query", normed, dq, True)
    kgrad = gradient("key", normed, dk, True)
    next(gate)
    grad_inputs, ln1g, ln1b = None, [], []

    def first_step(i):
        out, one, two = first_norm_back(line, i, rows, *thirds[i], inputs, gain1, dh[i], grad_inputs)
        ln1g.append(one)
        ln1b.append(two)
        return out

    grad_inputs = first_step(0)
    next(gate)
    grad_inputs = first_step(1)
    next(gate)
    fourths = [summed([hidden], [w_down], False, i) for i in pair]
    next(swish)
    next(up)
    small = jnp.concatenate([sum(v) for v in (ln1g, ln1b, ln2g, ln2b)], axis=0)
    small = small + lax.ppermute(small, "tensor", [(i, i ^ 1) for i in range(tensor)])
    small = lax.psum_scatter(small, "dp", scatter_dimension=1, tiled=True)
    next(up)
    output = output_rows(line, 0, rows, *fourths[0], joined[0], rows_here, None)[0]
    next(up)
    output = output_rows(line, 1, rows, *fourths[1], joined[1], rows_here, output)[0]
    next(up)
    next(vgrad)
    next(out)
    next(out)
    next(out)
    line.last.append(small)
    next(out)
    next(qgrad)
    for _ in range(4):
        next(swish)
    next(kgrad)
    for _ in range(4):
        next(vgrad)
    for _ in range(4):
        next(qgrad)
    for left in (down, gate, up, out, swish, vgrad, qgrad, kgrad):
        for _ in left:
            pass
    return (
        output,
        grad_inputs,
        small[0],
        small[1],
        results["query"],
        results["key"],
        results["value"],
        results["swish"],
        results["out"],
        small[2],
        small[3],
        results["gate"],
        results["up"],
        results["down"],
    )


def solution(mesh):
    dp, tensor = mesh.shape["dp"], mesh.shape["tensor"]

    def body(*arrays):
        return on_device(dp, tensor, *arrays)

    return jax.shard_map(
        body,
        mesh=mesh,
        in_specs=(
            P("dp", None),
            P("dp", None),
            P("tensor"),
            P(),
            P(),
            P(None, "tensor"),
            P(None, "tensor"),
            P(None, "tensor"),
            P(None, "tensor"),
            P("tensor", None),
            P(),
            P(),
            P(None, "tensor"),
            P(None, "tensor"),
            P("tensor", None),
            P("dp", None),
        ),
        out_specs=(
            P("dp", None),
            P("dp", None),
            P("dp"),
            P("dp"),
            P("dp", "tensor"),
            P("dp", "tensor"),
            P("dp", "tensor"),
            P("dp", "tensor"),
            P("tensor", "dp"),
            P("dp"),
            P("dp"),
            P("dp", "tensor"),
            P("dp", "tensor"),
            P("tensor", "dp"),
        ),
        check_vma=False,
    )
```

time: 1920 us -> 1090 us (0.57)
  waiting for transfers between devices: 1530 us -> 526 us
  Pallas kernels: 0 us -> 473 us
  matrix products: 204 us -> 0 us
  other arithmetic: 87.4 us -> 12.3 us
  blocking collectives: 39.1 us -> 0 us
  starting transfers between devices: 0.84 us -> 28.8 us
    reduce_scatter x8 -> x0, waiting for transfers between devices: 1030 us -> none  [the longest x1 153 us: on_device(): lax.psum_scatter(grad_out, 'dp', scatter_dimension=1, tiled=True)]
    psum x3 -> x0, waiting for transfers between devices: 506 us -> none  [the longest x1 208 us: on_device(): feed_out = lax.psum(product_nn(hidden_low, w_down), 'tensor')]
    pallas_call x0 -> x67, Pallas kernels: none -> 473 us  [call(): pl.pallas_call(body, out_shape=tuple(outs), grid_spec=pltpu.PrefetchScala...]
    ppermute x0 -> x43, waiting for transfers between devices: none -> 456 us  [the longest x24 339 us: steps(): lax.ppermute(block, 'dp', [(i, (i + 2) % dp) for i in range(dp)])]
    dot_general x30 -> x0, matrix products: 204 us -> none  [the longest x8 67.5 us: product_tn(): lax.dot_general(left, right, (((0,), (0,)), ((), ())), preferred_element_...]
    unnamed x11 -> x2, waiting for transfers between devices: 0.18 us -> 70.3 us
    reduce_sum x11 -> x0, other arithmetic: 39.9 us -> none  [the longest x3 18.2 us: layer_norm(): return centred * lax.rsqrt(spread + 1e-05) * scales + shifts]
    unnamed x1 -> x0, blocking collectives: 39.1 us -> none
  transfers between devices with their start and end apart: 11 -> 44, of which waited for: 11 -> 29; matrix products, arithmetic and copies ran while one was open for 6% -> 2% of each run, Pallas kernels for 0% -> 36%
where the time goes in v1:
time: 1090 us
  waiting for transfers between devices  526 us (48%)
  Pallas kernels  473 us (43%)
  local copies, waits for them, and re-layouts  33.2 us (3%)
  starting transfers between devices  28.8 us (3%)
  between operations  14.8 us (1%)
  other arithmetic  12.3 us (1%)
    pallas_call x67, Pallas kernels, call(): pl.pallas_call(body, out_shape=tuple(outs), grid_spec=pltpu.PrefetchScala...  473 us
    ppermute x24, waiting for transfers between devices, steps(): lax.ppermute(block, 'dp', [(i, (i + 2) % dp) for i in range(dp)])  339 us
    ppermute x10, waiting for transfers between devices, across_chips(): return lax.ppermute(values, 'tensor', [(i, i ^ 2) for i in range(size)])  94 us
    unnamed x2, waiting for transfers between devices  70.3 us
    unnamed x51, local copies, waits for them, and re-layouts  27.9 us
  transfers between devices with their start and end apart: 44, of which 29 were waited for; matrix products, arithmetic and copies ran while one was open for 2% of the time, Pallas kernels for 36%

profile of v1, /device:TPU:0, one launch (start us, length us, event | category | flops | bytes accessed | tf_op | source)
XLA Modules:
  0.0 1088.2 jit_solution(3051856194265764373)
XLA Ops:
  15.6 22.8 %shard_map.263 = (bf16[1024,2048]{1,0:T(8,128)(2,1)}, bf16[1024,512]{1,0:T(8,128)(2,1)}, bf16[1024,512]{1,0:T(8,128)(2,1)}, bf16[1024,1024]{1,0:T(8,128)(2,1)}, f32[1024,1024]{1,0:T(8,128)}) custom-call(bf16[1024,2048]{1,0:T(8,128)(2,1)} %refs_2_.33, f32[1,2048]{1,0:T(1,128)} %bitcast.26, f32[1,2048]{1,0:T(1,128)} %bitcast.29, ...), custom_call_target="tpu_custom_call" | custom-call | flops 1 | bytes 1 | tf_op jit(solution)/shard_map/pallas_call | solution.py:103
  166.7 11.2 %shard_map.277.refs_4_.refs_0_ = f32[256,2048]{1,0:T(8,128)} custom-call(bf16[1024,1024]{1,0:T(8,128)(2,1)} %get-tuple-element.97.refs_0_.refs_2_, bf16[1024,1024]{1,0:T(8,128)(2,1)} %get-tuple-element.98.refs_1_.refs_2_, bf16[2048,1024]{1,0:T(8,128)(2,1)} %refs_2_.27, bf16[2048,1024]{1,0:T(8,128)(2,1)} %refs_3_.11, f32[4,1024,256]{2,1,0:T(8,128)} %shard_map.276.refs_4_), custom_call_target="tpu_custom_call" | custom-call | flops 1 | bytes 1 | tf_op jit(solution)/shard_map/pallas_call | solution.py:103
  179.4 11.1 %shard_map.278.refs_3_.refs_0_ = f32[256,2048]{1,0:T(8,128)} custom-call(bf16[1024,1024]{1,0:T(8,128)(2,1)} %get-tuple-element.97.refs_0_.refs_2_, bf16[1024,1024]{1,0:T(8,128)(2,1)} %get-tuple-element.98.refs_1_.refs_2_, bf16[2048,1024]{1,0:T(8,128)(2,1)} %refs_2_.27, bf16[2048,1024]{1,0:T(8,128)(2,1)} %refs_3_.11, f32[256,2048]{1,0:T(8,128)} %shard_map.277.refs_4_.refs_0_), custom_call_target="tpu_custom_call" | custom-call | flops 1 | bytes 1 | tf_op jit(solution)/shard_map/pallas_call | solution.py:103
  209.6 17.0 %collective-permute-done.6.refs_1_ = f32[256,2048]{1,0:T(8,128)} collective-permute-done((f32[256,2048]{1,0:T(8,128)}, f32[256,2048]{1,0:T(8,128)}, u32[]{:S(2)}, u32[]{:S(2)}) %collective-permute-start.6) | collective-permute-done | bytes 2097184 | tf_op jit(solution)/shard_map/ppermute | solution.py:395
  226.7 10.8 shard_map.281
  237.4 21.2 %collective-permute-done.7.refs_3_ = f32[4,1024,256]{2,1,0:T(8,128)} collective-permute-done((f32[4,1024,256]{2,1,0:T(8,128)}, f32[4,1024,256]{2,1,0:T(8,128)}, u32[]{:S(2)}, u32[]{:S(2)}) %collective-permute-start.7) | collective-permute-done | bytes 4194336 | tf_op jit(solution)/shard_map/ppermute | solution.py:700
  283.1 12.8 %shard_map.284 = (bf16[1024,1024]{1,0:T(8,128)(2,1)}, bf16[1024,1024]{1,0:T(8,128)(2,1)}) custom-call(bf16[1024,2048]{1,0:T(8,128)(2,1)} %get-tuple-element.108.refs_0_.refs_4_.refs_2_, bf16[1024,2048]{1,0:T(8,128)(2,1)} %refs_1_.11, f32[1024,1024]{1,0:T(8,128)} %pad_maximum_fusion.refs_2_, f32[1024,1024]{1,0:T(8,128)} %get-tuple-element.77.refs_3_, ...), custom_call_target="tpu_custom_call" | custom-call | flops 1 | bytes 1 | tf_op jit(solution)/shard_map/pallas_call | solution.py:103
  302.2 12.5 %shard_map.286 = (bf16[1024,512]{1,0:T(8,128)(2,1)}, bf16[1024,512]{1,0:T(8,128)(2,1)}, bf16[1024,1024]{1,0:T(8,128)(2,1)}) custom-call(bf16[1024,512]{1,0:T(8,128)(2,1)} %get-tuple-element.74.refs_0_, bf16[1024,512]{1,0:T(8,128)(2,1)} %get-tuple-element.75.refs_1_, bf16[1024,1024]{1,0:T(8,128)(2,1)} %get-tuple-element.76.refs_2_, ...), custom_call_target="tpu_custom_call" | custom-call | flops 1 | bytes 1 | tf_op jit(solution)/shard_map/pallas_call | solution.py:103
  314.7 13.3 %collective-permute-done.9.refs_4_ = f32[1024,256]{1,0:T(8,128)} collective-permute-done((f32[1024,256]{1,0:T(8,128)}, f32[1024,256]{1,0:T(8,128)}, u32[]{:S(2)}, u32[]{:S(2)}) %collective-permute-start.9) | collective-permute-done | bytes 1048608 | tf_op jit(solution)/shard_map/ppermute | solution.py:706
  337.9 13.9 %shard_map.288.refs_8_.refs_0_ = f32[256,2048]{1,0:T(8,128)} custom-call(bf16[1024,512]{1,0:T(8,128)(2,1)} %get-tuple-element.118.refs_5_.refs_0_.refs_2_, bf16[1024,512]{1,0:T(8,128)(2,1)} %get-tuple-element.119.refs_1_.refs_2_, bf16[1024,1024]{1,0:T(8,128)(2,1)} %get-tuple-element.120.refs_2_, bf16[1024,1024]{1,0:T(8,128)(2,1)} %get-tuple-element.121.refs_3_.refs_2_, ...), custom_call_target="tpu_custom_call" | custom-call | flops 1 | bytes 1 | tf_op jit(solution)/shard_map/pallas_call | solution.py:103
  352.6 13.8 %shard_map.289.refs_5_.refs_0_ = f32[256,2048]{1,0:T(8,128)} custom-call(bf16[1024,512]{1,0:T(8,128)(2,1)} %get-tuple-element.118.refs_5_.refs_0_.refs_2_, bf16[1024,512]{1,0:T(8,128)(2,1)} %get-tuple-element.119.refs_1_.refs_2_, bf16[1024,1024]{1,0:T(8,128)(2,1)} %get-tuple-element.120.refs_2_, bf16[1024,1024]{1,0:T(8,128)(2,1)} %get-tuple-element.121.refs_3_.refs_2_, ...), custom_call_target="tpu_custom_call" | custom-call | flops 1 | bytes 1 | tf_op jit(solution)/shard_map/pallas_call | solution.py:103
  385.7 26.0 %collective-permute-done.11.refs_4_ = f32[256,1024]{1,0:T(8,128)} collective-permute-done((f32[256,1024]{1,0:T(8,128)}, f32[256,1024]{1,0:T(8,128)}, u32[]{:S(2)}, u32[]{:S(2)}) %collective-permute-start.11) | collective-permute-done | bytes 1048608 | tf_op jit(solution)/shard_map/ppermute | solution.py:706
  430.1 12.9 %collective-permute-done.12.refs_4_ = f32[256,1024]{1,0:T(8,128)} collective-permute-done((f32[256,1024]{1,0:T(8,128)}, f32[256,1024]{1,0:T(8,128)}, u32[]{:S(2)}, u32[]{:S(2)}) %collective-permute-start.12) | collective-permute-done | bytes 1048608 | tf_op jit(solution)/shard_map/ppermute | solution.py:706
  448.2 15.8 %collective-permute-done.15.refs_1_ = f32[256,2048]{1,0:T(8,128)} collective-permute-done((f32[256,2048]{1,0:T(8,128)}, f32[256,2048]{1,0:T(8,128)}, u32[]{:S(2)}, u32[]{:S(2)}) %collective-permute-start.15) | collective-permute-done | bytes 2097184 | tf_op jit(solution)/shard_map/ppermute | solution.py:395
  464.0 10.8 shard_map.296
  512.8 24.2 %collective-permute-done.19.refs_4_ = f32[256,1024]{1,0:T(8,128)} collective-permute-done((f32[256,1024]{1,0:T(8,128)}, f32[256,1024]{1,0:T(8,128)}, u32[]{:S(2)}, u32[]{:S(2)}) %collective-permute-start.19) | collective-permute-done | bytes 1048608 | tf_op jit(solution)/shard_map/ppermute | solution.py:706
  541.8 17.9 %collective-permute-done.17.refs_1_ = f32[256,2048]{1,0:T(8,128)} collective-permute-done((f32[256,2048]{1,0:T(8,128)}, f32[256,2048]{1,0:T(8,128)}, u32[]{:S(2)}, u32[]{:S(2)}) %collective-permute-start.17) | collective-permute-done | bytes 2097184 | tf_op jit(solution)/shard_map/ppermute | solution.py:395
  574.2 29.3 %collective-permute-done.16.refs_1_ = f32[256,2048]{1,0:T(8,128)} collective-permute-done((f32[256,2048]{1,0:T(8,128)}, f32[256,2048]{1,0:T(8,128)}, u32[]{:S(2)}, u32[]{:S(2)}) %collective-permute-start.16) | collective-permute-done | bytes 2097184 | tf_op jit(solution)/shard_map/ppermute | solution.py:395
  629.0 26.8 %collective-permute-done.24.refs_4_ = f32[1024,256]{1,0:T(8,128)} collective-permute-done((f32[1024,256]{1,0:T(8,128)}, f32[1024,256]{1,0:T(8,128)}, u32[]{:S(2)}, u32[]{:S(2)}) %collective-permute-start.24) | collective-permute-done | bytes 1048608 | tf_op jit(solution)/shard_map/ppermute | solution.py:706
  660.6 26.5 %collective-permute-done.25.refs_4_ = f32[1024,256]{1,0:T(8,128)} collective-permute-done((f32[1024,256]{1,0:T(8,128)}, f32[1024,256]{1,0:T(8,128)}, u32[]{:S(2)}, u32[]{:S(2)}) %collective-permute-start.25) | collective-permute-done | bytes 1048608 | tf_op jit(solution)/shard_map/ppermute | solution.py:706
  695.2 70.2 %reduce-scatter.4.cloned.1.call-done = f32[256,4]{1,0:T(8,128)} async-done(((f32[2048,4]{1,0:T(8,128)}), f32[256,4]{1,0:T(8,128)}) %reduce-scatter.4.cloned.1.call-update) | async-done | bytes 4112
  782.4 25.4 %collective-permute-done.30.refs_4_ = f32[256,1024]{1,0:T(8,128)} collective-permute-done((f32[256,1024]{1,0:T(8,128)}, f32[256,1024]{1,0:T(8,128)}, u32[]{:S(2)}, u32[]{:S(2)}) %collective-permute-start.30) | collective-permute-done | bytes 1048608 | tf_op jit(solution)/shard_map/ppermute | solution.py:706
  812.5 25.0 %collective-permute-done.31.refs_4_ = f32[256,1024]{1,0:T(8,128)} collective-permute-done((f32[256,1024]{1,0:T(8,128)}, f32[256,1024]{1,0:T(8,128)}, u32[]{:S(2)}, u32[]{:S(2)}) %collective-permute-start.31) | collective-permute-done | bytes 1048608 | tf_op jit(solution)/shard_map/ppermute | solution.py:706
  842.3 24.1 %collective-permute-done.32.refs_4_ = f32[256,1024]{1,0:T(8,128)} collective-permute-done((f32[256,1024]{1,0:T(8,128)}, f32[256,1024]{1,0:T(8,128)}, u32[]{:S(2)}, u32[]{:S(2)}) %collective-permute-start.32) | collective-permute-done | bytes 1048608 | tf_op jit(solution)/shard_map/ppermute | solution.py:706
  881.2 23.2 %collective-permute-done.33.refs_4_ = f32[256,1024]{1,0:T(8,128)} collective-permute-done((f32[256,1024]{1,0:T(8,128)}, f32[256,1024]{1,0:T(8,128)}, u32[]{:S(2)}, u32[]{:S(2)}) %collective-permute-start.33) | collective-permute-done | bytes 1048608 | tf_op jit(solution)/shard_map/ppermute | solution.py:706
  911.0 20.4 %collective-permute-done.34.refs_4_ = f32[256,1024]{1,0:T(8,128)} collective-permute-done((f32[256,1024]{1,0:T(8,128)}, f32[256,1024]{1,0:T(8,128)}, u32[]{:S(2)}, u32[]{:S(2)}) %collective-permute-start.34) | collective-permute-done | bytes 1048608 | tf_op jit(solution)/shard_map/ppermute | solution.py:706
  938.4 19.1 %collective-permute-done.35.refs_4_ = f32[256,1024]{1,0:T(8,128)} collective-permute-done((f32[256,1024]{1,0:T(8,128)}, f32[256,1024]{1,0:T(8,128)}, u32[]{:S(2)}, u32[]{:S(2)}) %collective-permute-start.35) | collective-permute-done | bytes 1048608 | tf_op jit(solution)/shard_map/ppermute | solution.py:706
  965.9 11.2 %collective-permute-done.36.refs_4_ = f32[256,512]{1,0:T(8,128)S(1)} collective-permute-done((f32[256,512]{1,0:T(8,128)}, f32[256,512]{1,0:T(8,128)S(1)}, u32[]{:S(2)}, u32[]{:S(2)}) %collective-permute-start.36) | collective-permute-done | bytes 524320 | tf_op jit(solution)/shard_map/ppermute | solution.py:706
  981.4 11.2 %collective-permute-done.37.refs_4_ = f32[256,512]{1,0:T(8,128)S(1)} collective-permute-done((f32[256,512]{1,0:T(8,128)}, f32[256,512]{1,0:T(8,128)S(1)}, u32[]{:S(2)}, u32[]{:S(2)}) %collective-permute-start.37) | collective-permute-done | bytes 524320 | tf_op jit(solution)/shard_map/ppermute | solution.py:706
  997.0 11.2 %collective-permute-done.38.refs_4_ = f32[256,512]{1,0:T(8,128)S(1)} collective-permute-done((f32[256,512]{1,0:T(8,128)}, f32[256,512]{1,0:T(8,128)S(1)}, u32[]{:S(2)}, u32[]{:S(2)}) %collective-permute-start.38) | collective-permute-done | bytes 524320 | tf_op jit(solution)/shard_map/ppermute | solution.py:706
  1016.1 13.4 %collective-permute-done.40.refs_4_ = f32[256,512]{1,0:T(8,128)S(1)} collective-permute-done((f32[256,512]{1,0:T(8,128)}, f32[256,512]{1,0:T(8,128)S(1)}, u32[]{:S(2)}, u32[]{:S(2)}) %collective-permute-start.40) | collective-permute-done | bytes 524320 | tf_op jit(solution)/shard_map/ppermute | solution.py:706
  1033.9 14.5 %collective-permute-done.41.refs_4_ = f32[256,512]{1,0:T(8,128)S(1)} collective-permute-done((f32[256,512]{1,0:T(8,128)}, f32[256,512]{1,0:T(8,128)S(1)}, u32[]{:S(2)}, u32[]{:S(2)}) %collective-permute-start.41) | collective-permute-done | bytes 524320 | tf_op jit(solution)/shard_map/ppermute | solution.py:706
  (192 shorter events, 454.1 us)
Async XLA Ops:
  7.2 758.3 %reduce-scatter.4.cloned.1.call-start = ((), (), s32[]{:S(2)}) async-start(), calls=%async_computation.1 | async-start | bytes 1179648
  48.1 35.8 %collective-permute-start.3 = (f32[128,2048]{1,0:T(8,128)}, f32[128,2048]{1,0:T(8,128)}, u32[]{:S(2)}, u32[]{:S(2)}) collective-permute-start(f32[128,2048]{1,0:T(8,128)} %get-tuple-element.79.refs_8_.refs_0_), channel_id=1, source_target_pairs={{0,2},{1,3},{2,0},{3,1},{4,6},{5,7},{6,4},{7,5},{8,10},{9,11},{10,... | collective-permute-start | bytes 3145736 | tf_op jit(solution)/shard_map/ppermute | solution.py:395
  60.6 38.8 %collective-permute-start.2 = (f32[128,2048]{1,0:T(8,128)}, f32[128,2048]{1,0:T(8,128)}, u32[]{:S(2)}, u32[]{:S(2)}) collective-permute-start(f32[128,2048]{1,0:T(8,128)} %get-tuple-element.80.refs_8_.refs_0_), channel_id=1, source_target_pairs={{0,2},{1,3},{2,0},{3,1},{4,6},{5,7},{6,4},{7,5},{8,10},{9,11},{10,... | collective-permute-start | bytes 3145736 | tf_op jit(solution)/shard_map/ppermute | solution.py:395
  70.9 49.3 %collective-permute-start.1 = (f32[128,2048]{1,0:T(8,128)}, f32[128,2048]{1,0:T(8,128)}, u32[]{:S(2)}, u32[]{:S(2)}) collective-permute-start(f32[128,2048]{1,0:T(8,128)} %get-tuple-element.81.refs_8_.refs_0_), channel_id=1, source_target_pairs={{0,2},{1,3},{2,0},{3,1},{4,6},{5,7},{6,4},{7,5},{8,10},{9,11},{10,... | collective-permute-start | bytes 3145736 | tf_op jit(solution)/shard_map/ppermute | solution.py:395
  83.2 58.9 %collective-permute-start = (f32[128,2048]{1,0:T(8,128)}, f32[128,2048]{1,0:T(8,128)}, u32[]{:S(2)}, u32[]{:S(2)}) collective-permute-start(f32[128,2048]{1,0:T(8,128)} %get-tuple-element.82.refs_5_.refs_0_), channel_id=1, source_target_pairs={{0,2},{1,3},{2,0},{3,1},{4,6},{5,7},{6,4},{7,5},{8,10},{9,11},{10,... | collective-permute-start | bytes 3145736 | tf_op jit(solution)/shard_map/ppermute | solution.py:395
  164.9 93.7 %collective-permute-start.7 = (f32[4,1024,256]{2,1,0:T(8,128)}, f32[4,1024,256]{2,1,0:T(8,128)}, u32[]{:S(2)}, u32[]{:S(2)}) collective-permute-start(f32[4,1024,256]{2,1,0:T(8,128)} %shard_map.276.refs_4_), channel_id=1, source_target_pairs={{0,4},{4,0},{8,12},{12,8},{16,20},{20,16},{24,28},{28,24},{1,5},{5... | collective-permute-start | bytes 12582920 | tf_op jit(solution)/shard_map/ppermute | solution.py:700
  177.8 48.8 %collective-permute-start.6 = (f32[256,2048]{1,0:T(8,128)}, f32[256,2048]{1,0:T(8,128)}, u32[]{:S(2)}, u32[]{:S(2)}) collective-permute-start(f32[256,2048]{1,0:T(8,128)} %shard_map.277.refs_4_.refs_0_), channel_id=1, source_target_pairs={{0,2},{1,3},{2,0},{3,1},{4,6},{5,7},{6,4},{7,5},{8,10},{9,11},{10,... | collective-permute-start | bytes 6291464 | tf_op jit(solution)/shard_map/ppermute | solution.py:395
  190.6 81.9 %collective-permute-start.5 = (f32[256,2048]{1,0:T(8,128)}, f32[256,2048]{1,0:T(8,128)}, u32[]{:S(2)}, u32[]{:S(2)}) collective-permute-start(f32[256,2048]{1,0:T(8,128)} %shard_map.278.refs_3_.refs_0_), channel_id=1, source_target_pairs={{0,2},{1,3},{2,0},{3,1},{4,6},{5,7},{6,4},{7,5},{8,10},{9,11},{10,... | collective-permute-start | bytes 6291464 | tf_op jit(solution)/shard_map/ppermute | solution.py:395
  198.4 181.6 %collective-permute-start.4 = (f32[4,256,1024]{2,1,0:T(8,128)}, f32[4,256,1024]{2,1,0:T(8,128)}, u32[]{:S(2)}, u32[]{:S(2)}) collective-permute-start(f32[4,256,1024]{2,1,0:T(8,128)} %shard_map.279.refs_3_), channel_id=1, source_target_pairs={{0,4},{4,0},{8,12},{12,8},{16,20},{20,16},{24,28},{28,24},{1,5},{5... | collective-permute-start | bytes 12582920 | tf_op jit(solution)/shard_map/ppermute | solution.py:700
  263.1 32.8 %collective-permute-start.8 = (f32[1024,256]{1,0:T(8,128)}, f32[1024,256]{1,0:T(8,128)}, u32[]{:S(2)}, u32[]{:S(2)}) collective-permute-start(f32[1024,256]{1,0:T(8,128)} %shard_map.282.refs_6_), channel_id=1, source_target_pairs={{0,8},{4,12},{8,16},{12,20},{16,24},{20,28},{24,0},{28,4},{1,9},{5... | collective-permute-start | bytes 3145736 | tf_op jit(solution)/shard_map/ppermute | solution.py:706
  300.6 27.3 %collective-permute-start.9 = (f32[1024,256]{1,0:T(8,128)}, f32[1024,256]{1,0:T(8,128)}, u32[]{:S(2)}, u32[]{:S(2)}) collective-permute-start(f32[1024,256]{1,0:T(8,128)} %shard_map.285.refs_13_), channel_id=1, source_target_pairs={{0,8},{4,12},{8,16},{12,20},{16,24},{20,28},{24,0},{28,4},{1,9},{5... | collective-permute-start | bytes 3145736 | tf_op jit(solution)/shard_map/ppermute | solution.py:706
  332.8 33.5 %collective-permute-start.10 = (f32[1024,256]{1,0:T(8,128)}, f32[1024,256]{1,0:T(8,128)}, u32[]{:S(2)}, u32[]{:S(2)}) collective-permute-start(f32[1024,256]{1,0:T(8,128)} %shard_map.287.refs_8_), channel_id=1, source_target_pairs={{0,8},{4,12},{8,16},{12,20},{16,24},{20,28},{24,0},{28,4},{1,9},{5... | collective-permute-start | bytes 3145736 | tf_op jit(solution)/shard_map/ppermute | solution.py:706
  332.8 172.2 %collective-permute-start.18 = (f32[4,256,1024]{2,1,0:T(8,128)}, f32[4,256,1024]{2,1,0:T(8,128)}, u32[]{:S(2)}, u32[]{:S(2)}) collective-permute-start(f32[4,256,1024]{2,1,0:T(8,128)} %shard_map.280.refs_5_), channel_id=1, source_target_pairs={{0,4},{4,0},{8,12},{12,8},{16,20},{20,16},{24,28},{28,24},{1,5},{5... | collective-permute-start | bytes 12582920 | tf_op jit(solution)/shard_map/ppermute | solution.py:700
  371.1 48.2 %collective-permute-start.13 = (f32[256,2048]{1,0:T(8,128)}, f32[256,2048]{1,0:T(8,128)}, u32[]{:S(2)}, u32[]{:S(2)}) collective-permute-start(f32[256,2048]{1,0:T(8,128)} %shard_map.288.refs_8_.refs_0_), channel_id=1, source_target_pairs={{0,2},{1,3},{2,0},{3,1},{4,6},{5,7},{6,4},{7,5},{8,10},{9,11},{10,... | collective-permute-start | bytes 6291464 | tf_op jit(solution)/shard_map/ppermute | solution.py:395
  384.3 27.3 %collective-permute-start.11 = (f32[256,1024]{1,0:T(8,128)}, f32[256,1024]{1,0:T(8,128)}, u32[]{:S(2)}, u32[]{:S(2)}) collective-permute-start(f32[256,1024]{1,0:T(8,128)} %shard_map.292.refs_5_), channel_id=1, source_target_pairs={{0,8},{4,12},{8,16},{12,20},{16,24},{20,28},{24,0},{28,4},{1,9},{5... | collective-permute-start | bytes 3145736 | tf_op jit(solution)/shard_map/ppermute | solution.py:706
  416.3 26.6 %collective-permute-start.12 = (f32[256,1024]{1,0:T(8,128)}, f32[256,1024]{1,0:T(8,128)}, u32[]{:S(2)}, u32[]{:S(2)}) collective-permute-start(f32[256,1024]{1,0:T(8,128)} %shard_map.293.refs_5_), channel_id=1, source_target_pairs={{0,8},{4,12},{8,16},{12,20},{16,24},{20,28},{24,0},{28,4},{1,9},{5... | collective-permute-start | bytes 3145736 | tf_op jit(solution)/shard_map/ppermute | solution.py:706
  416.5 47.5 %collective-permute-start.15 = (f32[256,2048]{1,0:T(8,128)}, f32[256,2048]{1,0:T(8,128)}, u32[]{:S(2)}, u32[]{:S(2)}) collective-permute-start(f32[256,2048]{1,0:T(8,128)} %shard_map.289.refs_5_.refs_0_), channel_id=1, source_target_pairs={{0,2},{1,3},{2,0},{3,1},{4,6},{5,7},{6,4},{7,5},{8,10},{9,11},{10,... | collective-permute-start | bytes 6291464 | tf_op jit(solution)/shard_map/ppermute | solution.py:395
  447.7 27.1 %collective-permute-start.14 = (f32[256,1024]{1,0:T(8,128)}, f32[256,1024]{1,0:T(8,128)}, u32[]{:S(2)}, u32[]{:S(2)}) collective-permute-start(f32[256,1024]{1,0:T(8,128)} %shard_map.295.refs_6_), channel_id=1, source_target_pairs={{0,8},{4,12},{8,16},{12,20},{16,24},{20,28},{24,0},{28,4},{1,9},{5... | collective-permute-start | bytes 3145736 | tf_op jit(solution)/shard_map/ppermute | solution.py:706
  447.7 176.3 %collective-permute-start.22 = (f32[4,1024,256]{2,1,0:T(8,128)}, f32[4,1024,256]{2,1,0:T(8,128)}, u32[]{:S(2)}, u32[]{:S(2)}) collective-permute-start(f32[4,1024,256]{2,1,0:T(8,128)} %shard_map.291.refs_4_), channel_id=1, source_target_pairs={{0,4},{4,0},{8,12},{12,8},{16,20},{20,16},{24,28},{28,24},{1,5},{5... | collective-permute-start | bytes 12582920 | tf_op jit(solution)/shard_map/ppermute | solution.py:700
  509.4 27.6 %collective-permute-start.19 = (f32[256,1024]{1,0:T(8,128)}, f32[256,1024]{1,0:T(8,128)}, u32[]{:S(2)}, u32[]{:S(2)}) collective-permute-start(f32[256,1024]{1,0:T(8,128)} %shard_map.301.refs_5_), channel_id=1, source_target_pairs={{0,8},{4,12},{8,16},{12,20},{16,24},{20,28},{24,0},{28,4},{1,9},{5... | collective-permute-start | bytes 3145736 | tf_op jit(solution)/shard_map/ppermute | solution.py:706
  510.8 48.8 %collective-permute-start.17 = (f32[256,2048]{1,0:T(8,128)}, f32[256,2048]{1,0:T(8,128)}, u32[]{:S(2)}, u32[]{:S(2)}) collective-permute-start(f32[256,2048]{1,0:T(8,128)} %shard_map.298.refs_2_.refs_0_), channel_id=1, source_target_pairs={{0,2},{1,3},{2,0},{3,1},{4,6},{5,7},{6,4},{7,5},{8,10},{9,11},{10,... | collective-permute-start | bytes 6291464 | tf_op jit(solution)/shard_map/ppermute | solution.py:395
  512.3 91.1 %collective-permute-start.16 = (f32[256,2048]{1,0:T(8,128)}, f32[256,2048]{1,0:T(8,128)}, u32[]{:S(2)}, u32[]{:S(2)}) collective-permute-start(f32[256,2048]{1,0:T(8,128)} %shard_map.299.refs_3_.refs_0_), channel_id=1, source_target_pairs={{0,2},{1,3},{2,0},{3,1},{4,6},{5,7},{6,4},{7,5},{8,10},{9,11},{10,... | collective-permute-start | bytes 6291464 | tf_op jit(solution)/shard_map/ppermute | solution.py:395
  541.8 26.8 %collective-permute-start.20 = (f32[256,1024]{1,0:T(8,128)}, f32[256,1024]{1,0:T(8,128)}, u32[]{:S(2)}, u32[]{:S(2)}) collective-permute-start(f32[256,1024]{1,0:T(8,128)} %shard_map.302.refs_3_), channel_id=1, source_target_pairs={{0,8},{4,12},{8,16},{12,20},{16,24},{20,28},{24,0},{28,4},{1,9},{5... | collective-permute-start | bytes 3145736 | tf_op jit(solution)/shard_map/ppermute | solution.py:706
  573.3 38.8 %collective-permute-start.23 = (f32[256,1024]{1,0:T(8,128)}, f32[256,1024]{1,0:T(8,128)}, u32[]{:S(2)}, u32[]{:S(2)}) collective-permute-start(f32[256,1024]{1,0:T(8,128)} %shard_map.304.refs_4_), channel_id=1, source_target_pairs={{0,8},{4,12},{8,16},{12,20},{16,24},{20,28},{24,0},{28,4},{1,9},{5... | collective-permute-start | bytes 3145736 | tf_op jit(solution)/shard_map/ppermute | solution.py:706
  573.6 203.8 %collective-permute-start.29 = (f32[4,256,1024]{2,1,0:T(8,128)}, f32[4,256,1024]{2,1,0:T(8,128)}, u32[]{:S(2)}, u32[]{:S(2)}) collective-permute-start(f32[4,256,1024]{2,1,0:T(8,128)} %shard_map.300.refs_4_), channel_id=1, source_target_pairs={{0,4},{4,0},{8,12},{12,8},{16,20},{20,16},{24,28},{28,24},{1,5},{5... | collective-permute-start | bytes 12582920 | tf_op jit(solution)/shard_map/ppermute | solution.py:700
  628.4 27.3 %collective-permute-start.24 = (f32[1024,256]{1,0:T(8,128)}, f32[1024,256]{1,0:T(8,128)}, u32[]{:S(2)}, u32[]{:S(2)}) collective-permute-start(f32[1024,256]{1,0:T(8,128)} %shard_map.308.refs_5_), channel_id=1, source_target_pairs={{0,8},{4,12},{8,16},{12,20},{16,24},{20,28},{24,0},{28,4},{1,9},{5... | collective-permute-start | bytes 3145736 | tf_op jit(solution)/shard_map/ppermute | solution.py:706
  660.6 26.5 %collective-permute-start.25 = (f32[1024,256]{1,0:T(8,128)}, f32[1024,256]{1,0:T(8,128)}, u32[]{:S(2)}, u32[]{:S(2)}) collective-permute-start(f32[1024,256]{1,0:T(8,128)} %shard_map.309.refs_5_), channel_id=1, source_target_pairs={{0,8},{4,12},{8,16},{12,20},{16,24},{20,28},{24,0},{28,4},{1,9},{5... | collective-permute-start | bytes 3145736 | tf_op jit(solution)/shard_map/ppermute | solution.py:706
  691.8 75.2 %collective-permute-start.26 = (f32[1024,256]{1,0:T(8,128)}, f32[1024,256]{1,0:T(8,128)}, u32[]{:S(2)}, u32[]{:S(2)}) collective-permute-start(f32[1024,256]{1,0:T(8,128)} %shard_map.310.refs_5_), channel_id=1, source_target_pairs={{0,8},{4,12},{8,16},{12,20},{16,24},{20,28},{24,0},{28,4},{1,9},{5... | collective-permute-start | bytes 3145736 | tf_op jit(solution)/shard_map/ppermute | solution.py:706
  691.8 185.0 %collective-permute-start.28 = (f32[4,256,1024]{2,1,0:T(8,128)}, f32[4,256,1024]{2,1,0:T(8,128)}, u32[]{:S(2)}, u32[]{:S(2)}) collective-permute-start(f32[4,256,1024]{2,1,0:T(8,128)} %shard_map.307.refs_4_), channel_id=1, source_target_pairs={{0,4},{4,0},{8,12},{12,8},{16,20},{20,16},{24,28},{28,24},{1,5},{5... | collective-permute-start | bytes 12582920 | tf_op jit(solution)/shard_map/ppermute | solution.py:700
  781.8 26.0 %collective-permute-start.30 = (f32[256,1024]{1,0:T(8,128)}, f32[256,1024]{1,0:T(8,128)}, u32[]{:S(2)}, u32[]{:S(2)}) collective-permute-start(f32[256,1024]{1,0:T(8,128)} %shard_map.313.refs_5_), channel_id=1, source_target_pairs={{0,8},{4,12},{8,16},{12,20},{16,24},{20,28},{24,0},{28,4},{1,9},{5... | collective-permute-start | bytes 3145736 | tf_op jit(solution)/shard_map/ppermute | solution.py:706
  909.1 53.1 %collective-permute-start.27 = (f32[4,256,512]{2,1,0:T(8,128)}, f32[4,256,512]{2,1,0:T(8,128)}, u32[]{:S(2)}, u32[]{:S(2)}) collective-permute-start(f32[4,256,512]{2,1,0:T(8,128)} %shard_map.312.refs_4_), channel_id=1, source_target_pairs={{0,4},{4,0},{8,12},{12,8},{16,20},{20,16},{24,28},{28,24},{1,5},{5... | collective-permute-start | bytes 6291464 | tf_op jit(solution)/shard_map/ppermute | solution.py:700
  936.1 76.5 %collective-permute-start.39 = (f32[4,256,512]{2,1,0:T(8,128)}, f32[4,256,512]{2,1,0:T(8,128)}, u32[]{:S(2)}, u32[]{:S(2)}) collective-permute-start(f32[4,256,512]{2,1,0:T(8,128)} %shard_map.317.refs_4_), channel_id=1, source_target_pairs={{0,4},{4,0},{8,12},{12,8},{16,20},{20,16},{24,28},{28,24},{1,5},{5... | collective-permute-start | bytes 6291464 | tf_op jit(solution)/shard_map/ppermute | solution.py:700
  (33 other events, 502.4 us)
Sparse Core Ops, SparseCore 0:
  695.4 70.0 reduce-scatter.3

commit v2 on v1

--- a/solution.py
+++ b/solution.py
@@ -35,9 +35,9 @@
     half_width = KEY // 2
     column = jnp.arange(KEY, dtype=jnp.int32) // 2
     frequency = jnp.power(10000.0, -column.astype(F32) / (half_width - 1))
-    position = jnp.arange(length, dtype=jnp.int32).astype(F32)
-    angles = position[:, None] * frequency[None, :]
-    return jnp.cos(angles), jnp.sin(angles)
+    inside = jnp.arange(BLOCK, dtype=jnp.int32).astype(F32)[:, None] * frequency[None, :]
+    starts = jnp.arange(0, length, BLOCK, dtype=jnp.int32).astype(F32)[:, None] * frequency[None, :]
+    return jnp.cos(inside), jnp.sin(inside), jnp.cos(starts), jnp.sin(starts)
 
 
 def rotate(values, cosines, sines, sign):
@@ -54,11 +54,15 @@
     return centred, lax.rsqrt(spread + eps)
 
 
-def decay_block(log_keep, seg_rows, seg_columns, row_start, column_start):
+def down_rows(seg):
+    return jnp.transpose(jnp.broadcast_to(seg.astype(F32), (BLOCK, BLOCK)))
+
+
+def decay_block(log_keep, seg_rows, seg, row_start, column_start):
     rows = row_start + lax.broadcasted_iota(jnp.int32, (BLOCK, BLOCK), 0)
     columns = column_start + lax.broadcasted_iota(jnp.int32, (BLOCK, BLOCK), 1)
     gap = rows - columns
-    keep = (seg_rows == seg_columns) & (gap >= 0)
+    keep = (seg_rows == seg.astype(F32)) & (gap >= 0)
     return jnp.where(keep, jnp.exp(jnp.maximum(gap, 0).astype(F32) * log_keep), 0.0)
 
 
@@ -85,7 +89,8 @@
         onto=(),
         paired=False,
     ):
-        extra = [array for _, array in onto] + self.last
+        held = list(ins) + [array for _, array in onto]
+        extra = held[len(ins) :] + [array for array in self.last if not any(array is other for other in held)]
         scalar_count = 0 if scalars is None else 1
         in_count = len(ins)
         skipped = len(extra)
@@ -172,59 +177,56 @@
 SMEM = pl.BlockSpec(memory_space=pltpu.SMEM)
 
 
-def proj_kernel(x, gain, bias, cos, sin, wq, wk, wv, ws, a_out, q_out, k_out, v_out, s_out):
+def proj_kernel(
+    begin, x, gain, bias, cos, sin, cos0, sin0, wq, wk, wv, ws, a_out, q_out, k_out, v_out, s_out, c_out, n_out
+):
+    chunk = begin + pl.program_id(0)
     centred, scale = normal_rows(x[...].astype(F32), 1e-05)
     normed = (centred * scale * gain[...] + bias[...]).astype(BF16)
     a_out[...] = normed
+    first_cos, first_sin = cos0[pl.ds(chunk, 1), :], sin0[pl.ds(chunk, 1), :]
+    cosines = cos[...] * first_cos - sin[...] * first_sin
+    sines = sin[...] * first_cos + cos[...] * first_sin
+    c_out[...] = cosines
+    n_out[...] = sines
     query = product_nn(normed, wq[...])
     key = product_nn(normed, wk[...])
     for first in range(0, query.shape[1], KEY):
         part = slice(first, first + KEY)
-        q_out[:, part] = rotate(query[:, part], cos[...], sin[...], 1.0).astype(BF16)
-        turned = rotate(key[:, part], cos[...], sin[...], 1.0) * float(KEY) ** (-0.5)
+        q_out[:, part] = rotate(query[:, part], cosines, sines, 1.0).astype(BF16)
+        turned = rotate(key[:, part], cosines, sines, 1.0) * float(KEY) ** (-0.5)
         k_out[:, part] = turned.astype(BF16)
     v_out[...] = product_nn(normed, wv[...]).astype(BF16)
     s_out[...] = product_nn(normed, ws[...])
 
 
-def projections(line, x, gain, bias, cos, sin, wq, wk, wv, ws):
+def projections(line, begin, end, x, gain, bias, tables, wq, wk, wv, ws, before):
     rows, width = x.shape
-
-    def rowed(columns):
-        return pl.BlockSpec((BLOCK, columns), lambda i: (i, 0))
-
     kw, vw = wq.shape[1], wv.shape[1]
+    wide = [(width, BF16), (kw, BF16), (kw, BF16), (vw, BF16), (vw, F32), (KEY, F32), (KEY, F32)]
+
+    def chunked(columns):
+        return pl.BlockSpec((BLOCK, columns), lambda i: (begin + i, 0))
+
     return line.call(
-        proj_kernel,
-        [
-            shape((rows, width), BF16),
-            shape((rows, kw), BF16),
-            shape((rows, kw), BF16),
-            shape((rows, vw), BF16),
-            shape((rows, vw), F32),
-        ],
-        [rowed(width), rowed(kw), rowed(kw), rowed(vw), rowed(vw)],
-        [x, gain, bias, cos, sin, wq, wk, wv, ws],
-        [
-            rowed(width),
-            const_spec((1, width)),
-            const_spec((1, width)),
-            rowed(KEY),
-            rowed(KEY),
-            once_spec(wq.shape),
-            once_spec(wk.shape),
-            once_spec(wv.shape),
-            once_spec(ws.shape),
-        ],
-        grid=(rows // BLOCK,),
+        functools.partial(proj_kernel, begin),
+        [shape((rows, columns), kind) for columns, kind in wide],
+        [chunked(columns) for columns, _ in wide],
+        [x, gain, bias, *tables, wq, wk, wv, ws],
+        [chunked(width), const_spec((1, width)), const_spec((1, width))]
+        + [const_spec(table.shape) for table in tables]
+        + [once_spec(w.shape) for w in (wq, wk, wv, ws)],
+        grid=(end - begin,),
+        onto=() if before is None else tuple(enumerate(before)),
     )
 
 
 TILES = 4
 
 
-def retain_kernel(chunk, q, k, v, switch, seg_col, seg_row, logs, w, chip, u_out, o_out, p_out, full, sent, got, s1, s2):
+def retain_kernel(chunk, q, k, v, switch, seg_row, logs, w, chip, u_out, o_out, p_out, full, sent, got, s1, s2):
     meet_other_core()
+    seg_rows = down_rows(seg_row[:, chunk * BLOCK : (chunk + 1) * BLOCK])
     heads = q.shape[1] // KEY
     low = first_key_block(chunk)
     for head in range(heads):
@@ -233,7 +235,7 @@
         for block in range(low, chunk + 1):
             rows = slice(block * BLOCK, (block + 1) * BLOCK)
             raw = product_nt(q[:, kpart], k[rows, kpart])
-            mask = decay_block(logs[head], seg_col[...], seg_row[:, rows], chunk * BLOCK, block * BLOCK)
+            mask = decay_block(logs[head], seg_rows, seg_row[:, rows], chunk * BLOCK, block * BLOCK)
             weights = (raw * mask).astype(BF16)
             p_out[head, :, (block - low) * BLOCK : (block - low + 1) * BLOCK] = weights
             part = product_nn(weights, v[rows, vpart])
@@ -256,31 +258,31 @@
         chip[:, columns] = full[core_rows(True, 0), columns] + got[j]
 
 
-def retention(line, chunk, q, k, v, switch, seg_col, seg_row, logs, w):
-    kw, vw, width = q.shape[1], v.shape[1], w.shape[1]
+def retention(line, chunk, q, k, v, switch, seg_row, logs, w, before):
+    rows, kw = q.shape
+    vw, width = v.shape[1], w.shape[1]
     heads = kw // KEY
     blocks = chunk + 1 - first_key_block(chunk)
     return line.call(
         functools.partial(retain_kernel, chunk),
         [
             shape((HALF, width), F32),
-            shape((BLOCK, vw), BF16),
-            shape((BLOCK, vw), F32),
+            shape((rows, vw), BF16),
+            shape((rows, vw), F32),
             shape((heads, BLOCK, blocks * BLOCK), BF16),
         ],
         [
             const_spec((HALF, width)),
-            const_spec((BLOCK, vw)),
-            const_spec((BLOCK, vw)),
+            row_spec(BLOCK, vw, chunk),
+            row_spec(BLOCK, vw, chunk),
             const_spec((heads, BLOCK, blocks * BLOCK)),
         ],
-        [q, k, v, switch, seg_col, seg_row, logs, w],
+        [q, k, v, switch, seg_row, logs, w],
         [
             row_spec(BLOCK, kw, chunk),
             const_spec(k.shape),
             const_spec(v.shape),
             row_spec(BLOCK, vw, chunk),
-            row_spec(BLOCK, 1, chunk),
             const_spec(seg_row.shape),
             SMEM,
             const_spec(w.shape),
@@ -292,6 +294,7 @@
             pltpu.SemaphoreType.DMA((TILES,)),
             pltpu.SemaphoreType.DMA((TILES,)),
         ],
+        onto=() if before is None else ((1, before[0]), (2, before[1])),
         paired=True,
     )
 
@@ -391,10 +394,6 @@
     )[0]
 
 
-def across_chips(values, size):
-    return lax.ppermute(values, "tensor", [(i, i ^ 2) for i in range(size)])
-
-
 def shared_kernel(work, in_count, *refs):
     ins, out = refs[:in_count], refs[in_count]
     extras, (sent, got, s1, s2) = refs[in_count + 1 : -4], refs[-4:]
@@ -416,8 +415,8 @@
     half = rows // 2
     return line.call(
         functools.partial(shared_kernel, work, len(ins)),
-        [shape((total_rows, width), kind)] + [shape(dims, F32) for dims in extras],
-        [row_spec(rows, width, chunk)] + [const_spec(dims) for dims in extras],
+        [shape((total_rows, width), kind)] + [shape(dims, F32) for dims, _ in extras],
+        [row_spec(rows, width, chunk)] + [spec for _, spec in extras],
         ins,
         in_specs,
         scratch=[
@@ -426,9 +425,38 @@
             pltpu.SemaphoreType.DMA((half // HALF,)),
             pltpu.SemaphoreType.DMA((half // HALF,)),
         ],
-        onto=() if before is None else ((0, before),),
+        onto=before,
         paired=True,
     )
+
+
+def core_half_kernel(x, out):
+    out[...] = x[core_rows(True, 0), :].astype(F32)
+
+
+def core_half(line, x):
+    rows, width = x.shape
+    return line.call(
+        core_half_kernel,
+        [shape((rows // 2, width), F32)],
+        [pl.BlockSpec((HALF, width), lambda i: (i, 0))],
+        [x],
+        [pl.BlockSpec((BLOCK, width), lambda i: (i, 0))],
+        grid=(rows // BLOCK,),
+    )[0]
+
+
+def partner_work(n, part, rows, got, gain, bias):
+    centred, scale = normal_rows(got[part, :], 1e-05)
+    return (centred * scale * gain[...] + bias[...]).astype(BF16).astype(F32)
+
+
+def partner_rows(line, got, gain, bias):
+    half, width = got.shape
+    specs = [const_spec(got.shape), const_spec((1, width)), const_spec((1, width))]
+    return shared_rows(
+        line, partner_work, 0, 2 * half, [got, gain, bias], specs, BF16, 2 * half, width, [], ()
+    )[0]
 
 
 def norm_work(n, part, rows, chip, crossed, x, gain, bias, h_out):
@@ -439,7 +467,7 @@
 
 
 def second_norm(line, chunk, rows, chip, crossed, x, gain, bias, before):
-    width = x.shape[1]
+    total, width = x.shape
     half = rows // 2
     return shared_rows(
         line,
@@ -450,10 +478,10 @@
         [const_spec((half, width)), const_spec((half, width)), row_spec(rows, width, chunk)]
         + [const_spec((1, width))] * 2,
         BF16,
-        x.shape[0],
+        total,
         width,
-        [(half, width)],
-        before,
+        [((total // 2, width), row_spec(half, width, chunk))],
+        () if before is None else tuple(enumerate(before)),
     )
 
 
@@ -477,20 +505,21 @@
 
 
 def second_norm_back(line, chunk, rows, chip, crossed, h, gain, c, before):
-    width = c.shape[1]
+    total, width = c.shape
     half = rows // 2
+    owned = row_spec(half, width, chunk)
     return shared_rows(
         line,
         mid_work,
         chunk,
         rows,
         [chip, crossed, h, gain, c],
-        [const_spec((half, width))] * 3 + [const_spec((1, width)), row_spec(rows, width, chunk)],
+        [const_spec((half, width))] * 2 + [owned, const_spec((1, width)), row_spec(rows, width, chunk)],
         BF16,
-        c.shape[0],
+        total,
         width,
-        [(half, width), (1, width), (1, width)],
-        before,
+        [((total // 2, width), owned)] + [((1, width), const_spec((1, width)))] * 2,
+        () if before is None else ((0, before[0]), (1, before[1])),
     )
 
 
@@ -501,7 +530,7 @@
 
 
 def first_norm_back(line, chunk, rows, chip, crossed, x, gain, dh, before):
-    width = x.shape[1]
+    total, width = x.shape
     half = rows // 2
     return shared_rows(
         line,
@@ -510,12 +539,12 @@
         rows,
         [chip, crossed, x, gain, dh],
         [const_spec((half, width))] * 2
-        + [row_spec(rows, width, chunk), const_spec((1, width)), const_spec((half, width))],
+        + [row_spec(rows, width, chunk), const_spec((1, width)), row_spec(half, width, chunk)],
         F32,
-        x.shape[0],
+        total,
         width,
-        [(1, width), (1, width)],
-        before,
+        [((1, width), const_spec((1, width)))] * 2,
+        () if before is None else ((0, before[0]),),
     )
 
 
@@ -523,8 +552,8 @@
     return h[part, :] + (chip[part, :] + crossed[part, :])
 
 
-def output_rows(line, chunk, rows, chip, crossed, h, total_rows, before):
-    width = h.shape[1]
+def output_rows(line, chunk, rows, chip, crossed, h, before):
+    half_total, width = h.shape
     half = rows // 2
     return shared_rows(
         line,
@@ -532,13 +561,32 @@
         chunk,
         rows,
         [chip, crossed, h],
-        [const_spec((half, width))] * 3,
+        [const_spec((half, width))] * 2 + [row_spec(half, width, chunk)],
         BF16,
-        total_rows,
+        2 * half_total,
         width,
         [],
-        before,
-    )
+        () if before is None else ((0, before),),
+    )[0]
+
+
+def copy_kernel(source, out):
+    out[...] = source[...]
+
+
+def own_copy(line, source):
+    rows, width = source.shape
+    spec = pl.BlockSpec((BLOCK, width), lambda i: (i, 0))
+    return line.call(copy_kernel, [shape(source.shape, source.dtype)], [spec], [source], [spec], grid=(rows // BLOCK,))[0]
+
+
+def add_kernel(a, b, out):
+    out[...] = a[...] + b[...]
+
+
+def add(line, a, b):
+    spec = const_spec(a.shape)
+    return line.call(add_kernel, [shape(a.shape, F32)], [spec], [a, b], [spec, spec])[0]
 
 
 def gate_kernel(dz, w, o, switch, do_out, ds_out):
@@ -573,32 +621,37 @@
     )
 
 
-def retain_back_kernel(q, k, v, do, seg_col, seg_row, logs, cos, sin, *rest):
+def retain_back_kernel(q, k, v, do, seg_row, logs, cos, sin, *rest):
     weights = rest[:CHUNKS]
-    dq_out, dk_out, dv_out, dq_sum, dk_sum, dv_sum = rest[CHUNKS:]
+    dq_out, dk_out, dv_out, both_out, dq_sum, dk_sum, dv_sum = rest[CHUNKS:]
     head = pl.program_id(0)
     dk_sum[...] = jnp.zeros_like(dk_sum)
     dv_sum[...] = jnp.zeros_like(dv_sum)
     for chunk in range(CHUNKS):
         low = first_key_block(chunk)
         here = slice(chunk * BLOCK, (chunk + 1) * BLOCK)
+        seg_rows = down_rows(seg_row[:, here])
         total = None
         for block in range(low, chunk + 1):
             rows = slice(block * BLOCK, (block + 1) * BLOCK)
             part = slice((block - low) * BLOCK, (block - low + 1) * BLOCK)
-            mask = decay_block(logs[head], seg_col[here, :], seg_row[:, rows], chunk * BLOCK, block * BLOCK)
+            mask = decay_block(logs[head], seg_rows, seg_row[:, rows], chunk * BLOCK, block * BLOCK)
             scores = (product_nt(do[here, :], v[rows, :]) * mask).astype(BF16)
             dv_sum[rows, :] += product_tn(weights[chunk][0, :, part], do[here, :])
             dk_sum[rows, :] += product_tn(scores, q[here, :])
             term = product_nn(scores, k[rows, :])
             total = term if total is None else total + term
         dq_sum[here, :] = total
-    dq_out[...] = rotate(dq_sum[...], cos[...], sin[...], -1.0).astype(BF16)
-    dk_out[...] = (rotate(dk_sum[...], cos[...], sin[...], -1.0) * float(KEY) ** (-0.5)).astype(BF16)
+    dq = rotate(dq_sum[...], cos[...], sin[...], -1.0).astype(BF16)
+    dk = (rotate(dk_sum[...], cos[...], sin[...], -1.0) * float(KEY) ** (-0.5)).astype(BF16)
+    dq_out[...] = dq
+    dk_out[...] = dk
+    both_out[:, :KEY] = dq
+    both_out[:, KEY:] = dk
     dv_out[...] = dv_sum[...].astype(BF16)
 
 
-def retention_back(line, q, k, v, do, seg_col, seg_row, logs, cos, sin, weights):
+def retention_back(line, q, k, v, do, seg_row, logs, cos, sin, weights):
     rows, kw = q.shape
     vw = v.shape[1]
 
@@ -607,15 +660,14 @@
 
     return line.call(
         retain_back_kernel,
-        [shape((rows, kw), BF16), shape((rows, kw), BF16), shape((rows, vw), BF16)],
-        [headed(KEY), headed(KEY), headed(VALUE)],
-        [q, k, v, do, seg_col, seg_row, logs, cos, sin] + list(weights),
+        [shape((rows, columns), BF16) for columns in (kw, kw, vw, 2 * kw)],
+        [headed(KEY), headed(KEY), headed(VALUE), headed(2 * KEY)],
+        [q, k, v, do, seg_row, logs, cos, sin] + list(weights),
         [
             headed(KEY),
             headed(KEY),
             headed(VALUE),
             headed(VALUE),
-            const_spec(seg_col.shape),
             const_spec(seg_row.shape),
             SMEM,
             const_spec(cos.shape),
@@ -627,86 +679,240 @@
     )
 
 
-def block_kernel(by_rows, extra, where, left, right, *refs):
+def outer_place(where, position, groups):
+    return lax.rem(where[1] + 2 * groups - 1 - position, groups)
+
+
+def column_block(where, position, groups, own):
+    return outer_place(where, position, groups) * 2 + (where[0] if own else 1 - where[0])
+
+
+def plain_block(where, left, right, by_rows, groups, position, own, extra):
+    width = (left if by_rows else right).shape[1] // (2 * groups)
+    column = column_block(where, position, groups, own) * width
+    if by_rows:
+        return product_tn(lax.dynamic_slice_in_dim(left, column, width, 1), right)
+    block = product_tn(left, lax.dynamic_slice_in_dim(right, column, width, 1))
+    if extra:
+        more = lax.dynamic_slice_in_dim(extra[0] + extra[1], column, width, 1)
+        block = jnp.concatenate([block, more], axis=0)
+    return block
+
+
+def sent_kernel(where, left, right, *rest):
+    extra, out = rest[:-1], rest[-1]
+    rows = left.shape[1]
+    out[0, :rows] = product_tn(left[...], right[...])
+    if extra:
+        out[0, rows:] = extra[0][...] + extra[1][...]
+
+
+def sent_blocks(line, where, left, right, by_rows, groups, first, count, extra=()):
+    width = (left if by_rows else right).shape[1] // (2 * groups)
+    if width % 128:
+        blocks = [plain_block(where, left, right, by_rows, groups, first + j, False, extra) for j in range(count)]
+        return jnp.stack(blocks)
+    rows = left.shape[0]
+    moving = pl.BlockSpec((rows, width), lambda j, w: (0, column_block(w, first + j, groups, False)))
+    more = extra[0].shape[0] if extra else 0
+    block = (width, right.shape[1]) if by_rows else (left.shape[1] + more, width)
+    specs = [moving if by_rows else const_spec(left.shape), const_spec(right.shape) if by_rows else moving]
+    small = pl.BlockSpec((more, width), lambda j, w: (0, column_block(w, first + j, groups, False)))
+    return line.call(
+        sent_kernel,
+        [shape((count,) + block, F32)],
+        [pl.BlockSpec((1,) + block, lambda j, w: (j, 0, 0))],
+        [left, right, *extra],
+        specs + [small] * len(extra),
+        grid=(count,),
+        scalars=where,
+    )[0]
+
+
+def kept_kernel(has_travelling, extra_count, where, left, right, received, *rest):
+    more, rest = rest[:extra_count], rest[extra_count:]
     total = product_tn(left[...], right[...])
-    for term in refs[:extra]:
-        total = total + term[...].reshape(total.shape)
-    out = refs[extra]
-    out[...] = total.reshape(out.shape)
-
-
-class Weight:
-    def __init__(self, line, where, left, right, by_rows, dp):
-        self.line, self.where, self.left, self.right, self.by_rows, self.dp = line, where, left, right, by_rows, dp
-        self.groups = dp // 2
-        split = left if by_rows else right
-        self.width = split.shape[1] // dp
-        self.block = (self.width, right.shape[1]) if by_rows else (left.shape[1], self.width)
-
-    def blocks(self, position, count, own, received=None, travelling=None):
-        groups, width = self.groups, self.width
-        if width % 128:
-            return self.plain_blocks(position, count, own, received, travelling)
-
-        def column(j, where):
-            outer = lax.rem(where[1] + 2 * groups - 1 - position - j, groups)
-            return outer * 2 + (where[0] if own else 1 - where[0])
-
-        rows = self.left.shape[0]
-        moving = pl.BlockSpec((rows, width), lambda j, where: (0, column(j, where)))
-        left = moving if self.by_rows else const_spec(self.left.shape)
-        right = const_spec(self.right.shape) if self.by_rows else moving
-        ins, specs = [self.left, self.right], [left, right]
-        if received is not None:
-            ins.append(received)
-            specs.append(pl.BlockSpec((1,) + self.block, lambda j, where: (position + j, 0, 0)))
-        if travelling is not None:
-            ins.append(travelling)
-            specs.append(const_spec(self.block))
-        if received is None:
-            out, out_spec = (count,) + self.block, pl.BlockSpec((1,) + self.block, lambda j, where: (j, 0, 0))
+    rows = total.shape[0]
+    total = total + received[0, :rows]
+    if has_travelling:
+        total = total + rest[0][:rows]
+    if not extra_count:
+        rest[-1][...] = total
+        return
+    small = more[0][...] + more[1][...] + received[0, rows:]
+    if has_travelling:
+        small = small + rest[0][rows:]
+    outs = rest[1:] if has_travelling else rest
+    outs[0][:rows] = total
+    if len(outs) == 2:
+        outs[1][...] = small
+    else:
+        outs[0][rows:] = small
+
+
+def kept_block(
+    line, where, left, right, by_rows, groups, position, received, index, travelling, extra=(), last=False
+):
+    width = (left if by_rows else right).shape[1] // (2 * groups)
+    if width % 128:
+        block = plain_block(where, left, right, by_rows, groups, position, True, extra) + received[index]
+        block = block if travelling is None else block + travelling
+        return (block[: left.shape[1]], block[left.shape[1] :]) if extra and last else block
+    if extra:
+        return extended_block(line, where, left, right, groups, position, received, index, travelling, extra, last)
+    rows, tiles = left.shape[0], 2
+    moving = pl.BlockSpec((rows, width), lambda j, w: (0, column_block(w, position, groups, True)))
+    if by_rows:
+        part = right.shape[1] // tiles
+        left_spec, right_spec = moving, pl.BlockSpec((rows, part), lambda j, w: (0, j))
+        block, piece, at = (width, right.shape[1]), (width, part), lambda j: (0, j)
+    else:
+        part = left.shape[1] // tiles
+        left_spec, right_spec = pl.BlockSpec((rows, part), lambda j, w: (0, j)), moving
+        block, piece, at = (left.shape[1], width), (part, width), lambda j: (j, 0)
+    flat = pl.BlockSpec(piece, lambda j, w: at(j))
+    ins = [left, right, received] + ([] if travelling is None else [travelling])
+    specs = [left_spec, right_spec, pl.BlockSpec((1,) + piece, lambda j, w: (index,) + at(j))]
+    return line.call(
+        functools.partial(kept_kernel, travelling is not None, 0),
+        [shape(block, F32)],
+        [flat],
+        ins,
+        specs + ([] if travelling is None else [flat]),
+        grid=(tiles,),
+        scalars=where,
+    )[0]
+
+
+def extended_block(line, where, left, right, groups, position, received, index, travelling, extra, last):
+    width = right.shape[1] // (2 * groups)
+    rows, more = left.shape[0], extra[0].shape[0]
+    block = (left.shape[1] + more, width)
+    moving = pl.BlockSpec((rows, width), lambda j, w: (0, column_block(w, position, groups, True)))
+    small = pl.BlockSpec((more, width), lambda j, w: (0, column_block(w, position, groups, True)))
+    ins = [left, right, received, *extra] + ([] if travelling is None else [travelling])
+    specs = [const_spec(left.shape), moving, pl.BlockSpec((1,) + block, lambda j, w: (index, 0, 0)), small, small]
+    outs = [(left.shape[1], width), (more, width)] if last else [block]
+    result = line.call(
+        functools.partial(kept_kernel, travelling is not None, len(extra)),
+        [shape(dims, F32) for dims in outs],
+        [const_spec(dims) for dims in outs],
+        ins,
+        specs + ([] if travelling is None else [const_spec(block)]),
+        scalars=where,
+    )
+    return result if last else result[0]
+
+
+def wide_kernel(pair_count, has_travelling, last, where, *refs):
+    total = None
+    for n in range(pair_count):
+        part = product_tn(refs[2 * n][...], refs[2 * n + 1][...].astype(BF16))
+        total = part if total is None else total + part
+    rest = refs[2 * pair_count :]
+    if has_travelling:
+        total = total + rest[0][...]
+        rest = rest[1:]
+    if not last:
+        rest[0][...] = total
+        return
+    send, keep, full = rest
+    full[...] = total
+    half = send.shape[0]
+    keep[...] = full[pl.ds(pl.multiple_of(where[0] * half, half), half), :]
+    send[...] = full[pl.ds(pl.multiple_of((1 - where[0]) * half, half), half), :]
+
+
+def wide_block(line, where, pairs, groups, position, travelling, last, columns):
+    rows, depth = pairs[0][0].shape
+    width = depth // groups
+    tiles = 2
+    part = columns // tiles
+    ins, specs = [], []
+    for left, right in pairs:
+        ins += [left, right]
+        specs.append(pl.BlockSpec((rows, width), lambda j, w: (0, outer_place(w, position, groups))))
+        if right.shape[1] > columns:
+            specs.append(pl.BlockSpec((rows, part), lambda j, w: (0, w[0] * tiles + j)))
         else:
-            out, out_spec = self.block, const_spec(self.block)
-        return self.line.call(
-            functools.partial(block_kernel, self.by_rows, len(ins) - 2),
-            [shape(out, F32)],
-            [out_spec],
-            ins,
-            specs,
-            grid=(count,),
-            scalars=self.where,
-        )[0]
-
-    def plain_blocks(self, position, count, own, received, travelling):
-        where, groups, width = self.where, self.groups, self.width
-        parts = []
-        for j in range(position, position + count):
-            outer = lax.rem(where[1] + 2 * groups - 1 - j, groups)
-            column = (outer * 2 + (where[0] if own else 1 - where[0])) * width
-            if self.by_rows:
-                part = product_tn(lax.dynamic_slice_in_dim(self.left, column, width, 1), self.right)
-            else:
-                part = product_tn(self.left, lax.dynamic_slice_in_dim(self.right, column, width, 1))
-            if received is not None:
-                part = part + received[j]
-            if travelling is not None:
-                part = part + travelling
-            parts.append(part)
-        return parts[0] if received is not None else jnp.stack(parts)
-
-    def steps(self):
-        dp, groups = self.dp, self.groups
-        sent = self.blocks(0, groups, False)
-        received = lax.ppermute(sent, "dp", [(i, i ^ 1) for i in range(dp)])
-        yield None
-        travelling = None
-        for position in range(groups):
-            block = self.blocks(position, 1, True, received, travelling)
-            if position < groups - 1:
-                travelling = lax.ppermute(block, "dp", [(i, (i + 2) % dp) for i in range(dp)])
-                yield None
-            else:
-                yield block
+            specs.append(pl.BlockSpec((rows, part), lambda j, w: (0, j)))
+    if travelling is not None:
+        ins.append(travelling)
+        specs.append(pl.BlockSpec((width, part), lambda j, w: (0, j)))
+    height = width // 2 if last else width
+    result = line.call(
+        functools.partial(wide_kernel, len(pairs), travelling is not None, last),
+        [shape((height, columns), F32)] * (2 if last else 1),
+        [pl.BlockSpec((height, part), lambda j, w: (0, j))] * (2 if last else 1),
+        ins,
+        specs,
+        grid=(tiles,),
+        scalars=where,
+        scratch=[pltpu.VMEM((width, part), F32)] if last else [],
+    )
+    return result if last else result[0]
+
+
+def half_kernel(where, source, out):
+    out[...] = source[...].astype(F32)
+
+
+def neighbour_half(line, where, source):
+    rows, columns = source.shape
+    part = rows // 2
+    return line.call(
+        half_kernel,
+        [shape((rows, columns // 2), F32)],
+        [pl.BlockSpec((part, columns // 2), lambda i, w: (i, 0))],
+        [source],
+        [pl.BlockSpec((part, columns // 2), lambda i, w: (i, 1 - w[0]))],
+        grid=(2,),
+        scalars=where,
+    )[0]
+
+
+def join_kernel(where, keep, got, *outs):
+    mine, theirs = keep[...], got[...]
+    low = where[0] == 0
+    first, second = jnp.where(low, mine, theirs), jnp.where(low, theirs, mine)
+    part = first.shape[1] // len(outs)
+    for n, out in enumerate(outs):
+        out[:, :part] = first[:, n * part : (n + 1) * part]
+        out[:, part:] = second[:, n * part : (n + 1) * part]
+
+
+def join_halves(line, where, keep, got, count):
+    rows, columns = keep.shape
+    out = (rows, 2 * columns // count)
+    return line.call(
+        join_kernel,
+        [shape(out, F32)] * count,
+        [const_spec(out)] * count,
+        [keep, got],
+        [const_spec(keep.shape)] * 2,
+        scalars=where,
+    )
+
+
+class Plan:
+    def __init__(self, line):
+        self.line, self.steps, self.found, self.sent = line, {}, {}, {}
+
+    def step(self, name, needs, work):
+        self.steps[name] = (needs, work)
+
+    def run(self, *names):
+        for name in names:
+            if name.startswith("~"):
+                if name[1:] in self.sent:
+                    self.line.last.append(self.sent[name[1:]])
+            elif name in self.steps and name not in self.found:
+                needs, work = self.steps[name]
+                self.run(*needs)
+                self.found[name] = work()
+
+    def __getitem__(self, name):
+        return self.found[name]
 
 
 def on_device(
@@ -730,139 +936,216 @@
     cotangent,
 ):
     line = Line()
+    plan = Plan(line)
+    groups = dp // 2
     place = lax.axis_index("dp")
     where = jnp.stack([lax.rem(place, 2), lax.div(place, 2)]).astype(jnp.int32)
-    cos, sin = angle_tables(SEQ_LEN)
+    tables = angle_tables(SEQ_LEN)
     logs = jnp.log1p(-jnp.exp2(-(decay_order + 5).astype(F32)))
     seg_row = segments.reshape(1, SEQ_LEN)
-    seg_col = segments.reshape(SEQ_LEN, 1)
     gain1, bias1, gain2, bias2 = (v.reshape(1, -1) for v in (ln1_gain, ln1_bias, ln2_gain, ln2_bias))
-    rows_here = inputs.shape[0]
-
-    normed, query, key, value, switch = projections(
-        line, inputs, gain1, bias1, cos, sin, w_query, w_key, w_value, w_swish
-    )
-    every = range(CHUNKS)
-    firsts, gated, retained, weights = [], [], [], []
-    for chunk in every:
-        chip, u, o, p = retention(line, chunk, query, key, value, switch, seg_col, seg_row, logs, w_out)
-        firsts.append((chip, across_chips(chip, tensor)))
-        gated.append(u)
-        retained.append(o)
-        weights.append(p)
-    middle, normed2, inner = [], None, None
-    for chunk in every:
-        normed2, h = second_norm(line, chunk, BLOCK, *firsts[chunk], inputs, gain2, bias2, normed2)
-        inner = feed_forward(line, chunk, BLOCK, normed2, cotangent, w_gate, w_up, w_down, inner)
-        middle.append(h)
-    hidden, back_gate, back_up = inner
-    gated, retained = jnp.concatenate(gated, axis=0), jnp.concatenate(retained, axis=0)
-    results = {}
-
-    def gradient(name, left, right, by_rows):
-        for step in Weight(line, where, left, right, by_rows, dp).steps():
-            if step is not None:
-                results[name] = step
-            yield
-
     rows = 2 * BLOCK
+
+    def beside(name, values):
+        plan.sent[name] = lax.ppermute(values, "dp", [(i, i ^ 1) for i in range(dp)])
+        return plan.sent[name]
+
+    def onward(name, values):
+        plan.sent[name] = lax.ppermute(values, "dp", [(i, (i + 2) % dp) for i in range(dp)])
+        return plan.sent[name]
+
+    def across(name, values):
+        plan.sent[name] = lax.ppermute(values, "tensor", [(i, i ^ 2) for i in range(tensor)])
+        return plan.sent[name]
+
+
+    def projected(n, begin, end):
+        before = plan["P0"] if n else None
+        return projections(line, begin, end, inputs, gain1, bias1, tables, w_query, w_key, w_value, w_swish, before)
+
+    def retained(i):
+        a, q, k, v, switch, cos, sin = plan["P1" if i else "P0"]
+        before = plan[f"R{i - 1}"][1:3] if i else None
+        chip, u, o, p = retention(line, i, q, k, v, switch, seg_row, logs, w_out, before)
+        return (chip, across(f"R{i}", chip)), u, o, p
+
+    def normed(i):
+        before = plan[f"N{i - 1}"] if i else None
+        return second_norm(line, i, BLOCK, *plan[f"R{i}"][0], inputs, gain2, bias2, before)
+
+    def fed(i):
+        before = plan[f"F{i - 1}"] if i else None
+        return feed_forward(line, i, BLOCK, plan[f"N{i}"][0], cotangent, w_gate, w_up, w_down, before)
+
+    last = CHUNKS - 1
+    plan.step("P0", [], lambda: projected(0, 0, 1))
+    plan.step("R0", ["P0"], lambda: retained(0))
+    plan.step("P1", ["R0"], lambda: projected(1, 1, CHUNKS))
+    for i in range(CHUNKS):
+        plan.step(f"R{i}", ["P1", f"R{i - 1}"] if i else ["P0"], lambda i=i: retained(i))
+        plan.step(f"N{i}", [f"R{i}"] + ([f"N{i - 1}"] if i else []), lambda i=i: normed(i))
+        plan.step(f"F{i}", [f"N{i}"] + ([f"F{i - 1}"] if i else []), lambda i=i: fed(i))
+    plan.step("H", [], lambda: beside("H", core_half(line, inputs)))
+    plan.step("G", ["H"], lambda: partner_rows(line, plan["H"], gain1, bias1))
+
+    def first(n):
+        return plan["P1"][n]
+
+
+    def summed(name, lefts, rights, transposed, i):
+        chip = chip_sum(line, rows, lefts, rights, transposed, i)
+        return chip, across(f"{name}{i}", chip)
+
     pair = range(2)
-    joined = [jnp.concatenate([middle[2 * i], middle[2 * i + 1]], axis=0) for i in pair]
-
-    def summed(lefts, rights, transposed, chunk):
-        chip = chip_sum(line, rows, lefts, rights, transposed, chunk)
-        return chip, across_chips(chip, tensor)
-
-    down = gradient("down", hidden, cotangent, False)
-    gate = gradient("gate", normed2, back_gate, True)
-    up = gradient("up", normed2, back_up, True)
-    next(down)
-    seconds = [summed([back_gate, back_up], [w_gate, w_up], True, i) for i in pair]
-    next(gate)
-    next(up)
-    dz, dh, ln2g, ln2b = None, [], [], []
-
-    def middle_step(i):
-        out, own, one, two = second_norm_back(line, i, rows, *seconds[i], joined[i], gain2, cotangent, dz)
-        dh.append(own)
-        ln2g.append(one)
-        ln2b.append(two)
-        return out
-
-    dz = middle_step(0)
-    next(down)
-    dz = middle_step(1)
-    do, ds = gate_back(line, dz, w_out, retained, switch)
-    next(down)
-    dq, dk, dv = retention_back(line, query, key, value, do, seg_col, seg_row, logs, cos, sin, weights)
-    next(down)
-    thirds = [
-        summed([dq, dk, dv, ds], [w_query, w_key, w_value, w_swish], True, i) for i in pair
-    ]
-    out = gradient("out", gated, dz, False)
-    next(down)
-    next(out)
-    next(gate)
-    swish = gradient("swish", normed, ds, True)
-    vgrad = gradient("value", normed, dv, True)
-    qgrad = gradient("query", normed, dq, True)
-    kgrad = gradient("key", normed, dk, True)
-    next(gate)
-    grad_inputs, ln1g, ln1b = None, [], []
-
-    def first_step(i):
-        out, one, two = first_norm_back(line, i, rows, *thirds[i], inputs, gain1, dh[i], grad_inputs)
-        ln1g.append(one)
-        ln1b.append(two)
-        return out
-
-    grad_inputs = first_step(0)
-    next(gate)
-    grad_inputs = first_step(1)
-    next(gate)
-    fourths = [summed([hidden], [w_down], False, i) for i in pair]
-    next(swish)
-    next(up)
-    small = jnp.concatenate([sum(v) for v in (ln1g, ln1b, ln2g, ln2b)], axis=0)
-    small = small + lax.ppermute(small, "tensor", [(i, i ^ 1) for i in range(tensor)])
-    small = lax.psum_scatter(small, "dp", scatter_dimension=1, tiled=True)
-    next(up)
-    output = output_rows(line, 0, rows, *fourths[0], joined[0], rows_here, None)[0]
-    next(up)
-    output = output_rows(line, 1, rows, *fourths[1], joined[1], rows_here, output)[0]
-    next(up)
-    next(vgrad)
-    next(out)
-    next(out)
-    next(out)
-    line.last.append(small)
-    next(out)
-    next(qgrad)
-    for _ in range(4):
-        next(swish)
-    next(kgrad)
-    for _ in range(4):
-        next(vgrad)
-    for _ in range(4):
-        next(qgrad)
-    for left in (down, gate, up, out, swish, vgrad, qgrad, kgrad):
-        for _ in left:
-            pass
+
+    def second_sum(i):
+        _, dg, du = plan[f"F{last}"]
+        return summed("B", [dg, du], [w_gate, w_up], True, i)
+
+    def middle_back(i):
+        before = plan["M1"] if i == 0 else None
+        return second_norm_back(line, i, rows, *plan[f"B{i}"], plan[f"N{last}"][1], gain2, cotangent, before)
+
+    def first_sum(i):
+        dq, dk, dv, _ = plan["AB"]
+        return summed("C", [dq, dk, dv, plan["GB"][1]], [w_query, w_key, w_value, w_swish], True, i)
+
+    def inputs_back(i):
+        before = plan["I1"] if i == 0 else None
+        return first_norm_back(line, i, rows, *plan[f"C{i}"], inputs, gain1, plan["M0"][1], before)
+
+    def output_part(i):
+        before = plan["O1"] if i == 0 else None
+        return output_rows(line, i, rows, *plan[f"D{i}"], plan[f"N{last}"][1], before)
+
+    def retention_grads():
+        _, q, k, v, _, cos, sin = plan["P1"]
+        weights = [plan[f"R{i}"][3] for i in range(CHUNKS)]
+        return retention_back(line, q, k, v, plan["GB"][0], seg_row, logs, cos, sin, weights)
+
+    for i in reversed(pair):
+        after = [] if i else ["M1"]
+        plan.step(f"B{i}", [f"F{last}"], lambda i=i: second_sum(i))
+        plan.step(f"M{i}", [f"B{i}"] + after, lambda i=i: middle_back(i))
+        plan.step(f"D{i}", [f"F{last}"], lambda i=i: summed("D", [plan[f"F{last}"][0]], [w_down], False, i))
+        plan.step(f"O{i}", [f"D{i}"] + ([] if i else ["O1"]), lambda i=i: output_part(i))
+    plan.step("GB", ["M0"], lambda: gate_back(line, plan["M0"][0], w_out, plan[f"R{last}"][2], first(4)))
+    plan.step("AB", ["GB"], retention_grads)
+    for i in reversed(pair):
+        plan.step(f"C{i}", ["AB"], lambda i=i: first_sum(i))
+        plan.step(f"I{i}", [f"C{i}", "M0"] + ([] if i else ["I1"]), lambda i=i: inputs_back(i))
+    plan.step("CI", ["I0"], lambda: own_copy(line, plan["I0"][0]))
+    plan.step("CO", ["O0"], lambda: own_copy(line, plan["O0"]))
+
+
+    def small_sums():
+        ln1 = [plan[f"I{i}"][n] for n in (1, 2) for i in pair]
+        ln2 = [plan[f"M{i}"][n] for n in (2, 3) for i in pair]
+        parts = ln1 + ln2
+        own = [parts[2 * n] + parts[2 * n + 1] for n in range(4)]
+        own = jnp.concatenate(own + [jnp.zeros((4, own[0].shape[1]), F32)], axis=0)
+        plan.sent["L"] = lax.ppermute(own, "tensor", [(i, i ^ 1) for i in range(tensor)])
+        return own, plan.sent["L"]
+
+    plan.step("L", ["I0", "M0"], small_sums)
+
+
+    def products(name, needs, operands, by_rows, extra=tuple):
+        cut = (groups + 1) // 2
+
+        def send(part, begin, end):
+            left, right = operands()
+            blocks = sent_blocks(line, where, left, right, by_rows, groups, begin, end - begin, extra())
+            return beside(f"S{name}{part}", blocks)
+
+        def ring(j):
+            part, index = ("A", j) if j < cut else ("B", j - cut)
+            travelling = plan[f"K{name}{j - 1}"] if j else None
+            left, right = operands()
+            received = plan[f"S{name}{part}"]
+            block = kept_block(
+                line, where, left, right, by_rows, groups, j, received, index, travelling, extra(), j == groups - 1
+            )
+            return onward(f"K{name}{j}", block) if j < groups - 1 else block
+
+        plan.step(f"S{name}A", needs, lambda: send("A", 0, cut))
+        plan.step(f"S{name}B", needs, lambda: send("B", cut, groups))
+        for j in range(groups):
+            before = [f"K{name}{j - 1}"] if j else []
+            plan.step(f"K{name}{j}", [f"S{name}A" if j < cut else f"S{name}B"] + before, lambda j=j: ring(j))
+        return lambda: plan[f"K{name}{groups - 1}"]
+
+
+    def ring_first(name, needs, operands):
+        def ring(j):
+            travelling = plan[f"K{name}{j - 1}"] if j else None
+            left, right = operands()
+            block = wide_block(
+                line, where, [(left, right)], groups, j, travelling, j == groups - 1, right.shape[1]
+            )
+            if j < groups - 1:
+                return onward(f"K{name}{j}", block)
+            return beside(f"K{name}{j}", block[0]), block[1]
+
+        for j in range(groups):
+            plan.step(f"K{name}{j}", [f"K{name}{j - 1}"] if j else needs, lambda j=j: ring(j))
+        plan.step(f"E{name}", [f"K{name}{groups - 1}"], lambda: add(line, *plan[f"K{name}{groups - 1}"]))
+        return lambda: plan[f"E{name}"]
+
+
+    def shares(name, needs, operand, count):
+        def ring(j):
+            travelling = plan[f"J{name}{j - 1}"] if j else None
+            right = operand()
+            pairs = [(first(0), right), (plan["G"], plan[f"T{name}"])]
+            block = wide_block(
+                line, where, pairs, groups, j, travelling, j == groups - 1, right.shape[1] // 2
+            )
+            if j < groups - 1:
+                return onward(f"J{name}{j}", block)
+            return block[1], beside(f"J{name}{j}", block[0])
+
+        plan.step(f"T{name}", needs, lambda: beside(f"T{name}", neighbour_half(line, where, operand())))
+        for j in range(groups):
+            plan.step(f"J{name}{j}", [f"T{name}", "G"] + ([f"J{name}{j - 1}"] if j else []), lambda j=j: ring(j))
+        plan.step(f"E{name}", [f"J{name}{groups - 1}"], lambda: join_halves(line, where, *plan[f"J{name}{groups - 1}"], count))
+        return lambda: plan[f"E{name}"]
+
+    fed_all = lambda n: plan[f"F{last}"][n]
+    normed2 = lambda: plan[f"N{last}"][0]
+    down = products("d", [f"F{last}"], lambda: (fed_all(0), cotangent), False)
+    gate = products("g", [f"F{last}"], lambda: (normed2(), fed_all(1)), True)
+    up = ring_first("u", [f"F{last}"], lambda: (normed2(), fed_all(2)))
+    out = products("o", ["M0", "L"], lambda: (plan[f"R{last}"][1], plan["M0"][0]), False, lambda: plan["L"])
+    swish = shares("s", ["GB"], lambda: plan["GB"][1], 1)
+    vgrad = shares("v", ["AB"], lambda: plan["AB"][2], 1)
+    both = shares("q", ["AB"], lambda: plan["AB"][3], 2)
+
+    plan.run(
+        "P0", "R0", "P1", "R1", "N0", "R2", "R3", "F0", "N1", "F1", "H", "N2", "F2", "N3", "F3", "Ku0", "B1", "SdA",
+        "B0", "Ku1", "SgA", "M1", "SdB", "G", "Kd0", "Ku2", "M0", "Kd1", "GB", "AB", "Ts", "Kg0", "C1", "Tv", "C0",
+        "Ku3", "Kg1", "Tq", "Kd2", "Js0", "SgB", "~Kg1", "D1", "I1", "Kd3", "Jv0", "I0", "L", "Js1", "SoA", "Jv1",
+        "Jq0", "Js2", "D0", "Jv2", "SoB", "Jq1", "~Js2", "Kg2", "Ko0", "O1", "Jq2", "Js3", "CI", "Ko1", "O0", "CO",
+        "Jq3", "Eu", "Eq", "Ko2", "Es", "Jv3", "Ev", "Ko3", "Kg3",
+    )
+    plan.run(*plan.steps)
+    query, key = both()
+    grad_out, small = out()
     return (
-        output,
-        grad_inputs,
+        plan["CO"],
+        plan["CI"],
         small[0],
         small[1],
-        results["query"],
-        results["key"],
-        results["value"],
-        results["swish"],
-        results["out"],
+        query,
+        key,
+        vgrad()[0],
+        swish()[0],
+        grad_out,
         small[2],
         small[3],
-        results["gate"],
-        results["up"],
-        results["down"],
+        gate(),
+        up(),
+        down(),
     )
 
 

time: 1090 us -> 734 us (0.67)
  waiting for transfers between devices: 526 us -> 169 us
  Pallas kernels: 473 us -> 502 us
  local copies, waits for them, and re-layouts: 33.2 us -> 4.57 us
  starting transfers between devices: 28.8 us -> 44.1 us
  between operations: 14.8 us -> 1.35 us
    ppermute x43 -> x46, waiting for transfers between devices: 456 us -> 169 us  [the longest x21 127 us: onward(): lax.ppermute(values, 'dp', [(i, (i + 2) % dp) for i in range(dp)])]
    unnamed x2 -> x0, waiting for transfers between devices: 70.3 us -> none
    pallas_call x67 -> x73, Pallas kernels: 473 us -> 502 us  [call(): pl.pallas_call(body, out_shape=tuple(outs), grid_spec=pltpu.PrefetchScala...]
    unnamed x51 -> x28, local copies, waits for them, and re-layouts: 27.9 us -> 3.06 us
    ppermute x43 -> x46, starting transfers between devices: 28.7 us -> 44.1 us  [the longest x14 16 us: beside(): lax.ppermute(values, 'dp', [(i, i ^ 1) for i in range(dp)])]
  transfers between devices with their start and end apart: 44 -> 46, of which waited for: 29 -> 19; matrix products, arithmetic and copies ran while one was open for 2% -> 0% of each run, Pallas kernels for 36% -> 66%
where the time goes in v2:
time: 734 us; the launch traced here: 726 us
  Pallas kernels  502 us (68%)
  waiting for transfers between devices  169 us (23%)
  starting transfers between devices  44.1 us (6%)
    pallas_call x73, Pallas kernels, call(): pl.pallas_call(body, out_shape=tuple(outs), grid_spec=pltpu.PrefetchScala...  502 us
    ppermute x21, waiting for transfers between devices, onward(): lax.ppermute(values, 'dp', [(i, (i + 2) % dp) for i in range(dp)])  127 us
    ppermute x14, waiting for transfers between devices, beside(): lax.ppermute(values, 'dp', [(i, i ^ 1) for i in range(dp)])  40.8 us
    ppermute x14, starting transfers between devices, beside(): lax.ppermute(values, 'dp', [(i, i ^ 1) for i in range(dp)])  16 us
    ppermute x21, starting transfers between devices, onward(): lax.ppermute(values, 'dp', [(i, (i + 2) % dp) for i in range(dp)])  15.7 us
  transfers between devices with their start and end apart: 46, of which 19 were waited for; matrix products, arithmetic and copies ran while one was open for 0% of the time, Pallas kernels for 66%

profile of v2, /device:TPU:0, one launch (start us, length us, event | category | flops | bytes accessed | tf_op | source)
XLA Modules:
  0.0 725.9 jit_solution(16370245470292335137)
XLA Ops:
  4.4 10.1 %shard_map.263 = (bf16[1024,2048]{1,0:T(8,128)(2,1)}, bf16[1024,512]{1,0:T(8,128)(2,1)}, bf16[1024,512]{1,0:T(8,128)(2,1)}, bf16[1024,1024]{1,0:T(8,128)(2,1)}, ...) custom-call(bf16[1024,2048]{1,0:T(8,128)(2,1)} %refs_2_.35, f32[1,2048]{1,0:T(1,128)} %bitcast.16, ...), custom_call_target="tpu_custom_call" | custom-call | flops 1 | bytes 1 | tf_op jit(solution)/shard_map/pallas_call | solution.py:108
  14.5 9.6 %shard_map.264 = (f32[128,2048]{1,0:T(8,128)}, bf16[1024,1024]{1,0:T(8,128)(2,1)}, f32[1024,1024]{1,0:T(8,128)}, bf16[2,256,256]{2,1,0:T(8,128)(2,1)}) custom-call(bf16[1024,512]{1,0:T(8,128)(2,1)} %get-tuple-element.97.refs_0_.refs_12_, bf16[1024,512]{1,0:T(8,128)(2,1)} %get-tuple-element.98.refs_1_.refs_13_, ...), custom_call_target="tpu_custom_call" | custom-call | flops 1 | bytes 1 | tf_op jit(solution)/shard_map/pallas_call | solution.py:108
  27.0 18.5 %shard_map.265 = (bf16[1024,2048]{1,0:T(8,128)(2,1)}, bf16[1024,512]{1,0:T(8,128)(2,1)}, bf16[1024,512]{1,0:T(8,128)(2,1)}, bf16[1024,1024]{1,0:T(8,128)(2,1)}, ...) custom-call(bf16[1024,2048]{1,0:T(8,128)(2,1)} %refs_2_.35, ...), custom_call_target="tpu_custom_call", output_to_operand_aliasing={{0}: (11, {}), {1}: (12, {}), {2}: (13, {}), {3}: (14, {}),... | custom-call | flops 1 | bytes 1 | tf_op jit(solution)/shard_map/pallas_call | solution.py:108
  45.5 9.7 %shard_map.266 = (f32[128,2048]{1,0:T(8,128)}, bf16[1024,1024]{1,0:T(8,128)(2,1)}, f32[1024,1024]{1,0:T(8,128)}, bf16[2,256,512]{2,1,0:T(8,128)(2,1)}) custom-call(bf16[1024,512]{1,0:T(8,128)(2,1)} %get-tuple-element.104.refs_0_, bf16[1024,512]{1,0:T(8,128)(2,1)} %get-tuple-element.105.refs_1_, ...), custom_call_target="tpu_custom_call", output_to_operand_aliasing={{1}: (7, {}), {2}: (8, {})} | custom-call | flops 1 | bytes 1 | tf_op jit(solution)/shard_map/pallas_call | solution.py:108
  61.8 10.1 %shard_map.268 = (f32[128,2048]{1,0:T(8,128)}, bf16[1024,1024]{1,0:T(8,128)(2,1)}, f32[1024,1024]{1,0:T(8,128)}, bf16[2,256,768]{2,1,0:T(8,128)(2,1)}) custom-call(bf16[1024,512]{1,0:T(8,128)(2,1)} %get-tuple-element.104.refs_0_, bf16[1024,512]{1,0:T(8,128)(2,1)} %get-tuple-element.105.refs_1_, ...), custom_call_target="tpu_custom_call", output_to_operand_aliasing={{1}: (7, {}), {2}: (8, {})} | custom-call | flops 1 | bytes 1 | tf_op jit(solution)/shard_map/pallas_call | solution.py:108
  73.9 10.1 %shard_map.269 = (f32[128,2048]{1,0:T(8,128)}, bf16[1024,1024]{1,0:T(8,128)(2,1)}, f32[1024,1024]{1,0:T(8,128)}, bf16[2,256,768]{2,1,0:T(8,128)(2,1)}) custom-call(bf16[1024,512]{1,0:T(8,128)(2,1)} %get-tuple-element.104.refs_0_, bf16[1024,512]{1,0:T(8,128)(2,1)} %get-tuple-element.105.refs_1_, ...), custom_call_target="tpu_custom_call", output_to_operand_aliasing={{1}: (7, {}), {2}: (8, {})} | custom-call | flops 1 | bytes 1 | tf_op jit(solution)/shard_map/pallas_call | solution.py:108
  84.1 9.0 %shard_map.270 = (bf16[1024,1024]{1,0:T(8,128)(2,1)}, bf16[1024,1024]{1,0:T(8,128)(2,1)}, bf16[1024,1024]{1,0:T(8,128)(2,1)}) custom-call(bf16[1024,2048]{1,0:T(8,128)(2,1)} %get-tuple-element.114.refs_9_.refs_0_.refs_5_, bf16[1024,2048]{1,0:T(8,128)(2,1)} %refs_2_.34, bf16[2048,1024]{1,0:T(8,128)(2,1)} %refs_2_.28, bf16[2048,1024]{1,0:T(8,128)(2,1)} %refs_3_.11, ...), custom_call_target="tpu_custom_call" | custom-call | flops 1 | bytes 1 | tf_op jit(solution)/shard_map/pallas_call | solution.py:108
  99.7 9.0 %shard_map.272 = (bf16[1024,1024]{1,0:T(8,128)(2,1)}, bf16[1024,1024]{1,0:T(8,128)(2,1)}, bf16[1024,1024]{1,0:T(8,128)(2,1)}) custom-call(bf16[1024,2048]{1,0:T(8,128)(2,1)} %get-tuple-element.121.refs_0_.refs_5_, bf16[1024,2048]{1,0:T(8,128)(2,1)} %refs_2_.34, ...), custom_call_target="tpu_custom_call", output_to_operand_aliasing={{0}: (5, {}), {1}: (6, {}), {2}: (7, {})} | custom-call | flops 1 | bytes 1 | tf_op jit(solution)/shard_map/pallas_call | solution.py:108
  122.4 9.6 %shard_map.275 = (bf16[1024,1024]{1,0:T(8,128)(2,1)}, bf16[1024,1024]{1,0:T(8,128)(2,1)}, bf16[1024,1024]{1,0:T(8,128)(2,1)}) custom-call(bf16[1024,2048]{1,0:T(8,128)(2,1)} %get-tuple-element.126.refs_0_.refs_5_, bf16[1024,2048]{1,0:T(8,128)(2,1)} %refs_2_.34, ...), custom_call_target="tpu_custom_call", output_to_operand_aliasing={{0}: (5, {}), {1}: (6, {}), {2}: (7, {})} | custom-call | flops 1 | bytes 1 | tf_op jit(solution)/shard_map/pallas_call | solution.py:108
  138.5 9.0 %shard_map.277 = (bf16[1024,1024]{1,0:T(8,128)(2,1)}, bf16[1024,1024]{1,0:T(8,128)(2,1)}, bf16[1024,1024]{1,0:T(8,128)(2,1)}) custom-call(bf16[1024,2048]{1,0:T(8,128)(2,1)} %get-tuple-element.131.refs_0_.refs_1_, bf16[1024,2048]{1,0:T(8,128)(2,1)} %refs_2_.34, ...), custom_call_target="tpu_custom_call", output_to_operand_aliasing={{0}: (5, {}), {1}: (6, {}), {2}: (7, {})} | custom-call | flops 1 | bytes 1 | tf_op jit(solution)/shard_map/pallas_call | solution.py:108
  153.8 11.1 %shard_map.279.refs_3_.refs_0_ = f32[256,2048]{1,0:T(8,128)} custom-call(bf16[1024,1024]{1,0:T(8,128)(2,1)} %get-tuple-element.135.refs_0_.refs_2_, bf16[1024,1024]{1,0:T(8,128)(2,1)} %get-tuple-element.136.refs_2_.refs_1_, bf16[2048,1024]{1,0:T(8,128)(2,1)} %refs_2_.28, bf16[2048,1024]{1,0:T(8,128)(2,1)} %refs_3_.11, f32[512,1024]{1,0:T(8,128)} %shard_map.278.refs_4_), custom_call_target="tpu_custom_call" | custom-call | flops 1 | bytes 1 | tf_op jit(solution)/shard_map/pallas_call | solution.py:108
  172.1 11.2 %shard_map.281.refs_4_.refs_0_ = f32[256,2048]{1,0:T(8,128)} custom-call(bf16[1024,1024]{1,0:T(8,128)(2,1)} %get-tuple-element.135.refs_0_.refs_2_, bf16[1024,1024]{1,0:T(8,128)(2,1)} %get-tuple-element.136.refs_2_.refs_1_, bf16[2048,1024]{1,0:T(8,128)(2,1)} %refs_2_.28, bf16[2048,1024]{1,0:T(8,128)(2,1)} %refs_3_.11, f32[2,1024,256]{2,1,0:T(8,128)} %shard_map.280.refs_4_), custom_call_target="tpu_custom_call" | custom-call | flops 1 | bytes 1 | tf_op jit(solution)/shard_map/pallas_call | solution.py:108
  183.3 18.8 %collective-permute-done.6.refs_3_ = f32[512,1024]{1,0:T(8,128)} collective-permute-done((f32[512,1024]{1,0:T(8,128)}, f32[512,1024]{1,0:T(8,128)}, u32[]{:S(2)}, u32[]{:S(2)}) %collective-permute-start.6) | collective-permute-done | bytes 2097184 | tf_op jit(solution)/shard_map/ppermute | solution.py:954
  214.3 10.8 %shard_map.284 = (bf16[1024,2048]{1,0:T(8,128)(2,1)}, f32[512,2048]{1,0:T(8,128)}, f32[1,2048]{1,0:T(1,128)}, f32[1,2048]{1,0:T(1,128)}) custom-call(f32[256,2048]{1,0:T(8,128)} %shard_map.279.refs_3_.refs_0_, f32[256,2048]{1,0:T(8,128)} %collective-permute-done.5.refs_1_, f32[512,2048]{1,0:T(8,128)} %get-tuple-element.137.refs_2_, f32[1,2048]{1,0:T(1,128)} %bitcast.14, ...), custom_call_target="tpu_custom_call" | custom-call | flops 1 | bytes 1 | tf_op jit(solution)/shard_map/pallas_call | solution.py:108
  230.2 12.0 %shard_map.286.refs_4_.refs_3_ = bf16[1024,2048]{1,0:T(8,128)(2,1)} custom-call(f32[512,2048]{1,0:T(8,128)} %collective-permute-done.9.refs_0_, f32[1,2048]{1,0:T(1,128)} %bitcast.18, f32[1,2048]{1,0:T(1,128)} %bitcast.27, f32[2,1024,256]{2,1,0:T(8,128)} %shard_map.285.refs_3_), custom_call_target="tpu_custom_call" | custom-call | flops 1 | bytes 1 | tf_op jit(solution)/shard_map/pallas_call | solution.py:108
  242.2 9.8 %collective-permute-done.8.refs_3_ = f32[2,1024,256]{2,1,0:T(8,128)} collective-permute-done((f32[2,1024,256]{2,1,0:T(8,128)}, f32[2,1024,256]{2,1,0:T(8,128)}, u32[]{:S(2)}, u32[]{:S(2)}) %collective-permute-start.8) | collective-permute-done | bytes 2097184 | tf_op jit(solution)/shard_map/ppermute | solution.py:950
  266.2 10.7 %shard_map.289 = (bf16[1024,2048]{1,0:T(8,128)(2,1)}, f32[512,2048]{1,0:T(8,128)}, f32[1,2048]{1,0:T(1,128)}, f32[1,2048]{1,0:T(1,128)}) custom-call(f32[256,2048]{1,0:T(8,128)} %shard_map.281.refs_4_.refs_0_, f32[256,2048]{1,0:T(8,128)} %collective-permute-done.4.refs_1_, ...), custom_call_target="tpu_custom_call", output_to_operand_aliasing={{0}: (5, {}), {1}: (6, {})} | custom-call | flops 1 | bytes 1 | tf_op jit(solution)/shard_map/pallas_call | solution.py:108
  289.0 12.7 %shard_map.291 = (bf16[1024,1024]{1,0:T(8,128)(2,1)}, bf16[1024,1024]{1,0:T(8,128)(2,1)}) custom-call(bf16[1024,2048]{1,0:T(8,128)(2,1)} %get-tuple-element.140.refs_5_.refs_0_.refs_2_, bf16[1024,2048]{1,0:T(8,128)(2,1)} %refs_1_.11, f32[1024,1024]{1,0:T(8,128)} %get-tuple-element.141.refs_2_, f32[1024,1024]{1,0:T(8,128)} %get-tuple-element.107.refs_3_, ...), custom_call_target="tpu_custom_call" | custom-call | flops 1 | bytes 1 | tf_op jit(solution)/shard_map/pallas_call | solution.py:108
  301.7 12.2 %shard_map.292 = (bf16[1024,512]{1,0:T(8,128)(2,1)}, bf16[1024,512]{1,0:T(8,128)(2,1)}, bf16[1024,1024]{1,0:T(8,128)(2,1)}, bf16[1024,1024]{1,0:T(8,128)(2,1)}) custom-call(bf16[1024,512]{1,0:T(8,128)(2,1)} %get-tuple-element.104.refs_0_, bf16[1024,512]{1,0:T(8,128)(2,1)} %get-tuple-element.105.refs_1_, bf16[1024,1024]{1,0:T(8,128)(2,1)} %get-tuple-element.106.refs_2_, ...), custom_call_target="tpu_custom_call" | custom-call | flops 1 | bytes 1 | tf_op jit(solution)/shard_map/pallas_call | solution.py:108
  322.7 13.8 %shard_map.295.refs_2_.refs_0_ = f32[256,2048]{1,0:T(8,128)} custom-call(bf16[1024,512]{1,0:T(8,128)(2,1)} %get-tuple-element.150.refs_2_.refs_0_, bf16[1024,512]{1,0:T(8,128)(2,1)} %get-tuple-element.152.refs_1_, bf16[1024,1024]{1,0:T(8,128)(2,1)} %get-tuple-element.153.refs_2_.refs_1_, bf16[1024,1024]{1,0:T(8,128)(2,1)} %get-tuple-element.142.refs_1_.refs_3_.refs_2_, ...), custom_call_target="tpu_custom_call" | custom-call | flops 1 | bytes 1 | tf_op jit(solution)/shard_map/pallas_call | solution.py:108
  338.1 11.6 %collective-permute-done.15.refs_4_ = f32[256,1024]{1,0:T(8,128)} collective-permute-done((f32[256,1024]{1,0:T(8,128)}, f32[256,1024]{1,0:T(8,128)}, u32[]{:S(2)}, u32[]{:S(2)}) %collective-permute-start.15) | collective-permute-done | bytes 1048608 | tf_op jit(solution)/shard_map/ppermute | solution.py:954
  354.3 13.8 %shard_map.297.refs_4_.refs_0_ = f32[256,2048]{1,0:T(8,128)} custom-call(bf16[1024,512]{1,0:T(8,128)(2,1)} %get-tuple-element.150.refs_2_.refs_0_, bf16[1024,512]{1,0:T(8,128)(2,1)} %get-tuple-element.152.refs_1_, bf16[1024,1024]{1,0:T(8,128)(2,1)} %get-tuple-element.153.refs_2_.refs_1_, bf16[1024,1024]{1,0:T(8,128)(2,1)} %get-tuple-element.142.refs_1_.refs_3_.refs_2_, ...), custom_call_target="tpu_custom_call" | custom-call | flops 1 | bytes 1 | tf_op jit(solution)/shard_map/pallas_call | solution.py:108
  395.9 11.2 %collective-permute-done.20.refs_3_.refs_4_ = f32[256,1024]{1,0:T(8,128)} collective-permute-done((f32[256,1024]{1,0:T(8,128)}, f32[256,1024]{1,0:T(8,128)}, u32[]{:S(2)}, u32[]{:S(2)}) %collective-permute-start.20) | collective-permute-done | bytes 1048608 | tf_op jit(solution)/shard_map/ppermute | solution.py:954
  412.1 9.0 %shard_map.304.refs_5_.refs_0_ = f32[256,2048]{1,0:T(8,128)} custom-call(bf16[1024,1024]{1,0:T(8,128)(2,1)} %get-tuple-element.134.refs_3_.refs_1_.refs_0_, bf16[1024,2048]{1,0:T(8,128)(2,1)} %refs_1_.13, f32[2,256,1024]{2,1,0:T(8,128)} %shard_map.303.refs_2_, f32[256,1024]{1,0:T(8,128)} %collective-permute-done.20.refs_3_.refs_4_), custom_call_target="tpu_custom_call" | custom-call | flops 1 | bytes 1 | tf_op jit(solution)/shard_map/pallas_call | solution.py:108
  421.1 10.7 %shard_map.305 = (f32[1024,2048]{1,0:T(8,128)}, f32[1,2048]{1,0:T(1,128)}, f32[1,2048]{1,0:T(1,128)}) custom-call(f32[256,2048]{1,0:T(8,128)} %shard_map.295.refs_2_.refs_0_, f32[256,2048]{1,0:T(8,128)} %collective-permute-done.19.refs_1_, bf16[1024,2048]{1,0:T(8,128)(2,1)} %refs_2_.35, f32[1,2048]{1,0:T(1,128)} %bitcast.19, ...), custom_call_target="tpu_custom_call" | custom-call | flops 1 | bytes 1 | tf_op jit(solution)/shard_map/pallas_call | solution.py:108
  442.4 10.7 %shard_map.308 = (f32[1024,2048]{1,0:T(8,128)}, f32[1,2048]{1,0:T(1,128)}, f32[1,2048]{1,0:T(1,128)}) custom-call(f32[256,2048]{1,0:T(8,128)} %shard_map.297.refs_4_.refs_0_, f32[256,2048]{1,0:T(8,128)} %collective-permute-done.18.refs_1_, bf16[1024,2048]{1,0:T(8,128)(2,1)} %refs_2_.35, f32[1,2048]{1,0:T(1,128)} %bitcast.20, ...), custom_call_target="tpu_custom_call", output_to_operand_aliasing={{0}: (5, {})} | custom-call | flops 1 | bytes 1 | tf_op jit(solution)/shard_map/pallas_call | solution.py:108
  486.4 10.6 %collective-permute-done.23.refs_5_ = f32[512,512]{1,0:T(8,128)} collective-permute-done((f32[512,512]{1,0:T(8,128)}, f32[512,512]{1,0:T(8,128)}, u32[]{:S(2)}, u32[]{:S(2)}) %collective-permute-start.23) | collective-permute-done | bytes 1048608 | tf_op jit(solution)/shard_map/ppermute | solution.py:954
  503.0 16.4 %collective-permute-done.32.refs_5_ = f32[512,512]{1,0:T(8,128)} collective-permute-done((f32[512,512]{1,0:T(8,128)}, f32[512,512]{1,0:T(8,128)}, u32[]{:S(2)}, u32[]{:S(2)}) %collective-permute-start.32) | collective-permute-done | bytes 1048608 | tf_op jit(solution)/shard_map/ppermute | solution.py:954
  519.5 9.0 %shard_map.314.refs_6_.refs_0_ = f32[256,2048]{1,0:T(8,128)} custom-call(bf16[1024,1024]{1,0:T(8,128)(2,1)} %get-tuple-element.134.refs_3_.refs_1_.refs_0_, bf16[1024,2048]{1,0:T(8,128)(2,1)} %refs_1_.13, f32[512,512]{1,0:T(8,128)} %shard_map.313.refs_2_), custom_call_target="tpu_custom_call" | custom-call | flops 1 | bytes 1 | tf_op jit(solution)/shard_map/pallas_call | solution.py:108
  548.0 16.4 %collective-permute-done.33.refs_6_.refs_5_ = f32[512,512]{1,0:T(8,128)} collective-permute-done((f32[512,512]{1,0:T(8,128)}, f32[512,512]{1,0:T(8,128)}, u32[]{:S(2)}, u32[]{:S(2)}) %collective-permute-start.33) | collective-permute-done | bytes 1048608 | tf_op jit(solution)/shard_map/ppermute | solution.py:954
  686.3 9.7 %collective-permute-done.44.refs_2_ = f32[256,512]{1,0:T(8,128)S(1)} collective-permute-done((f32[256,512]{1,0:T(8,128)}, f32[256,512]{1,0:T(8,128)S(1)}, u32[]{:S(2)}, u32[]{:S(2)}) %collective-permute-start.44) | collective-permute-done | bytes 524320 | tf_op jit(solution)/shard_map/ppermute | solution.py:950
  705.9 15.5 %collective-permute-done.45.refs_4_ = f32[256,1024]{1,0:T(8,128)} collective-permute-done((f32[256,1024]{1,0:T(8,128)}, f32[256,1024]{1,0:T(8,128)}, u32[]{:S(2)}, u32[]{:S(2)}) %collective-permute-start.45) | collective-permute-done | bytes 1048608 | tf_op jit(solution)/shard_map/ppermute | solution.py:954
  (175 shorter events, 352.5 us)
Async XLA Ops:
  71.9 44.1 %collective-permute-start.2 = (f32[128,2048]{1,0:T(8,128)}, f32[128,2048]{1,0:T(8,128)}, u32[]{:S(2)}, u32[]{:S(2)}) collective-permute-start(f32[128,2048]{1,0:T(8,128)} %get-tuple-element.117.refs_9_.refs_0_), channel_id=1, source_target_pairs={{0,2},{1,3},{2,0},{3,1},{4,6},{5,7},{6,4},{7,5},{8,10},{9,11},{10,... | collective-permute-start | bytes 3145736 | tf_op jit(solution)/shard_map/ppermute | solution.py:958
  84.0 48.0 %collective-permute-start.1 = (f32[128,2048]{1,0:T(8,128)}, f32[128,2048]{1,0:T(8,128)}, u32[]{:S(2)}, u32[]{:S(2)}) collective-permute-start(f32[128,2048]{1,0:T(8,128)} %get-tuple-element.118.refs_5_.refs_0_), channel_id=1, source_target_pairs={{0,2},{1,3},{2,0},{3,1},{4,6},{5,7},{6,4},{7,5},{8,10},{9,11},{10,... | collective-permute-start | bytes 3145736 | tf_op jit(solution)/shard_map/ppermute | solution.py:958
  113.4 116.8 %collective-permute-start.9 = (f32[512,2048]{1,0:T(8,128)}, f32[512,2048]{1,0:T(8,128)}, u32[]{:S(2)}, u32[]{:S(2)}) collective-permute-start(f32[512,2048]{1,0:T(8,128)} %shard_map.273.refs_7_), channel_id=1, source_target_pairs={{0,4},{4,0},{8,12},{12,8},{16,20},{20,16},{24,28},{28,24},{1,5},{5... | collective-permute-start | bytes 12582920 | tf_op jit(solution)/shard_map/ppermute | solution.py:950
  152.3 49.8 %collective-permute-start.6 = (f32[512,1024]{1,0:T(8,128)}, f32[512,1024]{1,0:T(8,128)}, u32[]{:S(2)}, u32[]{:S(2)}) collective-permute-start(f32[512,1024]{1,0:T(8,128)} %shard_map.278.refs_4_), channel_id=1, source_target_pairs={{0,8},{4,12},{8,16},{12,20},{16,24},{20,28},{24,0},{28,4},{1,9},{5... | collective-permute-start | bytes 6291464 | tf_op jit(solution)/shard_map/ppermute | solution.py:954
  164.9 48.8 %collective-permute-start.5 = (f32[256,2048]{1,0:T(8,128)}, f32[256,2048]{1,0:T(8,128)}, u32[]{:S(2)}, u32[]{:S(2)}) collective-permute-start(f32[256,2048]{1,0:T(8,128)} %shard_map.279.refs_3_.refs_0_), channel_id=1, source_target_pairs={{0,2},{1,3},{2,0},{3,1},{4,6},{5,7},{6,4},{7,5},{8,10},{9,11},{10,... | collective-permute-start | bytes 6291464 | tf_op jit(solution)/shard_map/ppermute | solution.py:958
  171.6 80.4 %collective-permute-start.8 = (f32[2,1024,256]{2,1,0:T(8,128)}, f32[2,1024,256]{2,1,0:T(8,128)}, u32[]{:S(2)}, u32[]{:S(2)}) collective-permute-start(f32[2,1024,256]{2,1,0:T(8,128)} %shard_map.280.refs_4_), channel_id=1, source_target_pairs={{0,4},{4,0},{8,12},{12,8},{16,20},{20,16},{24,28},{28,24},{1,5},{5... | collective-permute-start | bytes 6291464 | tf_op jit(solution)/shard_map/ppermute | solution.py:950
  207.1 51.0 %collective-permute-start.7 = (f32[512,1024]{1,0:T(8,128)}, f32[512,1024]{1,0:T(8,128)}, u32[]{:S(2)}, u32[]{:S(2)}) collective-permute-start(f32[512,1024]{1,0:T(8,128)} %shard_map.282.refs_3_), channel_id=1, source_target_pairs={{0,8},{4,12},{8,16},{12,20},{16,24},{20,28},{24,0},{28,4},{1,9},{5... | collective-permute-start | bytes 6291464 | tf_op jit(solution)/shard_map/ppermute | solution.py:954
  207.1 59.1 %collective-permute-start.4 = (f32[256,2048]{1,0:T(8,128)}, f32[256,2048]{1,0:T(8,128)}, u32[]{:S(2)}, u32[]{:S(2)}) collective-permute-start(f32[256,2048]{1,0:T(8,128)} %shard_map.281.refs_4_.refs_0_), channel_id=1, source_target_pairs={{0,2},{1,3},{2,0},{3,1},{4,6},{5,7},{6,4},{7,5},{8,10},{9,11},{10,... | collective-permute-start | bytes 6291464 | tf_op jit(solution)/shard_map/ppermute | solution.py:958
  213.8 103.3 %collective-permute-start.14 = (f32[2,256,1024]{2,1,0:T(8,128)}, f32[2,256,1024]{2,1,0:T(8,128)}, u32[]{:S(2)}, u32[]{:S(2)}) collective-permute-start(f32[2,256,1024]{2,1,0:T(8,128)} %shard_map.283.refs_5_), channel_id=1, source_target_pairs={{0,4},{4,0},{8,12},{12,8},{16,20},{20,16},{24,28},{28,24},{1,5},{5... | collective-permute-start | bytes 6291464 | tf_op jit(solution)/shard_map/ppermute | solution.py:950
  263.1 89.7 %collective-permute-start.16 = (f32[512,1024]{1,0:T(8,128)}, f32[512,1024]{1,0:T(8,128)}, u32[]{:S(2)}, u32[]{:S(2)}) collective-permute-start(f32[512,1024]{1,0:T(8,128)} %shard_map.288.refs_7_), channel_id=1, source_target_pairs={{0,8},{4,12},{8,16},{12,20},{16,24},{20,28},{24,0},{28,4},{1,9},{5... | collective-permute-start | bytes 6291464 | tf_op jit(solution)/shard_map/ppermute | solution.py:954
  264.7 112.7 %collective-permute-start.12 = (f32[2,1024,256]{2,1,0:T(8,128)}, f32[2,1024,256]{2,1,0:T(8,128)}, u32[]{:S(2)}, u32[]{:S(2)}) collective-permute-start(f32[2,1024,256]{2,1,0:T(8,128)} %shard_map.285.refs_3_), channel_id=1, source_target_pairs={{0,4},{4,0},{8,12},{12,8},{16,20},{20,16},{24,28},{28,24},{1,5},{5... | collective-permute-start | bytes 6291464 | tf_op jit(solution)/shard_map/ppermute | solution.py:950
  321.0 66.7 %collective-permute-start.11 = (f32[1024,512]{1,0:T(8,128)}, f32[1024,512]{1,0:T(8,128)}, u32[]{:S(2)}, u32[]{:S(2)}) collective-permute-start(f32[1024,512]{1,0:T(8,128)} %shard_map.293.refs_4_), channel_id=1, source_target_pairs={{0,4},{4,0},{8,12},{12,8},{16,20},{20,16},{24,28},{28,24},{1,5},{5... | collective-permute-start | bytes 6291464 | tf_op jit(solution)/shard_map/ppermute | solution.py:950
  336.5 58.2 %collective-permute-start.19 = (f32[256,2048]{1,0:T(8,128)}, f32[256,2048]{1,0:T(8,128)}, u32[]{:S(2)}, u32[]{:S(2)}) collective-permute-start(f32[256,2048]{1,0:T(8,128)} %shard_map.295.refs_2_.refs_0_), channel_id=1, source_target_pairs={{0,2},{1,3},{2,0},{3,1},{4,6},{5,7},{6,4},{7,5},{8,10},{9,11},{10,... | collective-permute-start | bytes 6291464 | tf_op jit(solution)/shard_map/ppermute | solution.py:958
  352.8 83.4 %collective-permute-start.21 = (f32[1024,512]{1,0:T(8,128)}, f32[1024,512]{1,0:T(8,128)}, u32[]{:S(2)}, u32[]{:S(2)}) collective-permute-start(f32[1024,512]{1,0:T(8,128)} %shard_map.296.refs_8_), channel_id=1, source_target_pairs={{0,4},{4,0},{8,12},{12,8},{16,20},{20,16},{24,28},{28,24},{1,5},{5... | collective-permute-start | bytes 6291464 | tf_op jit(solution)/shard_map/ppermute | solution.py:950
  377.4 64.9 %collective-permute-start.18 = (f32[256,2048]{1,0:T(8,128)}, f32[256,2048]{1,0:T(8,128)}, u32[]{:S(2)}, u32[]{:S(2)}) collective-permute-start(f32[256,2048]{1,0:T(8,128)} %shard_map.297.refs_4_.refs_0_), channel_id=1, source_target_pairs={{0,2},{1,3},{2,0},{3,1},{4,6},{5,7},{6,4},{7,5},{8,10},{9,11},{10,... | collective-permute-start | bytes 6291464 | tf_op jit(solution)/shard_map/ppermute | solution.py:958
  387.7 44.2 %collective-permute-start.22 = (f32[1024,256]{1,0:T(8,128)}, f32[1024,256]{1,0:T(8,128)}, u32[]{:S(2)}, u32[]{:S(2)}) collective-permute-start(f32[1024,256]{1,0:T(8,128)} %shard_map.301.refs_5_), channel_id=1, source_target_pairs={{0,8},{4,12},{8,16},{12,20},{16,24},{20,28},{24,0},{28,4},{1,9},{5... | collective-permute-start | bytes 3145736 | tf_op jit(solution)/shard_map/ppermute | solution.py:954
  394.7 85.4 %collective-permute-start.24 = (f32[1024,512]{1,0:T(8,128)}, f32[1024,512]{1,0:T(8,128)}, u32[]{:S(2)}, u32[]{:S(2)}) collective-permute-start(f32[1024,512]{1,0:T(8,128)} %shard_map.300.refs_5_), channel_id=1, source_target_pairs={{0,4},{4,0},{8,12},{12,8},{16,20},{20,16},{24,28},{28,24},{1,5},{5... | collective-permute-start | bytes 6291464 | tf_op jit(solution)/shard_map/ppermute | solution.py:950
  407.1 46.0 %collective-permute-start.17 = (f32[512,512]{1,0:T(8,128)}, f32[512,512]{1,0:T(8,128)}, u32[]{:S(2)}, u32[]{:S(2)}) collective-permute-start(f32[512,512]{1,0:T(8,128)} %shard_map.302.refs_3_), channel_id=1, source_target_pairs={{0,8},{4,12},{8,16},{12,20},{16,24},{20,28},{24,0},{28,4},{1,9},{5... | collective-permute-start | bytes 3145736 | tf_op jit(solution)/shard_map/ppermute | solution.py:954
  458.8 38.1 %collective-permute-start.23 = (f32[512,512]{1,0:T(8,128)}, f32[512,512]{1,0:T(8,128)}, u32[]{:S(2)}, u32[]{:S(2)}) collective-permute-start(f32[512,512]{1,0:T(8,128)} %shard_map.309.refs_5_), channel_id=1, source_target_pairs={{0,8},{4,12},{8,16},{12,20},{16,24},{20,28},{24,0},{28,4},{1,9},{5... | collective-permute-start | bytes 3145736 | tf_op jit(solution)/shard_map/ppermute | solution.py:954
  460.9 87.1 %collective-permute-start.30 = (f32[2,256,1024]{2,1,0:T(8,128)}, f32[2,256,1024]{2,1,0:T(8,128)}, u32[]{:S(2)}, u32[]{:S(2)}) collective-permute-start(f32[2,256,1024]{2,1,0:T(8,128)} %shard_map.303.refs_2_), channel_id=1, source_target_pairs={{0,4},{4,0},{8,12},{12,8},{16,20},{20,16},{24,28},{28,24},{1,5},{5... | collective-permute-start | bytes 6291464 | tf_op jit(solution)/shard_map/ppermute | solution.py:950
  468.8 99.9 %collective-permute-start.29 = (f32[2,1032,256]{2,1,0:T(8,128)}, f32[2,1032,256]{2,1,0:T(8,128)}, u32[]{:S(2)}, u32[]{:S(2)}) collective-permute-start(f32[2,1032,256]{2,1,0:T(8,128)} %shard_map.310.refs_6_), channel_id=1, source_target_pairs={{0,4},{4,0},{8,12},{12,8},{16,20},{20,16},{24,28},{28,24},{1,5},{5... | collective-permute-start | bytes 6340616 | tf_op jit(solution)/shard_map/ppermute | solution.py:950
  480.1 39.3 %collective-permute-start.32 = (f32[512,512]{1,0:T(8,128)}, f32[512,512]{1,0:T(8,128)}, u32[]{:S(2)}, u32[]{:S(2)}) collective-permute-start(f32[512,512]{1,0:T(8,128)} %shard_map.311.refs_5_), channel_id=1, source_target_pairs={{0,8},{4,12},{8,16},{12,20},{16,24},{20,28},{24,0},{28,4},{1,9},{5... | collective-permute-start | bytes 3145736 | tf_op jit(solution)/shard_map/ppermute | solution.py:954
  485.4 56.6 %collective-permute-start.31 = (f32[512,512]{1,0:T(8,128)}, f32[512,512]{1,0:T(8,128)}, u32[]{:S(2)}, u32[]{:S(2)}) collective-permute-start(f32[512,512]{1,0:T(8,128)} %shard_map.312.refs_6_), channel_id=1, source_target_pairs={{0,8},{4,12},{8,16},{12,20},{16,24},{20,28},{24,0},{28,4},{1,9},{5... | collective-permute-start | bytes 3145736 | tf_op jit(solution)/shard_map/ppermute | solution.py:954
  497.0 77.2 %collective-permute-start.28 = (f32[256,2048]{1,0:T(8,128)}, f32[256,2048]{1,0:T(8,128)}, u32[]{:S(2)}, u32[]{:S(2)}) collective-permute-start(f32[256,2048]{1,0:T(8,128)} %shard_map.304.refs_5_.refs_0_), channel_id=1, source_target_pairs={{0,2},{1,3},{2,0},{3,1},{4,6},{5,7},{6,4},{7,5},{8,10},{9,11},{10,... | collective-permute-start | bytes 6291464 | tf_op jit(solution)/shard_map/ppermute | solution.py:958
  519.4 44.9 %collective-permute-start.33 = (f32[512,512]{1,0:T(8,128)}, f32[512,512]{1,0:T(8,128)}, u32[]{:S(2)}, u32[]{:S(2)}) collective-permute-start(f32[512,512]{1,0:T(8,128)} %shard_map.313.refs_2_), channel_id=1, source_target_pairs={{0,8},{4,12},{8,16},{12,20},{16,24},{20,28},{24,0},{28,4},{1,9},{5... | collective-permute-start | bytes 3145736 | tf_op jit(solution)/shard_map/ppermute | solution.py:954
  541.9 72.9 %collective-permute-start.27 = (f32[256,2048]{1,0:T(8,128)}, f32[256,2048]{1,0:T(8,128)}, u32[]{:S(2)}, u32[]{:S(2)}) collective-permute-start(f32[256,2048]{1,0:T(8,128)} %shard_map.314.refs_6_.refs_0_), channel_id=1, source_target_pairs={{0,2},{1,3},{2,0},{3,1},{4,6},{5,7},{6,4},{7,5},{8,10},{9,11},{10,... | collective-permute-start | bytes 6291464 | tf_op jit(solution)/shard_map/ppermute | solution.py:958
  548.0 38.9 %collective-permute-start.35 = (f32[512,512]{1,0:T(8,128)}, f32[512,512]{1,0:T(8,128)}, u32[]{:S(2)}, u32[]{:S(2)}) collective-permute-start(f32[512,512]{1,0:T(8,128)} %shard_map.317.refs_5_), channel_id=1, source_target_pairs={{0,8},{4,12},{8,16},{12,20},{16,24},{20,28},{24,0},{28,4},{1,9},{5... | collective-permute-start | bytes 3145736 | tf_op jit(solution)/shard_map/ppermute | solution.py:954
  573.1 84.0 %collective-permute-start.36 = (f32[2,1032,256]{2,1,0:T(8,128)}, f32[2,1032,256]{2,1,0:T(8,128)}, u32[]{:S(2)}, u32[]{:S(2)}) collective-permute-start(f32[2,1032,256]{2,1,0:T(8,128)} %shard_map.316.refs_6_), channel_id=1, source_target_pairs={{0,4},{4,0},{8,12},{12,8},{16,20},{20,16},{24,28},{28,24},{1,5},{5... | collective-permute-start | bytes 6340616 | tf_op jit(solution)/shard_map/ppermute | solution.py:950
  592.4 39.6 %collective-permute-start.38 = (f32[512,512]{1,0:T(8,128)}, f32[512,512]{1,0:T(8,128)}, u32[]{:S(2)}, u32[]{:S(2)}) collective-permute-start(f32[512,512]{1,0:T(8,128)} %shard_map.321.refs_6_), channel_id=1, source_target_pairs={{0,8},{4,12},{8,16},{12,20},{16,24},{20,28},{24,0},{28,4},{1,9},{5... | collective-permute-start | bytes 3145736 | tf_op jit(solution)/shard_map/ppermute | solution.py:954
  614.3 42.9 %collective-permute-start.37 = (f32[1032,256]{1,0:T(8,128)}, f32[1032,256]{1,0:T(8,128)}, u32[]{:S(2)}, u32[]{:S(2)}) collective-permute-start(f32[1032,256]{1,0:T(8,128)} %shard_map.324.refs_4_), channel_id=1, source_target_pairs={{0,8},{4,12},{8,16},{12,20},{16,24},{20,28},{24,0},{28,4},{1,9},{5... | collective-permute-start | bytes 3170312 | tf_op jit(solution)/shard_map/ppermute | solution.py:954
  638.1 41.1 %collective-permute-start.42 = (f32[512,512]{1,0:T(8,128)}, f32[512,512]{1,0:T(8,128)}, u32[]{:S(2)}, u32[]{:S(2)}) collective-permute-start(f32[512,512]{1,0:T(8,128)} %shard_map.315.refs_5_), channel_id=1, source_target_pairs={{0,8},{4,12},{8,16},{12,20},{16,24},{20,28},{24,0},{28,4},{1,9},{5... | collective-permute-start | bytes 3145736 | tf_op jit(solution)/shard_map/ppermute | solution.py:954
  665.2 56.2 %collective-permute-start.45 = (f32[256,1024]{1,0:T(8,128)}, f32[256,1024]{1,0:T(8,128)}, u32[]{:S(2)}, u32[]{:S(2)}) collective-permute-start(f32[256,1024]{1,0:T(8,128)} %shard_map.318.refs_6_), channel_id=1, source_target_pairs={{0,8},{4,12},{8,16},{12,20},{16,24},{20,28},{24,0},{28,4},{1,9},{5... | collective-permute-start | bytes 3145736 | tf_op jit(solution)/shard_map/ppermute | solution.py:954
  (28 other events, 439.9 us)

commit v3 on v2

--- a/solution.py
+++ b/solution.py
@@ -175,6 +175,17 @@
 
 
 SMEM = pl.BlockSpec(memory_space=pltpu.SMEM)
+ANY = pl.BlockSpec(memory_space=pl.ANY)
+
+
+def fetch_scratch(*arrays):
+    return [pltpu.VMEM(a.shape, a.dtype) for a in arrays] + [pltpu.SemaphoreType.DMA((len(arrays),))]
+
+
+def fetched(sources, held):
+    places, done = held[:-1], held[-1]
+    copies = [pltpu.make_async_copy(s, p, done.at[n]) for n, (s, p) in enumerate(zip(sources, places))]
+    return places, copies
 
 
 def proj_kernel(
@@ -224,7 +235,11 @@
 TILES = 4
 
 
-def retain_kernel(chunk, q, k, v, switch, seg_row, logs, w, chip, u_out, o_out, p_out, full, sent, got, s1, s2):
+def retain_kernel(
+    chunk, q, k, v, switch, seg_row, logs, w, chip, u_out, o_out, p_out, full, sent, got, s1, s2, *held
+):
+    (w,), (fetch,) = fetched((w,), held)
+    fetch.start()
     meet_other_core()
     seg_rows = down_rows(seg_row[:, chunk * BLOCK : (chunk + 1) * BLOCK])
     heads = q.shape[1] // KEY
@@ -246,6 +261,7 @@
         u_out[:, vpart] = (centred * scale * (gate * jax.nn.sigmoid(gate))).astype(BF16)
     tile = w.shape[1] // TILES
     copies = []
+    fetch.wait()
     for j in range(TILES):
         columns = slice(j * tile, (j + 1) * tile)
         full[:, columns] = product_nn(u_out[...], w[:, columns])
@@ -285,7 +301,7 @@
             row_spec(BLOCK, vw, chunk),
             const_spec(seg_row.shape),
             SMEM,
-            const_spec(w.shape),
+            ANY,
         ],
         scratch=[
             pltpu.VMEM((BLOCK, width), F32),
@@ -293,16 +309,39 @@
             pltpu.VMEM((TILES, HALF, width // TILES), F32),
             pltpu.SemaphoreType.DMA((TILES,)),
             pltpu.SemaphoreType.DMA((TILES,)),
+            *fetch_scratch(w),
         ],
         onto=() if before is None else ((1, before[0]), (2, before[1])),
         paired=True,
     )
 
 
-def feed_kernel(a, c, wg, wu, wd, hid_out, dg_out, du_out):
-    gate = product_nn(a[...], wg[...])
-    up = product_nn(a[...], wu[...])
+def feed_kernel(
+    chip, crossed, x, gain, bias, c, wg, wu, wd, hid_out, dg_out, du_out, a_out, h_out, sent, got, s1, s2
+):
+    copy = to_other_core(sent, got, s1, s2)
+    begin = pl.program_id(0) == 0
+
+    @pl.when(begin)
+    def _():
+        meet_other_core()
+        middle = x[core_rows(True, 0), :].astype(F32) + (chip[...] + crossed[...])
+        h_out[...] = middle
+        centred, scale = normal_rows(middle, 1e-05)
+        normed = (centred * scale * gain[...] + bias[...]).astype(BF16)
+        sent[...] = normed.astype(F32)
+        copy.start()
+        a_out[core_rows(True, 0), :] = normed
+
     back = product_nt(c[...], wd[...])
+
+    @pl.when(begin)
+    def _():
+        copy.wait()
+        a_out[core_rows(False, 0), :] = got[...].astype(BF16)
+
+    gate = product_nn(a_out[...], wg[...])
+    up = product_nn(a_out[...], wu[...])
     factor = 0.7978845608028654
     bent = jnp.tanh(factor * (gate + 0.044715 * (gate * gate * gate)))
     half = 0.5 * (1.0 + bent)
@@ -313,24 +352,36 @@
     du_out[...] = (back * active).astype(BF16)
 
 
-def feed_forward(line, chunk, rows, a, c, wg, wu, wd, before):
-    width, ff = wg.shape
+def feed_forward(line, chunk, chip, crossed, x, gain, bias, c, wg, wu, wd, before):
+    total, width = x.shape
+    ff = wg.shape[1]
     tile = min(256, ff)
-    whole = a.shape[0]
     return line.call(
         feed_kernel,
-        [shape((whole, ff), BF16)] * 3,
-        [pl.BlockSpec((rows, tile), lambda i: (chunk, i))] * 3,
-        [a, c, wg, wu, wd],
+        [shape((total, ff), BF16)] * 3 + [shape((total, width), BF16), shape((total // 2, width), F32)],
+        [pl.BlockSpec((BLOCK, tile), lambda i: (chunk, i))] * 3
+        + [row_spec(BLOCK, width, chunk), row_spec(HALF, width, chunk)],
+        [chip, crossed, x, gain, bias, c, wg, wu, wd],
         [
-            row_spec(rows, width, chunk),
-            row_spec(rows, width, chunk),
+            const_spec((HALF, width)),
+            const_spec((HALF, width)),
+            row_spec(BLOCK, width, chunk),
+            const_spec((1, width)),
+            const_spec((1, width)),
+            row_spec(BLOCK, width, chunk),
             pl.BlockSpec((width, tile), lambda i: (0, i)),
             pl.BlockSpec((width, tile), lambda i: (0, i)),
             pl.BlockSpec((tile, width), lambda i: (i, 0)),
         ],
         grid=(ff // tile,),
+        scratch=[
+            pltpu.VMEM((HALF, width), F32),
+            pltpu.VMEM((HALF, width), F32),
+            pltpu.SemaphoreType.DMA,
+            pltpu.SemaphoreType.DMA,
+        ],
         onto=() if before is None else tuple(enumerate(before)),
+        paired=True,
     )
 
 
@@ -459,32 +510,6 @@
     )[0]
 
 
-def norm_work(n, part, rows, chip, crossed, x, gain, bias, h_out):
-    middle = x[rows, :].astype(F32) + (chip[part, :] + crossed[part, :])
-    h_out[part, :] = middle
-    centred, scale = normal_rows(middle, 1e-05)
-    return (centred * scale * gain[...] + bias[...]).astype(BF16).astype(F32)
-
-
-def second_norm(line, chunk, rows, chip, crossed, x, gain, bias, before):
-    total, width = x.shape
-    half = rows // 2
-    return shared_rows(
-        line,
-        norm_work,
-        chunk,
-        rows,
-        [chip, crossed, x, gain, bias],
-        [const_spec((half, width)), const_spec((half, width)), row_spec(rows, width, chunk)]
-        + [const_spec((1, width))] * 2,
-        BF16,
-        total,
-        width,
-        [((total // 2, width), row_spec(half, width, chunk))],
-        () if before is None else tuple(enumerate(before)),
-    )
-
-
 def norm_back(n, back, centred, scale, gain, gain_out, bias_out):
     normed = centred * scale
     one, two = jnp.sum(back * normed, axis=0, keepdims=True), jnp.sum(back, axis=0, keepdims=True)
@@ -687,11 +712,11 @@
     return outer_place(where, position, groups) * 2 + (where[0] if own else 1 - where[0])
 
 
-def plain_block(where, left, right, by_rows, groups, position, own, extra):
+def plain_block(where, left, right, by_rows, groups, position, own, extra, skip):
     width = (left if by_rows else right).shape[1] // (2 * groups)
     column = column_block(where, position, groups, own) * width
     if by_rows:
-        return product_tn(lax.dynamic_slice_in_dim(left, column, width, 1), right)
+        return product_tn(lax.dynamic_slice_in_dim(left, column, width, 1), right[:, skip:])
     block = product_tn(left, lax.dynamic_slice_in_dim(right, column, width, 1))
     if extra:
         more = lax.dynamic_slice_in_dim(extra[0] + extra[1], column, width, 1)
@@ -707,16 +732,18 @@
         out[0, rows:] = extra[0][...] + extra[1][...]
 
 
-def sent_blocks(line, where, left, right, by_rows, groups, first, count, extra=()):
+def sent_blocks(line, where, left, right, by_rows, groups, first, count, extra=(), skip=0):
     width = (left if by_rows else right).shape[1] // (2 * groups)
     if width % 128:
-        blocks = [plain_block(where, left, right, by_rows, groups, first + j, False, extra) for j in range(count)]
+        blocks = [plain_block(where, left, right, by_rows, groups, first + j, False, extra, skip) for j in range(count)]
         return jnp.stack(blocks)
     rows = left.shape[0]
     moving = pl.BlockSpec((rows, width), lambda j, w: (0, column_block(w, first + j, groups, False)))
     more = extra[0].shape[0] if extra else 0
-    block = (width, right.shape[1]) if by_rows else (left.shape[1] + more, width)
-    specs = [moving if by_rows else const_spec(left.shape), const_spec(right.shape) if by_rows else moving]
+    columns = right.shape[1] - skip
+    block = (width, columns) if by_rows else (left.shape[1] + more, width)
+    fixed = pl.BlockSpec((rows, columns), lambda j, w: (0, skip // columns))
+    specs = [moving if by_rows else const_spec(left.shape), fixed if by_rows else moving]
     small = pl.BlockSpec((more, width), lambda j, w: (0, column_block(w, first + j, groups, False)))
     return line.call(
         sent_kernel,
@@ -751,21 +778,22 @@
 
 
 def kept_block(
-    line, where, left, right, by_rows, groups, position, received, index, travelling, extra=(), last=False
+    line, where, left, right, by_rows, groups, position, received, index, travelling, extra=(), last=False, skip=0
 ):
     width = (left if by_rows else right).shape[1] // (2 * groups)
     if width % 128:
-        block = plain_block(where, left, right, by_rows, groups, position, True, extra) + received[index]
+        block = plain_block(where, left, right, by_rows, groups, position, True, extra, skip) + received[index]
         block = block if travelling is None else block + travelling
         return (block[: left.shape[1]], block[left.shape[1] :]) if extra and last else block
     if extra:
         return extended_block(line, where, left, right, groups, position, received, index, travelling, extra, last)
-    rows, tiles = left.shape[0], 2
+    rows, columns = left.shape[0], right.shape[1] - skip
+    tiles = 1 if skip else 2
     moving = pl.BlockSpec((rows, width), lambda j, w: (0, column_block(w, position, groups, True)))
     if by_rows:
-        part = right.shape[1] // tiles
-        left_spec, right_spec = moving, pl.BlockSpec((rows, part), lambda j, w: (0, j))
-        block, piece, at = (width, right.shape[1]), (width, part), lambda j: (0, j)
+        part = columns // tiles
+        left_spec, right_spec = moving, pl.BlockSpec((rows, part), lambda j, w: (0, skip // part + j))
+        block, piece, at = (width, columns), (width, part), lambda j: (0, j)
     else:
         part = left.shape[1] // tiles
         left_spec, right_spec = pl.BlockSpec((rows, part), lambda j, w: (0, j)), moving
@@ -823,7 +851,7 @@
     send[...] = full[pl.ds(pl.multiple_of((1 - where[0]) * half, half), half), :]
 
 
-def wide_block(line, where, pairs, groups, position, travelling, last, columns):
+def wide_block(line, where, pairs, groups, position, travelling, last, columns, shared):
     rows, depth = pairs[0][0].shape
     width = depth // groups
     tiles = 2
@@ -832,7 +860,7 @@
     for left, right in pairs:
         ins += [left, right]
         specs.append(pl.BlockSpec((rows, width), lambda j, w: (0, outer_place(w, position, groups))))
-        if right.shape[1] > columns:
+        if shared and right.shape[1] > columns:
             specs.append(pl.BlockSpec((rows, part), lambda j, w: (0, w[0] * tiles + j)))
         else:
             specs.append(pl.BlockSpec((rows, part), lambda j, w: (0, j)))
@@ -892,6 +920,19 @@
         [const_spec(keep.shape)] * 2,
         scalars=where,
     )
+
+
+def side_kernel(first, second, out):
+    part = first.shape[1]
+    out[:, :part] = first[...]
+    out[:, part:] = second[...]
+
+
+def side_by_side(line, first, second):
+    rows, columns = first.shape
+    spec = const_spec(first.shape)
+    out = (rows, 2 * columns)
+    return line.call(side_kernel, [shape(out, F32)], [const_spec(out)], [first, second], [spec, spec])[0]
 
 
 class Plan:
@@ -969,13 +1010,10 @@
         chip, u, o, p = retention(line, i, q, k, v, switch, seg_row, logs, w_out, before)
         return (chip, across(f"R{i}", chip)), u, o, p
 
-    def normed(i):
-        before = plan[f"N{i - 1}"] if i else None
-        return second_norm(line, i, BLOCK, *plan[f"R{i}"][0], inputs, gain2, bias2, before)
-
     def fed(i):
         before = plan[f"F{i - 1}"] if i else None
-        return feed_forward(line, i, BLOCK, plan[f"N{i}"][0], cotangent, w_gate, w_up, w_down, before)
+        sums = plan[f"R{i}"][0]
+        return feed_forward(line, i, *sums, inputs, gain2, bias2, cotangent, w_gate, w_up, w_down, before)
 
     last = CHUNKS - 1
     plan.step("P0", [], lambda: projected(0, 0, 1))
@@ -983,8 +1021,7 @@
     plan.step("P1", ["R0"], lambda: projected(1, 1, CHUNKS))
     for i in range(CHUNKS):
         plan.step(f"R{i}", ["P1", f"R{i - 1}"] if i else ["P0"], lambda i=i: retained(i))
-        plan.step(f"N{i}", [f"R{i}"] + ([f"N{i - 1}"] if i else []), lambda i=i: normed(i))
-        plan.step(f"F{i}", [f"N{i}"] + ([f"F{i - 1}"] if i else []), lambda i=i: fed(i))
+        plan.step(f"F{i}", [f"R{i}"] + ([f"F{i - 1}"] if i else []), lambda i=i: fed(i))
     plan.step("H", [], lambda: beside("H", core_half(line, inputs)))
     plan.step("G", ["H"], lambda: partner_rows(line, plan["H"], gain1, bias1))
 
@@ -992,31 +1029,33 @@
         return plan["P1"][n]
 
 
-    def summed(name, lefts, rights, transposed, i):
-        chip = chip_sum(line, rows, lefts, rights, transposed, i)
-        return chip, across(f"{name}{i}", chip)
+    def summed(name, lefts, rights, transposed, i, count=rows):
+        chip = chip_sum(line, count, lefts, rights, transposed, i)
+        return chip, across(name, chip)
 
     pair = range(2)
 
     def second_sum(i):
-        _, dg, du = plan[f"F{last}"]
-        return summed("B", [dg, du], [w_gate, w_up], True, i)
+        dg, du = plan[f"F{last}"][1:3]
+        return summed(f"B{i}", [dg, du], [w_gate, w_up], True, i)
 
     def middle_back(i):
         before = plan["M1"] if i == 0 else None
-        return second_norm_back(line, i, rows, *plan[f"B{i}"], plan[f"N{last}"][1], gain2, cotangent, before)
+        return second_norm_back(line, i, rows, *plan[f"B{i}"], plan[f"F{last}"][4], gain2, cotangent, before)
 
     def first_sum(i):
         dq, dk, dv, _ = plan["AB"]
-        return summed("C", [dq, dk, dv, plan["GB"][1]], [w_query, w_key, w_value, w_swish], True, i)
+        return summed(f"C{i}", [dq, dk, dv, plan["GB"][1]], [w_query, w_key, w_value, w_swish], True, i)
 
     def inputs_back(i):
         before = plan["I1"] if i == 0 else None
         return first_norm_back(line, i, rows, *plan[f"C{i}"], inputs, gain1, plan["M0"][1], before)
 
-    def output_part(i):
-        before = plan["O1"] if i == 0 else None
-        return output_rows(line, i, rows, *plan[f"D{i}"], plan[f"N{last}"][1], before)
+    def feed_sum():
+        return summed("D", [plan[f"F{last}"][0]], [w_down], False, 0, SEQ_LEN)
+
+    def output_rows_all():
+        return output_rows(line, 0, SEQ_LEN, *plan["D"], plan[f"F{last}"][4], None)
 
     def retention_grads():
         _, q, k, v, _, cos, sin = plan["P1"]
@@ -1027,15 +1066,15 @@
         after = [] if i else ["M1"]
         plan.step(f"B{i}", [f"F{last}"], lambda i=i: second_sum(i))
         plan.step(f"M{i}", [f"B{i}"] + after, lambda i=i: middle_back(i))
-        plan.step(f"D{i}", [f"F{last}"], lambda i=i: summed("D", [plan[f"F{last}"][0]], [w_down], False, i))
-        plan.step(f"O{i}", [f"D{i}"] + ([] if i else ["O1"]), lambda i=i: output_part(i))
+    plan.step("D", [f"F{last}"], feed_sum)
+    plan.step("O", ["D"], output_rows_all)
     plan.step("GB", ["M0"], lambda: gate_back(line, plan["M0"][0], w_out, plan[f"R{last}"][2], first(4)))
     plan.step("AB", ["GB"], retention_grads)
     for i in reversed(pair):
         plan.step(f"C{i}", ["AB"], lambda i=i: first_sum(i))
         plan.step(f"I{i}", [f"C{i}", "M0"] + ([] if i else ["I1"]), lambda i=i: inputs_back(i))
     plan.step("CI", ["I0"], lambda: own_copy(line, plan["I0"][0]))
-    plan.step("CO", ["O0"], lambda: own_copy(line, plan["O0"]))
+    plan.step("CO", ["O"], lambda: own_copy(line, plan["O"]))
 
 
     def small_sums():
@@ -1050,12 +1089,12 @@
     plan.step("L", ["I0", "M0"], small_sums)
 
 
-    def products(name, needs, operands, by_rows, extra=tuple):
+    def products(name, needs, operands, by_rows, extra=tuple, skip=0):
         cut = (groups + 1) // 2
 
         def send(part, begin, end):
             left, right = operands()
-            blocks = sent_blocks(line, where, left, right, by_rows, groups, begin, end - begin, extra())
+            blocks = sent_blocks(line, where, left, right, by_rows, groups, begin, end - begin, extra(), skip)
             return beside(f"S{name}{part}", blocks)
 
         def ring(j):
@@ -1063,8 +1102,9 @@
             travelling = plan[f"K{name}{j - 1}"] if j else None
             left, right = operands()
             received = plan[f"S{name}{part}"]
+            done = j == groups - 1
             block = kept_block(
-                line, where, left, right, by_rows, groups, j, received, index, travelling, extra(), j == groups - 1
+                line, where, left, right, by_rows, groups, j, received, index, travelling, extra(), done, skip
             )
             return onward(f"K{name}{j}", block) if j < groups - 1 else block
 
@@ -1076,12 +1116,11 @@
         return lambda: plan[f"K{name}{groups - 1}"]
 
 
-    def ring_first(name, needs, operands):
+    def ring_first(name, needs, operands, columns):
         def ring(j):
             travelling = plan[f"K{name}{j - 1}"] if j else None
-            left, right = operands()
             block = wide_block(
-                line, where, [(left, right)], groups, j, travelling, j == groups - 1, right.shape[1]
+                line, where, [operands()], groups, j, travelling, j == groups - 1, columns, False
             )
             if j < groups - 1:
                 return onward(f"K{name}{j}", block)
@@ -1099,7 +1138,7 @@
             right = operand()
             pairs = [(first(0), right), (plan["G"], plan[f"T{name}"])]
             block = wide_block(
-                line, where, pairs, groups, j, travelling, j == groups - 1, right.shape[1] // 2
+                line, where, pairs, groups, j, travelling, j == groups - 1, right.shape[1] // 2, True
             )
             if j < groups - 1:
                 return onward(f"J{name}{j}", block)
@@ -1112,21 +1151,24 @@
         return lambda: plan[f"E{name}"]
 
     fed_all = lambda n: plan[f"F{last}"][n]
-    normed2 = lambda: plan[f"N{last}"][0]
+    normed2 = lambda: plan[f"F{last}"][3]
     down = products("d", [f"F{last}"], lambda: (fed_all(0), cotangent), False)
     gate = products("g", [f"F{last}"], lambda: (normed2(), fed_all(1)), True)
-    up = ring_first("u", [f"F{last}"], lambda: (normed2(), fed_all(2)))
+    half_ff = w_up.shape[1] // 2
+    up = ring_first("u", [f"F{last}"], lambda: (normed2(), fed_all(2)), half_ff)
+    more_up = products("w", [f"F{last}"], lambda: (normed2(), fed_all(2)), True, skip=half_ff)
     out = products("o", ["M0", "L"], lambda: (plan[f"R{last}"][1], plan["M0"][0]), False, lambda: plan["L"])
+    plan.step("U", ["Eu", f"Kw{groups - 1}"], lambda: side_by_side(line, up(), more_up()))
     swish = shares("s", ["GB"], lambda: plan["GB"][1], 1)
     vgrad = shares("v", ["AB"], lambda: plan["AB"][2], 1)
     both = shares("q", ["AB"], lambda: plan["AB"][3], 2)
 
     plan.run(
-        "P0", "R0", "P1", "R1", "N0", "R2", "R3", "F0", "N1", "F1", "H", "N2", "F2", "N3", "F3", "Ku0", "B1", "SdA",
-        "B0", "Ku1", "SgA", "M1", "SdB", "G", "Kd0", "Ku2", "M0", "Kd1", "GB", "AB", "Ts", "Kg0", "C1", "Tv", "C0",
-        "Ku3", "Kg1", "Tq", "Kd2", "Js0", "SgB", "~Kg1", "D1", "I1", "Kd3", "Jv0", "I0", "L", "Js1", "SoA", "Jv1",
-        "Jq0", "Js2", "D0", "Jv2", "SoB", "Jq1", "~Js2", "Kg2", "Ko0", "O1", "Jq2", "Js3", "CI", "Ko1", "O0", "CO",
-        "Jq3", "Eu", "Eq", "Ko2", "Es", "Jv3", "Ev", "Ko3", "Kg3",
+        "P0", "R0", "P1", "R1", "H", "R2", "F0", "~R1", "R3", "F1", "F2", "F3", "B1", "SwA", "Ku0", "SgA", "SwB",
+        "B0", "Kw0", "Ku1", "G", "Kw1", "~B1", "SdA", "M1", "Ku2", "~Kw1", "Kg0", "M0", "GB", "Ts", "~Ku2", "Kd0",
+        "AB", "Kg1", "C1", "Kd1", "Tq", "Ku3", "~Kg1", "Tv", "Js0", "C0", "~Kd1", "Kw2", "I1", "Js1", "Kw3", "Jv0",
+        "Js2", "I0", "L", "SgB", "SoA", "Jq0", "Jv1", "D", "CI", "SdB", "Js3", "Jq1", "Jv2", "Ko0", "Jq2", "SoB",
+        "Eu", "Kg2", "Ko1", "Jv3", "O", "U", "CO", "Ko2", "Jq3", "Kd2", "Eq", "Kg3", "Ko3", "Es", "Ev", "Kd3",
     )
     plan.run(*plan.steps)
     query, key = both()
@@ -1144,7 +1186,7 @@
         small[2],
         small[3],
         gate(),
-        up(),
+        plan["U"],
         down(),
     )
 

time: 734 us -> 696 us (0.948)
  waiting for transfers between devices: 169 us -> 115 us
  starting transfers between devices: 44.1 us -> 53.8 us
    ppermute x21 -> x24, waiting for transfers between devices: 127 us -> 86.5 us  [onward(): lax.ppermute(values, 'dp', [(i, (i + 2) % dp) for i in range(dp)])]
    ppermute x14 -> x16, waiting for transfers between devices: 40.8 us -> 25.8 us  [beside(): lax.ppermute(values, 'dp', [(i, i ^ 1) for i in range(dp)])]
    ppermute x21 -> x24, starting transfers between devices: 15.7 us -> 25.8 us  [onward(): lax.ppermute(values, 'dp', [(i, (i + 2) % dp) for i in range(dp)])]
    pallas_call x73 -> x74, Pallas kernels: 502 us -> 506 us  [call(): pl.pallas_call(body, out_shape=tuple(outs), grid_spec=pltpu.PrefetchScala...]
    ppermute x14 -> x16, starting transfers between devices: 16 us -> 16.6 us  [beside(): lax.ppermute(values, 'dp', [(i, i ^ 1) for i in range(dp)])]
  transfers between devices with their start and end apart: 46 -> 50, of which waited for: 19 -> 17; matrix products, arithmetic and copies ran while one was open for 0% -> 0% of each run, Pallas kernels for 66% -> 70%
where the time goes in v3:
time: 696 us; the launch traced here: 686 us
  Pallas kernels  506 us (73%)
  waiting for transfers between devices  115 us (17%)
  starting transfers between devices  53.8 us (8%)
    pallas_call x74, Pallas kernels, call(): pl.pallas_call(body, out_shape=tuple(outs), grid_spec=pltpu.PrefetchScala...  506 us
    ppermute x24, waiting for transfers between devices, onward(): lax.ppermute(values, 'dp', [(i, (i + 2) % dp) for i in range(dp)])  86.5 us
    ppermute x24, starting transfers between devices, onward(): lax.ppermute(values, 'dp', [(i, (i + 2) % dp) for i in range(dp)])  25.8 us
    ppermute x16, waiting for transfers between devices, beside(): lax.ppermute(values, 'dp', [(i, i ^ 1) for i in range(dp)])  25.8 us
    ppermute x16, starting transfers between devices, beside(): lax.ppermute(values, 'dp', [(i, i ^ 1) for i in range(dp)])  16.6 us
  transfers between devices with their start and end apart: 50, of which 17 were waited for; matrix products, arithmetic and copies ran while one was open for 0% of the time, Pallas kernels for 70%

profile of v3, /device:TPU:0, one launch (start us, length us, event | category | flops | bytes accessed | tf_op | source)
XLA Modules:
  0.0 686.2 jit_solution(18071141496893790830)
XLA Ops:
  4.4 10.1 %shard_map.263 = (bf16[1024,2048]{1,0:T(8,128)(2,1)}, bf16[1024,512]{1,0:T(8,128)(2,1)}, bf16[1024,512]{1,0:T(8,128)(2,1)}, bf16[1024,1024]{1,0:T(8,128)(2,1)}, ...) custom-call(bf16[1024,2048]{1,0:T(8,128)(2,1)} %refs_2_.24, f32[1,2048]{1,0:T(1,128)} %bitcast.16, ...), custom_call_target="tpu_custom_call" | custom-call | flops 1 | bytes 1 | tf_op jit(solution)/shard_map/pallas_call | solution.py:108
  14.5 9.7 %shard_map.264 = (f32[128,2048]{1,0:T(8,128)}, bf16[1024,1024]{1,0:T(8,128)(2,1)}, f32[1024,1024]{1,0:T(8,128)}, bf16[2,256,256]{2,1,0:T(8,128)(2,1)}) custom-call(bf16[1024,512]{1,0:T(8,128)(2,1)} %get-tuple-element.97.refs_0_.refs_12_, bf16[1024,512]{1,0:T(8,128)(2,1)} %get-tuple-element.98.refs_1_.refs_13_, ...), custom_call_target="tpu_custom_call" | custom-call | flops 1 | bytes 1 | tf_op jit(solution)/shard_map/pallas_call | solution.py:108
  27.0 18.3 %shard_map.265 = (bf16[1024,2048]{1,0:T(8,128)(2,1)}, bf16[1024,512]{1,0:T(8,128)(2,1)}, bf16[1024,512]{1,0:T(8,128)(2,1)}, bf16[1024,1024]{1,0:T(8,128)(2,1)}, ...) custom-call(bf16[1024,2048]{1,0:T(8,128)(2,1)} %refs_2_.24, ...), custom_call_target="tpu_custom_call", output_to_operand_aliasing={{0}: (11, {}), {1}: (12, {}), {2}: (13, {}), {3}: (14, {}),... | custom-call | flops 1 | bytes 1 | tf_op jit(solution)/shard_map/pallas_call | solution.py:108
  45.2 9.4 %shard_map.266 = (f32[128,2048]{1,0:T(8,128)}, bf16[1024,1024]{1,0:T(8,128)(2,1)}, f32[1024,1024]{1,0:T(8,128)}, bf16[2,256,512]{2,1,0:T(8,128)(2,1)}) custom-call(bf16[1024,512]{1,0:T(8,128)(2,1)} %get-tuple-element.104.refs_0_, bf16[1024,512]{1,0:T(8,128)(2,1)} %get-tuple-element.105.refs_1_, ...), custom_call_target="tpu_custom_call", output_to_operand_aliasing={{1}: (7, {}), {2}: (8, {})} | custom-call | flops 1 | bytes 1 | tf_op jit(solution)/shard_map/pallas_call | solution.py:108
  62.0 9.5 %shard_map.268 = (f32[128,2048]{1,0:T(8,128)}, bf16[1024,1024]{1,0:T(8,128)(2,1)}, f32[1024,1024]{1,0:T(8,128)}, bf16[2,256,768]{2,1,0:T(8,128)(2,1)}) custom-call(bf16[1024,512]{1,0:T(8,128)(2,1)} %get-tuple-element.104.refs_0_, bf16[1024,512]{1,0:T(8,128)(2,1)} %get-tuple-element.105.refs_1_, ...), custom_call_target="tpu_custom_call", output_to_operand_aliasing={{1}: (7, {}), {2}: (8, {})} | custom-call | flops 1 | bytes 1 | tf_op jit(solution)/shard_map/pallas_call | solution.py:108
  73.1 14.3 %shard_map.269 = (bf16[1024,1024]{1,0:T(8,128)(2,1)}, bf16[1024,1024]{1,0:T(8,128)(2,1)}, bf16[1024,1024]{1,0:T(8,128)(2,1)}, bf16[1024,2048]{1,0:T(8,128)(2,1)}, f32[512,2048]{1,0:T(8,128)}) custom-call(f32[128,2048]{1,0:T(8,128)} %get-tuple-element.103.refs_18_.refs_0_, f32[128,2048]{1,0:T(8,128)} %collective-permute-done.refs_1_, ...), custom_call_target="tpu_custom_call" | custom-call | flops 1 | bytes 1 | tf_op jit(solution)/shard_map/pallas_call | solution.py:108
  87.4 9.4 %shard_map.270 = (f32[128,2048]{1,0:T(8,128)}, bf16[1024,1024]{1,0:T(8,128)(2,1)}, f32[1024,1024]{1,0:T(8,128)}, bf16[2,256,768]{2,1,0:T(8,128)(2,1)}) custom-call(bf16[1024,512]{1,0:T(8,128)(2,1)} %get-tuple-element.104.refs_0_, bf16[1024,512]{1,0:T(8,128)(2,1)} %get-tuple-element.105.refs_1_, ...), custom_call_target="tpu_custom_call", output_to_operand_aliasing={{1}: (7, {}), {2}: (8, {})} | custom-call | flops 1 | bytes 1 | tf_op jit(solution)/shard_map/pallas_call | solution.py:108
  97.4 14.1 %shard_map.271 = (bf16[1024,1024]{1,0:T(8,128)(2,1)}, bf16[1024,1024]{1,0:T(8,128)(2,1)}, bf16[1024,1024]{1,0:T(8,128)(2,1)}, bf16[1024,2048]{1,0:T(8,128)(2,1)}, f32[512,2048]{1,0:T(8,128)}) custom-call(f32[128,2048]{1,0:T(8,128)} %get-tuple-element.113.refs_1_.refs_0_, ...), custom_call_target="tpu_custom_call", output_to_operand_aliasing={{0}: (9, {}), {1}: (10, {}), {2}: (11, {}), {3}: (12, {}), ... | custom-call | flops 1 | bytes 1 | tf_op jit(solution)/shard_map/pallas_call | solution.py:108
  111.6 14.2 %shard_map.272 = (bf16[1024,1024]{1,0:T(8,128)(2,1)}, bf16[1024,1024]{1,0:T(8,128)(2,1)}, bf16[1024,1024]{1,0:T(8,128)(2,1)}, bf16[1024,2048]{1,0:T(8,128)(2,1)}, f32[512,2048]{1,0:T(8,128)}) custom-call(f32[128,2048]{1,0:T(8,128)} %get-tuple-element.116.refs_9_.refs_0_, ...), custom_call_target="tpu_custom_call", output_to_operand_aliasing={{0}: (9, {}), {1}: (10, {}), {2}: (11, {}), {3}: (12, {}), ... | custom-call | flops 1 | bytes 1 | tf_op jit(solution)/shard_map/pallas_call | solution.py:108
  125.8 14.4 %shard_map.273 = (bf16[1024,1024]{1,0:T(8,128)(2,1)}, bf16[1024,1024]{1,0:T(8,128)(2,1)}, bf16[1024,1024]{1,0:T(8,128)(2,1)}, bf16[1024,2048]{1,0:T(8,128)(2,1)}, f32[512,2048]{1,0:T(8,128)}) custom-call(f32[128,2048]{1,0:T(8,128)} %get-tuple-element.118.refs_14_.refs_0_, ...), custom_call_target="tpu_custom_call", output_to_operand_aliasing={{0}: (9, {}), {1}: (10, {}), {2}: (11, {}), {3}: (12, {}), ... | custom-call | flops 1 | bytes 1 | tf_op jit(solution)/shard_map/pallas_call | solution.py:108
  140.2 11.2 %shard_map.274.refs_3_.refs_0_ = f32[256,2048]{1,0:T(8,128)} custom-call(bf16[1024,1024]{1,0:T(8,128)(2,1)} %get-tuple-element.134.refs_0_.refs_2_, bf16[1024,1024]{1,0:T(8,128)(2,1)} %get-tuple-element.135.refs_1_.refs_2_, bf16[2048,1024]{1,0:T(8,128)(2,1)} %refs_2_.19, bf16[2048,1024]{1,0:T(8,128)(2,1)} %refs_3_.3, ...), custom_call_target="tpu_custom_call" | custom-call | flops 1 | bytes 1 | tf_op jit(solution)/shard_map/pallas_call | solution.py:108
  173.7 11.2 %shard_map.279.refs_4_.refs_0_ = f32[256,2048]{1,0:T(8,128)} custom-call(bf16[1024,1024]{1,0:T(8,128)(2,1)} %get-tuple-element.134.refs_0_.refs_2_, bf16[1024,1024]{1,0:T(8,128)(2,1)} %get-tuple-element.135.refs_1_.refs_2_, bf16[2048,1024]{1,0:T(8,128)(2,1)} %refs_2_.19, bf16[2048,1024]{1,0:T(8,128)(2,1)} %refs_3_.3, f32[2,256,512]{2,1,0:T(8,128)} %shard_map.278.refs_4_), custom_call_target="tpu_custom_call" | custom-call | flops 1 | bytes 1 | tf_op jit(solution)/shard_map/pallas_call | solution.py:108
  196.0 12.0 %shard_map.282.refs_5_.refs_3_ = bf16[1024,2048]{1,0:T(8,128)(2,1)} custom-call(f32[512,2048]{1,0:T(8,128)} %collective-permute-done.8.refs_0_, f32[1,2048]{1,0:T(1,128)} %bitcast.18, f32[1,2048]{1,0:T(1,128)} %bitcast.27, f32[512,512]{1,0:T(8,128)} %shard_map.281.refs_3_), custom_call_target="tpu_custom_call" | custom-call | flops 1 | bytes 1 | tf_op jit(solution)/shard_map/pallas_call | solution.py:108
  219.1 10.7 %shard_map.285 = (bf16[1024,2048]{1,0:T(8,128)(2,1)}, f32[512,2048]{1,0:T(8,128)}, f32[1,2048]{1,0:T(1,128)}, f32[1,2048]{1,0:T(1,128)}) custom-call(f32[256,2048]{1,0:T(8,128)} %shard_map.274.refs_3_.refs_0_, f32[256,2048]{1,0:T(8,128)} %collective-permute-done.5.refs_4_.refs_1_, f32[512,2048]{1,0:T(8,128)} %get-tuple-element.137.refs_2_, ...), custom_call_target="tpu_custom_call" | custom-call | flops 1 | bytes 1 | tf_op jit(solution)/shard_map/pallas_call | solution.py:108
  244.6 10.7 %shard_map.288 = (bf16[1024,2048]{1,0:T(8,128)(2,1)}, f32[512,2048]{1,0:T(8,128)}, f32[1,2048]{1,0:T(1,128)}, f32[1,2048]{1,0:T(1,128)}) custom-call(f32[256,2048]{1,0:T(8,128)} %shard_map.279.refs_4_.refs_0_, f32[256,2048]{1,0:T(8,128)} %collective-permute-done.4.refs_1_, ...), custom_call_target="tpu_custom_call", output_to_operand_aliasing={{0}: (5, {}), {1}: (6, {})} | custom-call | flops 1 | bytes 1 | tf_op jit(solution)/shard_map/pallas_call | solution.py:108
  255.3 12.8 %shard_map.289 = (bf16[1024,1024]{1,0:T(8,128)(2,1)}, bf16[1024,1024]{1,0:T(8,128)(2,1)}) custom-call(bf16[1024,2048]{1,0:T(8,128)(2,1)} %get-tuple-element.140.refs_0_.refs_2_, bf16[1024,2048]{1,0:T(8,128)(2,1)} %refs_1_.2, f32[1024,1024]{1,0:T(8,128)} %get-tuple-element.141.refs_2_, f32[1024,1024]{1,0:T(8,128)} %get-tuple-element.107.refs_3_), custom_call_target="tpu_custom_call" | custom-call | flops 1 | bytes 1 | tf_op jit(solution)/shard_map/pallas_call | solution.py:108
  278.6 12.2 %shard_map.292 = (bf16[1024,512]{1,0:T(8,128)(2,1)}, bf16[1024,512]{1,0:T(8,128)(2,1)}, bf16[1024,1024]{1,0:T(8,128)(2,1)}, bf16[1024,1024]{1,0:T(8,128)(2,1)}) custom-call(bf16[1024,512]{1,0:T(8,128)(2,1)} %get-tuple-element.104.refs_0_, bf16[1024,512]{1,0:T(8,128)(2,1)} %get-tuple-element.105.refs_1_, bf16[1024,1024]{1,0:T(8,128)(2,1)} %get-tuple-element.106.refs_2_, ...), custom_call_target="tpu_custom_call" | custom-call | flops 1 | bytes 1 | tf_op jit(solution)/shard_map/pallas_call | solution.py:108
  296.7 13.8 %shard_map.294.refs_5_.refs_0_ = f32[256,2048]{1,0:T(8,128)} custom-call(bf16[1024,512]{1,0:T(8,128)(2,1)} %get-tuple-element.152.refs_5_.refs_0_, bf16[1024,512]{1,0:T(8,128)(2,1)} %get-tuple-element.153.refs_1_, bf16[1024,1024]{1,0:T(8,128)(2,1)} %get-tuple-element.150.refs_2_.refs_1_, bf16[1024,1024]{1,0:T(8,128)(2,1)} %get-tuple-element.149.refs_1_.refs_3_.refs_2_, ...), custom_call_target="tpu_custom_call" | custom-call | flops 1 | bytes 1 | tf_op jit(solution)/shard_map/pallas_call | solution.py:108
  338.6 13.8 %shard_map.300.refs_5_.refs_0_ = f32[256,2048]{1,0:T(8,128)} custom-call(bf16[1024,512]{1,0:T(8,128)(2,1)} %get-tuple-element.152.refs_5_.refs_0_, bf16[1024,512]{1,0:T(8,128)(2,1)} %get-tuple-element.153.refs_1_, bf16[1024,1024]{1,0:T(8,128)(2,1)} %get-tuple-element.150.refs_2_.refs_1_, bf16[1024,1024]{1,0:T(8,128)(2,1)} %get-tuple-element.149.refs_1_.refs_3_.refs_2_, ...), custom_call_target="tpu_custom_call" | custom-call | flops 1 | bytes 1 | tf_op jit(solution)/shard_map/pallas_call | solution.py:108
  361.1 10.8 %shard_map.302 = (f32[1024,2048]{1,0:T(8,128)}, f32[1,2048]{1,0:T(1,128)}, f32[1,2048]{1,0:T(1,128)}) custom-call(f32[256,2048]{1,0:T(8,128)} %shard_map.294.refs_5_.refs_0_, f32[256,2048]{1,0:T(8,128)} %collective-permute-done.24.refs_1_, bf16[1024,2048]{1,0:T(8,128)(2,1)} %refs_2_.24, f32[1,2048]{1,0:T(1,128)} %bitcast.19, ...), custom_call_target="tpu_custom_call" | custom-call | flops 1 | bytes 1 | tf_op jit(solution)/shard_map/pallas_call | solution.py:108
  395.2 12.9 %collective-permute-done.28.refs_5_ = f32[512,512]{1,0:T(8,128)} collective-permute-done((f32[512,512]{1,0:T(8,128)}, f32[512,512]{1,0:T(8,128)}, u32[]{:S(2)}, u32[]{:S(2)}) %collective-permute-start.28) | collective-permute-done | bytes 1048608 | tf_op jit(solution)/shard_map/ppermute | solution.py:995
  413.7 10.8 %shard_map.307 = (f32[1024,2048]{1,0:T(8,128)}, f32[1,2048]{1,0:T(1,128)}, f32[1,2048]{1,0:T(1,128)}) custom-call(f32[256,2048]{1,0:T(8,128)} %shard_map.300.refs_5_.refs_0_, f32[256,2048]{1,0:T(8,128)} %collective-permute-done.27.refs_1_, bf16[1024,2048]{1,0:T(8,128)(2,1)} %refs_2_.24, f32[1,2048]{1,0:T(1,128)} %bitcast.20, ...), custom_call_target="tpu_custom_call", output_to_operand_aliasing={{0}: (5, {})} | custom-call | flops 1 | bytes 1 | tf_op jit(solution)/shard_map/pallas_call | solution.py:108
  449.9 12.7 %shard_map.312.refs_1_.refs_0_ = f32[512,2048]{1,0:T(8,128)} custom-call(bf16[1024,1024]{1,0:T(8,128)(2,1)} %get-tuple-element.133.refs_4_.refs_1_.refs_0_, bf16[1024,2048]{1,0:T(8,128)(2,1)} %refs_1_.3, f32[512,512]{1,0:T(8,128)} %shard_map.311.refs_2_), custom_call_target="tpu_custom_call" | custom-call | flops 1 | bytes 1 | tf_op jit(solution)/shard_map/pallas_call | solution.py:108
  466.4 7.1 %shard_map.313.refs_3_ = f32[1024,2048]{1,0:T(8,128)} custom-call(f32[1024,2048]{1,0:T(8,128)} %get-tuple-element.166.refs_3_.refs_0_, f32[512,2048]{1,0:T(8,128)} %shard_map.312.refs_1_.refs_0_), custom_call_target="tpu_custom_call" | custom-call | flops 1 | bytes 1 | tf_op jit(solution)/shard_map/pallas_call | solution.py:108
  478.6 5.7 shard_map.315
  509.0 11.4 %collective-permute-done.39.refs_5_ = f32[512,512]{1,0:T(8,128)} collective-permute-done((f32[512,512]{1,0:T(8,128)}, f32[512,512]{1,0:T(8,128)}, u32[]{:S(2)}, u32[]{:S(2)}) %collective-permute-start.39) | collective-permute-done | bytes 1048608 | tf_op jit(solution)/shard_map/ppermute | solution.py:995
  532.1 10.2 %collective-permute-done.38.refs_0_ = f32[256,512]{1,0:T(8,128)} collective-permute-done((f32[256,512]{1,0:T(8,128)S(1)}, f32[256,512]{1,0:T(8,128)}, u32[]{:S(2)}, u32[]{:S(2)}) %collective-permute-start.38) | collective-permute-done | bytes 524320 | tf_op jit(solution)/shard_map/ppermute | solution.py:991
  557.3 13.3 %collective-permute-done.34.refs_5_ = f32[512,512]{1,0:T(8,128)} collective-permute-done((f32[512,512]{1,0:T(8,128)}, f32[512,512]{1,0:T(8,128)}, u32[]{:S(2)}, u32[]{:S(2)}) %collective-permute-start.34) | collective-permute-done | bytes 1048608 | tf_op jit(solution)/shard_map/ppermute | solution.py:995
  576.5 14.2 %shard_map.325.refs_2_.refs_0_ = bf16[1024,2048]{1,0:T(8,128)(2,1)} custom-call(f32[512,2048]{1,0:T(8,128)} %shard_map.312.refs_1_.refs_0_, f32[512,2048]{1,0:T(8,128)} %collective-permute-done.30.refs_1_, f32[512,2048]{1,0:T(8,128)} %get-tuple-element.137.refs_2_, f32[256,512]{1,0:T(8,128)} %get-tuple-element.169.refs_3_), custom_call_target="tpu_custom_call" | custom-call | flops 1 | bytes 1 | tf_op jit(solution)/shard_map/pallas_call | solution.py:108
  605.5 10.2 %collective-permute-done.44.refs_5_ = f32[512,512]{1,0:T(8,128)} collective-permute-done((f32[512,512]{1,0:T(8,128)}, f32[512,512]{1,0:T(8,128)}, u32[]{:S(2)}, u32[]{:S(2)}) %collective-permute-start.44) | collective-permute-done | bytes 1048608 | tf_op jit(solution)/shard_map/ppermute | solution.py:995
  622.3 10.3 %collective-permute-done.46.refs_3_ = f32[2,1024,256]{2,1,0:T(8,128)} collective-permute-done((f32[2,1024,256]{2,1,0:T(8,128)}, f32[2,1024,256]{2,1,0:T(8,128)}, u32[]{:S(2)}, u32[]{:S(2)}) %collective-permute-start.46) | collective-permute-done | bytes 2097184 | tf_op jit(solution)/shard_map/ppermute | solution.py:991
  647.7 13.1 %collective-permute-done.43.refs_4_ = f32[256,1024]{1,0:T(8,128)} collective-permute-done((f32[256,1024]{1,0:T(8,128)}, f32[256,1024]{1,0:T(8,128)}, u32[]{:S(2)}, u32[]{:S(2)}) %collective-permute-start.43) | collective-permute-done | bytes 1048608 | tf_op jit(solution)/shard_map/ppermute | solution.py:995
  (184 shorter events, 310.3 us)
Async XLA Ops:
  24.1 48.9 %collective-permute-start = (f32[128,2048]{1,0:T(8,128)}, f32[128,2048]{1,0:T(8,128)}, u32[]{:S(2)}, u32[]{:S(2)}) collective-permute-start(f32[128,2048]{1,0:T(8,128)} %get-tuple-element.103.refs_18_.refs_0_), channel_id=1, source_target_pairs={{0,2},{1,3},{2,0},{3,1},{4,6},{5,7},{6,4},{7,5},{8,10},{9,11},{10,... | collective-permute-start | bytes 3145736 | tf_op jit(solution)/shard_map/ppermute | solution.py:999
  60.1 134.3 %collective-permute-start.8 = (f32[512,2048]{1,0:T(8,128)}, f32[512,2048]{1,0:T(8,128)}, u32[]{:S(2)}, u32[]{:S(2)}) collective-permute-start(f32[512,2048]{1,0:T(8,128)} %shard_map.267.refs_9_), channel_id=1, source_target_pairs={{0,4},{4,0},{8,12},{12,8},{16,20},{20,16},{24,28},{28,24},{1,5},{5... | collective-permute-start | bytes 12582920 | tf_op jit(solution)/shard_map/ppermute | solution.py:991
  71.5 40.1 %collective-permute-start.3 = (f32[128,2048]{1,0:T(8,128)}, f32[128,2048]{1,0:T(8,128)}, u32[]{:S(2)}, u32[]{:S(2)}) collective-permute-start(f32[128,2048]{1,0:T(8,128)} %get-tuple-element.116.refs_9_.refs_0_), channel_id=1, source_target_pairs={{0,2},{1,3},{2,0},{3,1},{4,6},{5,7},{6,4},{7,5},{8,10},{9,11},{10,... | collective-permute-start | bytes 3145736 | tf_op jit(solution)/shard_map/ppermute | solution.py:999
  151.4 61.1 %collective-permute-start.5 = (f32[256,2048]{1,0:T(8,128)}, f32[256,2048]{1,0:T(8,128)}, u32[]{:S(2)}, u32[]{:S(2)}) collective-permute-start(f32[256,2048]{1,0:T(8,128)} %shard_map.274.refs_3_.refs_0_), channel_id=1, source_target_pairs={{0,2},{1,3},{2,0},{3,1},{4,6},{5,7},{6,4},{7,5},{8,10},{9,11},{10,... | collective-permute-start | bytes 6291464 | tf_op jit(solution)/shard_map/ppermute | solution.py:999
  168.3 66.9 %collective-permute-start.10 = (f32[2,256,1024]{2,1,0:T(8,128)}, f32[2,256,1024]{2,1,0:T(8,128)}, u32[]{:S(2)}, u32[]{:S(2)}) collective-permute-start(f32[2,256,1024]{2,1,0:T(8,128)} %shard_map.277.refs_3_), channel_id=1, source_target_pairs={{0,4},{4,0},{8,12},{12,8},{16,20},{20,16},{24,28},{28,24},{1,5},{5... | collective-permute-start | bytes 6291464 | tf_op jit(solution)/shard_map/ppermute | solution.py:991
  189.9 54.7 %collective-permute-start.4 = (f32[256,2048]{1,0:T(8,128)}, f32[256,2048]{1,0:T(8,128)}, u32[]{:S(2)}, u32[]{:S(2)}) collective-permute-start(f32[256,2048]{1,0:T(8,128)} %shard_map.279.refs_4_.refs_0_), channel_id=1, source_target_pairs={{0,2},{1,3},{2,0},{3,1},{4,6},{5,7},{6,4},{7,5},{8,10},{9,11},{10,... | collective-permute-start | bytes 6291464 | tf_op jit(solution)/shard_map/ppermute | solution.py:999
  217.5 55.2 %collective-permute-start.13 = (f32[2,1024,256]{2,1,0:T(8,128)}, f32[2,1024,256]{2,1,0:T(8,128)}, u32[]{:S(2)}, u32[]{:S(2)}) collective-permute-start(f32[2,1024,256]{2,1,0:T(8,128)} %shard_map.284.refs_5_), channel_id=1, source_target_pairs={{0,4},{4,0},{8,12},{12,8},{16,20},{20,16},{24,28},{28,24},{1,5},{5... | collective-permute-start | bytes 6291464 | tf_op jit(solution)/shard_map/ppermute | solution.py:991
  233.9 38.3 %collective-permute-start.14 = (f32[512,512]{1,0:T(8,128)}, f32[512,512]{1,0:T(8,128)}, u32[]{:S(2)}, u32[]{:S(2)}) collective-permute-start(f32[512,512]{1,0:T(8,128)} %shard_map.286.refs_4_), channel_id=1, source_target_pairs={{0,8},{4,12},{8,16},{12,20},{16,24},{20,28},{24,0},{28,4},{1,9},{5... | collective-permute-start | bytes 3145736 | tf_op jit(solution)/shard_map/ppermute | solution.py:995
  242.9 47.9 %collective-permute-start.16 = (f32[256,1024]{1,0:T(8,128)}, f32[256,1024]{1,0:T(8,128)}, u32[]{:S(2)}, u32[]{:S(2)}) collective-permute-start(f32[256,1024]{1,0:T(8,128)} %shard_map.287.refs_7_), channel_id=1, source_target_pairs={{0,8},{4,12},{8,16},{12,20},{16,24},{20,28},{24,0},{28,4},{1,9},{5... | collective-permute-start | bytes 3145736 | tf_op jit(solution)/shard_map/ppermute | solution.py:995
  271.2 62.3 %collective-permute-start.20 = (f32[1024,512]{1,0:T(8,128)}, f32[1024,512]{1,0:T(8,128)}, u32[]{:S(2)}, u32[]{:S(2)}) collective-permute-start(f32[1024,512]{1,0:T(8,128)} %shard_map.290.refs_4_), channel_id=1, source_target_pairs={{0,4},{4,0},{8,12},{12,8},{16,20},{20,16},{24,28},{28,24},{1,5},{5... | collective-permute-start | bytes 6291464 | tf_op jit(solution)/shard_map/ppermute | solution.py:991
  276.7 35.9 %collective-permute-start.15 = (f32[1024,256]{1,0:T(8,128)}, f32[1024,256]{1,0:T(8,128)}, u32[]{:S(2)}, u32[]{:S(2)}) collective-permute-start(f32[1024,256]{1,0:T(8,128)} %shard_map.291.refs_12_), channel_id=1, source_target_pairs={{0,8},{4,12},{8,16},{12,20},{16,24},{20,28},{24,0},{28,4},{1,9},{5... | collective-permute-start | bytes 3145736 | tf_op jit(solution)/shard_map/ppermute | solution.py:995
  310.5 48.9 %collective-permute-start.24 = (f32[256,2048]{1,0:T(8,128)}, f32[256,2048]{1,0:T(8,128)}, u32[]{:S(2)}, u32[]{:S(2)}) collective-permute-start(f32[256,2048]{1,0:T(8,128)} %shard_map.294.refs_5_.refs_0_), channel_id=1, source_target_pairs={{0,2},{1,3},{2,0},{3,1},{4,6},{5,7},{6,4},{7,5},{8,10},{9,11},{10,... | collective-permute-start | bytes 6291464 | tf_op jit(solution)/shard_map/ppermute | solution.py:999
  311.1 41.3 %collective-permute-start.19 = (f32[2,256,512]{2,1,0:T(8,128)}, f32[2,256,512]{2,1,0:T(8,128)}, u32[]{:S(2)}, u32[]{:S(2)}) collective-permute-start(f32[2,256,512]{2,1,0:T(8,128)} %shard_map.278.refs_4_), channel_id=1, source_target_pairs={{0,4},{4,0},{8,12},{12,8},{16,20},{20,16},{24,28},{28,24},{1,5},{5... | collective-permute-start | bytes 3145736 | tf_op jit(solution)/shard_map/ppermute | solution.py:991
  316.9 37.1 %collective-permute-start.21 = (f32[1024,256]{1,0:T(8,128)}, f32[1024,256]{1,0:T(8,128)}, u32[]{:S(2)}, u32[]{:S(2)}) collective-permute-start(f32[1024,256]{1,0:T(8,128)} %shard_map.295.refs_2_), channel_id=1, source_target_pairs={{0,8},{4,12},{8,16},{12,20},{16,24},{20,28},{24,0},{28,4},{1,9},{5... | collective-permute-start | bytes 3145736 | tf_op jit(solution)/shard_map/ppermute | solution.py:995
  332.5 57.4 %collective-permute-start.18 = (f32[1024,512]{1,0:T(8,128)}, f32[1024,512]{1,0:T(8,128)}, u32[]{:S(2)}, u32[]{:S(2)}) collective-permute-start(f32[1024,512]{1,0:T(8,128)} %shard_map.298.refs_5_), channel_id=1, source_target_pairs={{0,4},{4,0},{8,12},{12,8},{16,20},{20,16},{24,28},{28,24},{1,5},{5... | collective-permute-start | bytes 6291464 | tf_op jit(solution)/shard_map/ppermute | solution.py:991
  352.4 61.3 %collective-permute-start.27 = (f32[256,2048]{1,0:T(8,128)}, f32[256,2048]{1,0:T(8,128)}, u32[]{:S(2)}, u32[]{:S(2)}) collective-permute-start(f32[256,2048]{1,0:T(8,128)} %shard_map.300.refs_5_.refs_0_), channel_id=1, source_target_pairs={{0,2},{1,3},{2,0},{3,1},{4,6},{5,7},{6,4},{7,5},{8,10},{9,11},{10,... | collective-permute-start | bytes 6291464 | tf_op jit(solution)/shard_map/ppermute | solution.py:999
  354.0 84.0 %collective-permute-start.26 = (f32[1024,512]{1,0:T(8,128)}, f32[1024,512]{1,0:T(8,128)}, u32[]{:S(2)}, u32[]{:S(2)}) collective-permute-start(f32[1024,512]{1,0:T(8,128)} %shard_map.296.refs_4_), channel_id=1, source_target_pairs={{0,4},{4,0},{8,12},{12,8},{16,20},{20,16},{24,28},{28,24},{1,5},{5... | collective-permute-start | bytes 6291464 | tf_op jit(solution)/shard_map/ppermute | solution.py:991
  395.1 49.2 %collective-permute-start.25 = (f32[512,512]{1,0:T(8,128)}, f32[512,512]{1,0:T(8,128)}, u32[]{:S(2)}, u32[]{:S(2)}) collective-permute-start(f32[512,512]{1,0:T(8,128)} %shard_map.305.refs_6_), channel_id=1, source_target_pairs={{0,8},{4,12},{8,16},{12,20},{16,24},{20,28},{24,0},{28,4},{1,9},{5... | collective-permute-start | bytes 3145736 | tf_op jit(solution)/shard_map/ppermute | solution.py:995
  413.6 51.2 %collective-permute-start.33 = (f32[512,512]{1,0:T(8,128)}, f32[512,512]{1,0:T(8,128)}, u32[]{:S(2)}, u32[]{:S(2)}) collective-permute-start(f32[512,512]{1,0:T(8,128)} %shard_map.306.refs_6_), channel_id=1, source_target_pairs={{0,8},{4,12},{8,16},{12,20},{16,24},{20,28},{24,0},{28,4},{1,9},{5... | collective-permute-start | bytes 3145736 | tf_op jit(solution)/shard_map/ppermute | solution.py:995
  437.0 67.5 %collective-permute-start.35 = (f32[2,1032,256]{2,1,0:T(8,128)}, f32[2,1032,256]{2,1,0:T(8,128)}, u32[]{:S(2)}, u32[]{:S(2)}) collective-permute-start(f32[2,1032,256]{2,1,0:T(8,128)} %shard_map.309.refs_5_), channel_id=1, source_target_pairs={{0,4},{4,0},{8,12},{12,8},{16,20},{20,16},{24,28},{28,24},{1,5},{5... | collective-permute-start | bytes 6340616 | tf_op jit(solution)/shard_map/ppermute | solution.py:991
  443.1 41.2 %collective-permute-start.32 = (f32[512,512]{1,0:T(8,128)}, f32[512,512]{1,0:T(8,128)}, u32[]{:S(2)}, u32[]{:S(2)}) collective-permute-start(f32[512,512]{1,0:T(8,128)} %shard_map.310.refs_6_), channel_id=1, source_target_pairs={{0,8},{4,12},{8,16},{12,20},{16,24},{20,28},{24,0},{28,4},{1,9},{5... | collective-permute-start | bytes 3145736 | tf_op jit(solution)/shard_map/ppermute | solution.py:995
  462.7 113.8 %collective-permute-start.30 = (f32[512,2048]{1,0:T(8,128)}, f32[512,2048]{1,0:T(8,128)}, u32[]{:S(2)}, u32[]{:S(2)}) collective-permute-start(f32[512,2048]{1,0:T(8,128)} %shard_map.312.refs_1_.refs_0_), channel_id=1, source_target_pairs={{0,2},{1,3},{2,0},{3,1},{4,6},{5,7},{6,4},{7,5},{8,10},{9,11},{10,... | collective-permute-start | bytes 12582920 | tf_op jit(solution)/shard_map/ppermute | solution.py:999
  464.3 79.2 %collective-permute-start.37 = (f32[2,256,1024]{2,1,0:T(8,128)}, f32[2,256,1024]{2,1,0:T(8,128)}, u32[]{:S(2)}, u32[]{:S(2)}) collective-permute-start(f32[2,256,1024]{2,1,0:T(8,128)} %shard_map.308.refs_5_), channel_id=1, source_target_pairs={{0,4},{4,0},{8,12},{12,8},{16,20},{20,16},{24,28},{28,24},{1,5},{5... | collective-permute-start | bytes 6291464 | tf_op jit(solution)/shard_map/ppermute | solution.py:991
  498.0 44.4 %collective-permute-start.38 = (f32[256,512]{1,0:T(8,128)S(1)}, f32[256,512]{1,0:T(8,128)}, u32[]{:S(2)}, u32[]{:S(2)}) collective-permute-start(f32[256,512]{1,0:T(8,128)S(1)} %copy-done.3), channel_id=1, source_target_pairs={{0,4},{4,0},{8,12},{12,8},{16,20},{20,16},{24,28},{28,24},{1,5},{5... | collective-permute-start | bytes 1572872 | tf_op jit(solution)/shard_map/ppermute | solution.py:991
  509.0 41.7 %collective-permute-start.36 = (f32[1032,256]{1,0:T(8,128)}, f32[1032,256]{1,0:T(8,128)}, u32[]{:S(2)}, u32[]{:S(2)}) collective-permute-start(f32[1032,256]{1,0:T(8,128)} %shard_map.318.refs_6_), channel_id=1, source_target_pairs={{0,8},{4,12},{8,16},{12,20},{16,24},{20,28},{24,0},{28,4},{1,9},{5... | collective-permute-start | bytes 3170312 | tf_op jit(solution)/shard_map/ppermute | solution.py:995
  531.1 66.5 %collective-permute-start.40 = (f32[2,1032,256]{2,1,0:T(8,128)}, f32[2,1032,256]{2,1,0:T(8,128)}, u32[]{:S(2)}, u32[]{:S(2)}) collective-permute-start(f32[2,1032,256]{2,1,0:T(8,128)} %shard_map.320.refs_2_), channel_id=1, source_target_pairs={{0,4},{4,0},{8,12},{12,8},{16,20},{20,16},{24,28},{28,24},{1,5},{5... | collective-permute-start | bytes 6340616 | tf_op jit(solution)/shard_map/ppermute | solution.py:991
  543.4 89.1 %collective-permute-start.46 = (f32[2,1024,256]{2,1,0:T(8,128)}, f32[2,1024,256]{2,1,0:T(8,128)}, u32[]{:S(2)}, u32[]{:S(2)}) collective-permute-start(f32[2,1024,256]{2,1,0:T(8,128)} %shard_map.314.refs_6_), channel_id=1, source_target_pairs={{0,4},{4,0},{8,12},{12,8},{16,20},{20,16},{24,28},{28,24},{1,5},{5... | collective-permute-start | bytes 6291464 | tf_op jit(solution)/shard_map/ppermute | solution.py:991
  555.6 42.0 %collective-permute-start.41 = (f32[1032,256]{1,0:T(8,128)}, f32[1032,256]{1,0:T(8,128)}, u32[]{:S(2)}, u32[]{:S(2)}) collective-permute-start(f32[1032,256]{1,0:T(8,128)} %shard_map.323.refs_6_), channel_id=1, source_target_pairs={{0,8},{4,12},{8,16},{12,20},{16,24},{20,28},{24,0},{28,4},{1,9},{5... | collective-permute-start | bytes 3170312 | tf_op jit(solution)/shard_map/ppermute | solution.py:995
  570.5 45.1 %collective-permute-start.44 = (f32[512,512]{1,0:T(8,128)}, f32[512,512]{1,0:T(8,128)}, u32[]{:S(2)}, u32[]{:S(2)}) collective-permute-start(f32[512,512]{1,0:T(8,128)} %shard_map.319.refs_5_), channel_id=1, source_target_pairs={{0,8},{4,12},{8,16},{12,20},{16,24},{20,28},{24,0},{28,4},{1,9},{5... | collective-permute-start | bytes 3145736 | tf_op jit(solution)/shard_map/ppermute | solution.py:995
  602.4 62.7 %collective-permute-start.42 = (f32[1032,256]{1,0:T(8,128)}, f32[1032,256]{1,0:T(8,128)}, u32[]{:S(2)}, u32[]{:S(2)}) collective-permute-start(f32[1032,256]{1,0:T(8,128)} %shard_map.328.refs_6_), channel_id=1, source_target_pairs={{0,8},{4,12},{8,16},{12,20},{16,24},{20,28},{24,0},{28,4},{1,9},{5... | collective-permute-start | bytes 3170312 | tf_op jit(solution)/shard_map/ppermute | solution.py:995
  603.3 57.5 %collective-permute-start.43 = (f32[256,1024]{1,0:T(8,128)}, f32[256,1024]{1,0:T(8,128)}, u32[]{:S(2)}, u32[]{:S(2)}) collective-permute-start(f32[256,1024]{1,0:T(8,128)} %shard_map.322.refs_7_), channel_id=1, source_target_pairs={{0,8},{4,12},{8,16},{12,20},{16,24},{20,28},{24,0},{28,4},{1,9},{5... | collective-permute-start | bytes 3145736 | tf_op jit(solution)/shard_map/ppermute | solution.py:995
  636.9 44.6 %collective-permute-start.49 = (f32[1024,256]{1,0:T(8,128)}, f32[1024,256]{1,0:T(8,128)}, u32[]{:S(2)}, u32[]{:S(2)}) collective-permute-start(f32[1024,256]{1,0:T(8,128)} %shard_map.330.refs_3_), channel_id=1, source_target_pairs={{0,8},{4,12},{8,16},{12,20},{16,24},{20,28},{24,0},{28,4},{1,9},{5... | collective-permute-start | bytes 3145736 | tf_op jit(solution)/shard_map/ppermute | solution.py:995
  (32 other events, 635.0 us)

commit v4 on v3

--- a/solution.py
+++ b/solution.py
@@ -188,27 +188,43 @@
     return places, copies
 
 
-def proj_kernel(
-    begin, x, gain, bias, cos, sin, cos0, sin0, wq, wk, wv, ws, a_out, q_out, k_out, v_out, s_out, c_out, n_out
-):
+def proj_kernel(begin, fetching, x, gain, bias, cos, sin, cos0, sin0, *refs):
+    wq, wk, wv, ws, a_out, q_out, k_out, v_out, s_out, c_out, n_out, x_out = refs[:12]
     chunk = begin + pl.program_id(0)
+    if fetching:
+        (wq, wk, wv, ws), fetch = fetched((wq, wk, wv, ws), refs[12:])
+        for copy in fetch:
+            copy.start()
+
+    def ready(n):
+        if fetching:
+            fetch[n].wait()
+
     centred, scale = normal_rows(x[...].astype(F32), 1e-05)
     normed = (centred * scale * gain[...] + bias[...]).astype(BF16)
     a_out[...] = normed
+    x_out[...] = x[core_rows(True, 0), :].astype(F32)
     first_cos, first_sin = cos0[pl.ds(chunk, 1), :], sin0[pl.ds(chunk, 1), :]
     cosines = cos[...] * first_cos - sin[...] * first_sin
     sines = sin[...] * first_cos + cos[...] * first_sin
     c_out[...] = cosines
     n_out[...] = sines
-    query = product_nn(normed, wq[...])
-    key = product_nn(normed, wk[...])
-    for first in range(0, query.shape[1], KEY):
-        part = slice(first, first + KEY)
-        q_out[:, part] = rotate(query[:, part], cosines, sines, 1.0).astype(BF16)
-        turned = rotate(key[:, part], cosines, sines, 1.0) * float(KEY) ** (-0.5)
+    parts = [slice(n, n + KEY) for n in range(0, wq.shape[1], KEY)]
+    ready(0)
+    for part in parts:
+        query = product_nn(normed, wq[:, part])
+        q_out[:, part] = rotate(query, cosines, sines, 1.0).astype(BF16)
+    ready(1)
+    for part in parts:
+        turned = rotate(product_nn(normed, wk[:, part]), cosines, sines, 1.0) * float(KEY) ** (-0.5)
         k_out[:, part] = turned.astype(BF16)
-    v_out[...] = product_nn(normed, wv[...]).astype(BF16)
-    s_out[...] = product_nn(normed, ws[...])
+    parts = [slice(n, n + VALUE) for n in range(0, wv.shape[1], VALUE)]
+    ready(2)
+    for part in parts:
+        v_out[:, part] = product_nn(normed, wv[:, part]).astype(BF16)
+    ready(3)
+    for part in parts:
+        s_out[:, part] = product_nn(normed, ws[:, part])
 
 
 def projections(line, begin, end, x, gain, bias, tables, wq, wk, wv, ws, before):
@@ -219,15 +235,18 @@
     def chunked(columns):
         return pl.BlockSpec((BLOCK, columns), lambda i: (begin + i, 0))
 
+    weights = (wq, wk, wv, ws)
+    alone = end - begin == 1
     return line.call(
-        functools.partial(proj_kernel, begin),
-        [shape((rows, columns), kind) for columns, kind in wide],
-        [chunked(columns) for columns, _ in wide],
+        functools.partial(proj_kernel, begin, alone),
+        [shape((rows, columns), kind) for columns, kind in wide] + [shape((rows // 2, width), F32)],
+        [chunked(columns) for columns, _ in wide] + [pl.BlockSpec((HALF, width), lambda i: (begin + i, 0))],
         [x, gain, bias, *tables, wq, wk, wv, ws],
         [chunked(width), const_spec((1, width)), const_spec((1, width))]
         + [const_spec(table.shape) for table in tables]
-        + [once_spec(w.shape) for w in (wq, wk, wv, ws)],
+        + ([ANY] * 4 if alone else [once_spec(w.shape) for w in weights]),
         grid=(end - begin,),
+        scratch=fetch_scratch(*weights) if alone else [],
         onto=() if before is None else tuple(enumerate(before)),
     )
 
@@ -296,8 +315,8 @@
         [q, k, v, switch, seg_row, logs, w],
         [
             row_spec(BLOCK, kw, chunk),
-            const_spec(k.shape),
-            const_spec(v.shape),
+            const_spec(((chunk + 1) * BLOCK, kw)),
+            const_spec(((chunk + 1) * BLOCK, vw)),
             row_spec(BLOCK, vw, chunk),
             const_spec(seg_row.shape),
             SMEM,
@@ -316,51 +335,71 @@
     )
 
 
+PIECES = 2
+
+
 def feed_kernel(
-    chip, crossed, x, gain, bias, c, wg, wu, wd, hid_out, dg_out, du_out, a_out, h_out, sent, got, s1, s2
+    chunk, chip, crossed, x, gain, bias, c, wg, wu, wd, hid_out, dg_out, du_out, a_out, h_out, back, *held
 ):
-    copy = to_other_core(sent, got, s1, s2)
-    begin = pl.program_id(0) == 0
-
-    @pl.when(begin)
-    def _():
-        meet_other_core()
-        middle = x[core_rows(True, 0), :].astype(F32) + (chip[...] + crossed[...])
-        h_out[...] = middle
+    places, loaded, sent, got, s1, s2 = held[:4], held[4], *held[5:]
+    c_in, wd_in, wg_in, wu_in = places
+    ff = back.shape[1]
+    tile = ff // TILES
+    tokens = c.at[pl.ds(chunk * BLOCK, BLOCK)]
+    fetch = [pltpu.make_async_copy(tokens, c_in, loaded.at[0]), pltpu.make_async_copy(wd, wd_in, loaded.at[1])]
+    for n, (source, place) in enumerate(((wg, wg_in), (wu, wu_in))):
+        for t in range(TILES):
+            columns = pl.ds(t * tile, tile)
+            semaphore = loaded.at[2 + 2 * t + n]
+            fetch.append(pltpu.make_async_copy(source.at[:, columns], place.at[:, columns], semaphore))
+    for copy in fetch:
+        copy.start()
+    meet_other_core()
+    piece = HALF // PIECES
+    copies = []
+    for n in range(PIECES):
+        part = pl.ds(n * piece, piece)
+        rows = pl.ds(pl.multiple_of(my_core() * HALF + n * piece, piece), piece)
+        copies.append(to_other_core(sent.at[part], got.at[part], s1.at[n], s2.at[n]))
+        middle = x[rows, :].astype(F32) + (chip[part, :] + crossed[part, :])
+        h_out[part, :] = middle
         centred, scale = normal_rows(middle, 1e-05)
         normed = (centred * scale * gain[...] + bias[...]).astype(BF16)
-        sent[...] = normed.astype(F32)
-        copy.start()
-        a_out[core_rows(True, 0), :] = normed
-
-    back = product_nt(c[...], wd[...])
-
-    @pl.when(begin)
-    def _():
-        copy.wait()
-        a_out[core_rows(False, 0), :] = got[...].astype(BF16)
-
-    gate = product_nn(a_out[...], wg[...])
-    up = product_nn(a_out[...], wu[...])
+        sent[part, :] = normed.astype(F32)
+        copies[n].start()
+        a_out[rows, :] = normed
+    fetch[0].wait()
+    fetch[1].wait()
+    for t in range(TILES):
+        columns = slice(t * tile, (t + 1) * tile)
+        back[:, columns] = product_nt(c_in[...], wd_in[columns, :])
+    for n in range(PIECES):
+        rows = pl.ds(pl.multiple_of((1 - my_core()) * HALF + n * piece, piece), piece)
+        copies[n].wait()
+        a_out[rows, :] = got[pl.ds(n * piece, piece), :].astype(BF16)
     factor = 0.7978845608028654
-    bent = jnp.tanh(factor * (gate + 0.044715 * (gate * gate * gate)))
-    half = 0.5 * (1.0 + bent)
-    active = gate * half
-    slope = half + 0.5 * gate * (1.0 - bent * bent) * (factor * (1.0 + 3 * 0.044715 * gate * gate))
-    hid_out[...] = (active * up).astype(BF16)
-    dg_out[...] = (back * up * slope).astype(BF16)
-    du_out[...] = (back * active).astype(BF16)
+    for t in range(TILES):
+        columns = slice(t * tile, (t + 1) * tile)
+        fetch[2 + t].wait()
+        fetch[2 + TILES + t].wait()
+        gate = product_nn(a_out[...], wg_in[:, columns])
+        up = product_nn(a_out[...], wu_in[:, columns])
+        bent = jnp.tanh(factor * (gate + 0.044715 * (gate * gate * gate)))
+        half = 0.5 * (1.0 + bent)
+        active = gate * half
+        slope = half + 0.5 * gate * (1.0 - bent * bent) * (factor * (1.0 + 3 * 0.044715 * gate * gate))
+        hid_out[:, columns] = (active * up).astype(BF16)
+        dg_out[:, columns] = (back[:, columns] * up * slope).astype(BF16)
+        du_out[:, columns] = (back[:, columns] * active).astype(BF16)
 
 
 def feed_forward(line, chunk, chip, crossed, x, gain, bias, c, wg, wu, wd, before):
     total, width = x.shape
     ff = wg.shape[1]
-    tile = min(256, ff)
     return line.call(
-        feed_kernel,
+        functools.partial(feed_kernel, chunk),
         [shape((total, ff), BF16)] * 3 + [shape((total, width), BF16), shape((total // 2, width), F32)],
-        [pl.BlockSpec((BLOCK, tile), lambda i: (chunk, i))] * 3
-        + [row_spec(BLOCK, width, chunk), row_spec(HALF, width, chunk)],
+        [row_spec(BLOCK, ff, chunk)] * 3 + [row_spec(BLOCK, width, chunk), row_spec(HALF, width, chunk)],
         [chip, crossed, x, gain, bias, c, wg, wu, wd],
         [
             const_spec((HALF, width)),
@@ -368,17 +407,19 @@
             row_spec(BLOCK, width, chunk),
             const_spec((1, width)),
             const_spec((1, width)),
-            row_spec(BLOCK, width, chunk),
-            pl.BlockSpec((width, tile), lambda i: (0, i)),
-            pl.BlockSpec((width, tile), lambda i: (0, i)),
-            pl.BlockSpec((tile, width), lambda i: (i, 0)),
-        ],
-        grid=(ff // tile,),
+        ]
+        + [ANY] * 4,
         scratch=[
+            pltpu.VMEM((BLOCK, ff), F32),
+            pltpu.VMEM((BLOCK, width), BF16),
+            pltpu.VMEM(wd.shape, BF16),
+            pltpu.VMEM(wg.shape, BF16),
+            pltpu.VMEM(wu.shape, BF16),
+            pltpu.SemaphoreType.DMA((2 + 2 * TILES,)),
             pltpu.VMEM((HALF, width), F32),
             pltpu.VMEM((HALF, width), F32),
-            pltpu.SemaphoreType.DMA,
-            pltpu.SemaphoreType.DMA,
+            pltpu.SemaphoreType.DMA((PIECES,)),
+            pltpu.SemaphoreType.DMA((PIECES,)),
         ],
         onto=() if before is None else tuple(enumerate(before)),
         paired=True,
@@ -445,154 +486,146 @@
     )[0]
 
 
-def shared_kernel(work, in_count, *refs):
+def shared_kernel(work, in_count, steps, *refs):
     ins, out = refs[:in_count], refs[in_count]
     extras, (sent, got, s1, s2) = refs[in_count + 1 : -4], refs[-4:]
-    meet_other_core()
-    copies = []
-    for n in range(sent.shape[0] // HALF):
-        part = pl.ds(n * HALF, HALF)
-        value = work(n, part, core_rows(True, n), *ins, *extras)
-        sent[part, :] = value
-        copies.append(to_other_core(sent.at[part], got.at[part], s1.at[n], s2.at[n]))
-        copies[-1].start()
-        out[core_rows(True, n), :] = value.astype(out.dtype)
-    for n, copy in enumerate(copies):
-        copy.wait()
-        out[core_rows(False, n), :] = got[pl.ds(n * HALF, HALF), :].astype(out.dtype)
-
-
-def shared_rows(line, work, chunk, rows, ins, in_specs, kind, total_rows, width, extras, before):
-    half = rows // 2
+    j = pl.program_id(0)
+
+    @pl.when(j == 0)
+    def _():
+        meet_other_core()
+
+    @pl.when(j < steps)
+    def _():
+        sent[j] = work(*ins, *extras)
+        to_other_core(sent.at[j], got.at[j], s1.at[j], s2.at[j]).start()
+
+    @pl.when(j > 0)
+    def _():
+        to_other_core(sent.at[j - 1], got.at[j - 1], s1.at[j - 1], s2.at[j - 1]).wait()
+        out[core_rows(True, 0), :] = sent[j - 1].astype(out.dtype)
+        out[core_rows(False, 0), :] = got[j - 1].astype(out.dtype)
+
+
+def shared_rows(line, work, begin, steps, ins, in_specs, kind, total_rows, width, extras=(), before=()):
     return line.call(
-        functools.partial(shared_kernel, work, len(ins)),
+        functools.partial(shared_kernel, work, len(ins), steps),
         [shape((total_rows, width), kind)] + [shape(dims, F32) for dims, _ in extras],
-        [row_spec(rows, width, chunk)] + [spec for _, spec in extras],
+        [pl.BlockSpec((BLOCK, width), lambda j: (begin + jnp.maximum(j, 1) - 1, 0))] + [spec for _, spec in extras],
         ins,
         in_specs,
+        grid=(steps + 1,),
         scratch=[
-            pltpu.VMEM((half, width), F32),
-            pltpu.VMEM((half, width), F32),
-            pltpu.SemaphoreType.DMA((half // HALF,)),
-            pltpu.SemaphoreType.DMA((half // HALF,)),
+            pltpu.VMEM((steps, HALF, width), F32),
+            pltpu.VMEM((steps, HALF, width), F32),
+            pltpu.SemaphoreType.DMA((steps,)),
+            pltpu.SemaphoreType.DMA((steps,)),
         ],
         onto=before,
         paired=True,
     )
 
 
-def core_half_kernel(x, out):
-    out[...] = x[core_rows(True, 0), :].astype(F32)
-
-
-def core_half(line, x):
-    rows, width = x.shape
-    return line.call(
-        core_half_kernel,
-        [shape((rows // 2, width), F32)],
-        [pl.BlockSpec((HALF, width), lambda i: (i, 0))],
-        [x],
-        [pl.BlockSpec((BLOCK, width), lambda i: (i, 0))],
-        grid=(rows // BLOCK,),
-    )[0]
-
-
-def partner_work(n, part, rows, got, gain, bias):
-    centred, scale = normal_rows(got[part, :], 1e-05)
+def stepped(rows, width, steps, begin=0):
+    return pl.BlockSpec((rows, width), lambda j: (begin + jnp.minimum(j, steps - 1), 0))
+
+
+def partner_work(got, gain, bias):
+    centred, scale = normal_rows(got[...], 1e-05)
     return (centred * scale * gain[...] + bias[...]).astype(BF16).astype(F32)
 
 
 def partner_rows(line, got, gain, bias):
     half, width = got.shape
-    specs = [const_spec(got.shape), const_spec((1, width)), const_spec((1, width))]
-    return shared_rows(
-        line, partner_work, 0, 2 * half, [got, gain, bias], specs, BF16, 2 * half, width, [], ()
-    )[0]
-
-
-def norm_back(n, back, centred, scale, gain, gain_out, bias_out):
+    steps = half // HALF
+    specs = [stepped(HALF, width, steps), const_spec((1, width)), const_spec((1, width))]
+    return shared_rows(line, partner_work, 0, steps, [got, gain, bias], specs, BF16, 2 * half, width)[0]
+
+
+def norm_back(back, centred, scale, gain, gain_out, bias_out):
     normed = centred * scale
+    begin = pl.program_id(0) == 0
     one, two = jnp.sum(back * normed, axis=0, keepdims=True), jnp.sum(back, axis=0, keepdims=True)
-    gain_out[...] = one if n == 0 else gain_out[...] + one
-    bias_out[...] = two if n == 0 else bias_out[...] + two
+
+    @pl.when(begin)
+    def _():
+        gain_out[...] = one
+        bias_out[...] = two
+
+    @pl.when(jnp.logical_not(begin))
+    def _():
+        gain_out[...] += one
+        bias_out[...] += two
+
     scaled = back * gain[...]
     first = jnp.mean(scaled, axis=-1, keepdims=True)
     second = jnp.mean(scaled * normed, axis=-1, keepdims=True)
     return scale * (scaled - first - normed * second)
 
 
-def mid_work(n, part, rows, chip, crossed, h, gain, c, dh_out, gain_out, bias_out):
-    centred, scale = normal_rows(h[part, :], 1e-05)
-    back = chip[part, :] + crossed[part, :]
-    value = c[rows, :].astype(F32) + norm_back(n, back, centred, scale, gain, gain_out, bias_out)
-    dh_out[part, :] = value
+def middle_work(chip, crossed, h, gain, c, dh_out, gain_out, bias_out):
+    centred, scale = normal_rows(h[...], 1e-05)
+    back = chip[...] + crossed[...]
+    value = c[core_rows(True, 0), :].astype(F32) + norm_back(back, centred, scale, gain, gain_out, bias_out)
+    dh_out[...] = value
     return value
 
 
-def second_norm_back(line, chunk, rows, chip, crossed, h, gain, c, before):
+def second_norm_back(line, begin, chip, crossed, h, gain, c, before):
     total, width = c.shape
-    half = rows // 2
-    owned = row_spec(half, width, chunk)
+    steps = chip.shape[0] // HALF
+    part, own = stepped(HALF, width, steps), stepped(HALF, width, steps, begin)
+    small = ((1, width), const_spec((1, width)))
     return shared_rows(
         line,
-        mid_work,
-        chunk,
-        rows,
+        middle_work,
+        begin,
+        steps,
         [chip, crossed, h, gain, c],
-        [const_spec((half, width))] * 2 + [owned, const_spec((1, width)), row_spec(rows, width, chunk)],
+        [part, part, own, const_spec((1, width)), stepped(BLOCK, width, steps, begin)],
         BF16,
         total,
         width,
-        [((total // 2, width), owned)] + [((1, width), const_spec((1, width)))] * 2,
+        [((total // 2, width), own), small, small],
         () if before is None else ((0, before[0]), (1, before[1])),
     )
 
 
-def first_work(n, part, rows, chip, crossed, x, gain, dh, gain_out, bias_out):
-    centred, scale = normal_rows(x[rows, :].astype(F32), 1e-05)
-    back = chip[part, :] + crossed[part, :]
-    return dh[part, :] + norm_back(n, back, centred, scale, gain, gain_out, bias_out)
-
-
-def first_norm_back(line, chunk, rows, chip, crossed, x, gain, dh, before):
+def first_work(chip, crossed, x, gain, dh, gain_out, bias_out):
+    centred, scale = normal_rows(x[core_rows(True, 0), :].astype(F32), 1e-05)
+    back = chip[...] + crossed[...]
+    return dh[...] + norm_back(back, centred, scale, gain, gain_out, bias_out)
+
+
+def first_norm_back(line, begin, chip, crossed, x, gain, dh, before):
     total, width = x.shape
-    half = rows // 2
+    steps = chip.shape[0] // HALF
+    part, own = stepped(HALF, width, steps), stepped(HALF, width, steps, begin)
+    small = ((1, width), const_spec((1, width)))
     return shared_rows(
         line,
         first_work,
-        chunk,
-        rows,
+        begin,
+        steps,
         [chip, crossed, x, gain, dh],
-        [const_spec((half, width))] * 2
-        + [row_spec(rows, width, chunk), const_spec((1, width)), row_spec(half, width, chunk)],
+        [part, part, stepped(BLOCK, width, steps, begin), const_spec((1, width)), own],
         F32,
         total,
         width,
-        [((1, width), const_spec((1, width)))] * 2,
+        [small, small],
         () if before is None else ((0, before[0]),),
     )
 
 
-def output_work(n, part, rows, chip, crossed, h):
-    return h[part, :] + (chip[part, :] + crossed[part, :])
-
-
-def output_rows(line, chunk, rows, chip, crossed, h, before):
-    half_total, width = h.shape
-    half = rows // 2
-    return shared_rows(
-        line,
-        output_work,
-        chunk,
-        rows,
-        [chip, crossed, h],
-        [const_spec((half, width))] * 2 + [row_spec(half, width, chunk)],
-        BF16,
-        2 * half_total,
-        width,
-        [],
-        () if before is None else ((0, before),),
-    )[0]
+def output_work(chip, crossed, h):
+    return h[...] + (chip[...] + crossed[...])
+
+
+def output_rows(line, chip, crossed, h):
+    half, width = h.shape
+    steps = half // HALF
+    specs = [stepped(HALF, width, steps)] * 3
+    return shared_rows(line, output_work, 0, steps, [chip, crossed, h], specs, BF16, 2 * half, width)[0]
 
 
 def copy_kernel(source, out):
@@ -614,41 +647,45 @@
     return line.call(add_kernel, [shape(a.shape, F32)], [spec], [a, b], [spec, spec])[0]
 
 
-def gate_kernel(dz, w, o, switch, do_out, ds_out):
-    grad = product_nt(dz[...], w[...])
-    centred, scale = normal_rows(o[...], 1.0)
-    gate = switch[...]
-    sig = jax.nn.sigmoid(gate)
-    ds_out[...] = (grad * (centred * scale) * (sig * (1.0 + gate * (1.0 - sig)))).astype(BF16)
-    dn = grad * (gate * sig)
-    one = jnp.mean(dn, axis=-1, keepdims=True)
-    two = jnp.mean(dn * centred, axis=-1, keepdims=True)
-    do_out[...] = (scale * (dn - one) - (scale * scale * scale) * centred * two).astype(BF16)
-
-
-def gate_back(line, dz, w, o, switch):
-    rows, width = dz.shape
-    vw = w.shape[0]
-    part = 512
-    tiled = pl.BlockSpec((part, VALUE), lambda h, i: (i, h))
+def gate_kernel(where, dz, w, o, switch, do_out, ds_out, far_out):
+    for head in range(o.shape[1] // VALUE):
+        part = slice(head * VALUE, (head + 1) * VALUE)
+        grad = product_nt(dz[...], w[part, :])
+        centred, scale = normal_rows(o[:, part], 1.0)
+        gate = switch[:, part]
+        sig = jax.nn.sigmoid(gate)
+        ds = (grad * (centred * scale) * (sig * (1.0 + gate * (1.0 - sig)))).astype(BF16)
+        ds_out[:, part] = ds
+        dn = grad * (gate * sig)
+        one = jnp.mean(dn, axis=-1, keepdims=True)
+        two = jnp.mean(dn * centred, axis=-1, keepdims=True)
+        do_out[:, part] = (scale * (dn - one) - (scale * scale * scale) * centred * two).astype(BF16)
+
+        @pl.when(where[0] != head)
+        def _(ds=ds):
+            far_out[...] = ds.astype(F32)
+
+
+def gate_back(line, where, dz, w, o, switch):
+    rows, vw = o.shape
+
+    def rowed(columns):
+        return pl.BlockSpec((BLOCK, columns), lambda n, w: (n, 0))
+
     return line.call(
         gate_kernel,
-        [shape((rows, vw), BF16)] * 2,
-        [tiled] * 2,
+        [shape((rows, vw), BF16), shape((rows, vw), BF16), shape((rows, vw // 2), F32)],
+        [rowed(vw), rowed(vw), rowed(vw // 2)],
         [dz, w, o, switch],
-        [
-            pl.BlockSpec((part, width), lambda h, i: (i, 0)),
-            pl.BlockSpec((VALUE, width), lambda h, i: (h, 0)),
-            tiled,
-            tiled,
-        ],
-        grid=(vw // VALUE, rows // part),
-    )
-
-
-def retain_back_kernel(q, k, v, do, seg_row, logs, cos, sin, *rest):
+        [rowed(dz.shape[1]), const_spec(w.shape), rowed(vw), rowed(vw)],
+        grid=(rows // BLOCK,),
+        scalars=where,
+    )
+
+
+def retain_back_kernel(where, q, k, v, do, seg_row, logs, cos, sin, *rest):
     weights = rest[:CHUNKS]
-    dq_out, dk_out, dv_out, both_out, dq_sum, dk_sum, dv_sum = rest[CHUNKS:]
+    dq_out, dk_out, dv_out, both_out, far_out, far_v_out, dq_sum, dk_sum, dv_sum = rest[CHUNKS:]
     head = pl.program_id(0)
     dk_sum[...] = jnp.zeros_like(dk_sum)
     dv_sum[...] = jnp.zeros_like(dv_sum)
@@ -673,20 +710,29 @@
     dk_out[...] = dk
     both_out[:, :KEY] = dq
     both_out[:, KEY:] = dk
-    dv_out[...] = dv_sum[...].astype(BF16)
-
-
-def retention_back(line, q, k, v, do, seg_row, logs, cos, sin, weights):
+    dv = dv_sum[...].astype(BF16)
+    dv_out[...] = dv
+
+    @pl.when(where[0] != head)
+    def _():
+        far_out[:, :KEY] = dq.astype(F32)
+        far_out[:, KEY:] = dk.astype(F32)
+        far_v_out[...] = dv.astype(F32)
+
+
+def retention_back(line, where, q, k, v, do, seg_row, logs, cos, sin, weights):
     rows, kw = q.shape
     vw = v.shape[1]
 
     def headed(columns):
-        return pl.BlockSpec((rows, columns), lambda h: (0, h))
+        return pl.BlockSpec((rows, columns), lambda h, w: (0, h))
 
     return line.call(
         retain_back_kernel,
-        [shape((rows, columns), BF16) for columns in (kw, kw, vw, 2 * kw)],
-        [headed(KEY), headed(KEY), headed(VALUE), headed(2 * KEY)],
+        [shape((rows, columns), BF16) for columns in (kw, kw, vw, 2 * kw)]
+        + [shape((rows, 2 * KEY), F32), shape((rows, VALUE), F32)],
+        [headed(KEY), headed(KEY), headed(VALUE), headed(2 * KEY)]
+        + [const_spec((rows, 2 * KEY)), const_spec((rows, VALUE))],
         [q, k, v, do, seg_row, logs, cos, sin] + list(weights),
         [
             headed(KEY),
@@ -698,8 +744,9 @@
             const_spec(cos.shape),
             const_spec(sin.shape),
         ]
-        + [pl.BlockSpec((1,) + part.shape[1:], lambda h: (h, 0, 0)) for part in weights],
+        + [pl.BlockSpec((1,) + part.shape[1:], lambda h, w: (h, 0, 0)) for part in weights],
         grid=(kw // KEY,),
+        scalars=where,
         scratch=[pltpu.VMEM((rows, KEY), F32), pltpu.VMEM((rows, KEY), F32), pltpu.VMEM((rows, VALUE), F32)],
     )
 
@@ -881,24 +928,6 @@
     return result if last else result[0]
 
 
-def half_kernel(where, source, out):
-    out[...] = source[...].astype(F32)
-
-
-def neighbour_half(line, where, source):
-    rows, columns = source.shape
-    part = rows // 2
-    return line.call(
-        half_kernel,
-        [shape((rows, columns // 2), F32)],
-        [pl.BlockSpec((part, columns // 2), lambda i, w: (i, 0))],
-        [source],
-        [pl.BlockSpec((part, columns // 2), lambda i, w: (i, 1 - w[0]))],
-        grid=(2,),
-        scalars=where,
-    )[0]
-
-
 def join_kernel(where, keep, got, *outs):
     mine, theirs = keep[...], got[...]
     low = where[0] == 0
@@ -980,7 +1009,7 @@
     plan = Plan(line)
     groups = dp // 2
     place = lax.axis_index("dp")
-    where = jnp.stack([lax.rem(place, 2), lax.div(place, 2)]).astype(jnp.int32)
+    where = jnp.stack([lax.rem(place, 2), lax.div(place, 2), my_core()]).astype(jnp.int32)
     tables = angle_tables(SEQ_LEN)
     logs = jnp.log1p(-jnp.exp2(-(decay_order + 5).astype(F32)))
     seg_row = segments.reshape(1, SEQ_LEN)
@@ -1002,10 +1031,11 @@
 
     def projected(n, begin, end):
         before = plan["P0"] if n else None
-        return projections(line, begin, end, inputs, gain1, bias1, tables, w_query, w_key, w_value, w_swish, before)
+        result = projections(line, begin, end, inputs, gain1, bias1, tables, w_query, w_key, w_value, w_swish, before)
+        return tuple(result[:7]) + (beside("H", result[7]) if n else result[7],)
 
     def retained(i):
-        a, q, k, v, switch, cos, sin = plan["P1" if i else "P0"]
+        a, q, k, v, switch = plan["P1" if i else "P0"][:5]
         before = plan[f"R{i - 1}"][1:3] if i else None
         chip, u, o, p = retention(line, i, q, k, v, switch, seg_row, logs, w_out, before)
         return (chip, across(f"R{i}", chip)), u, o, p
@@ -1022,8 +1052,7 @@
     for i in range(CHUNKS):
         plan.step(f"R{i}", ["P1", f"R{i - 1}"] if i else ["P0"], lambda i=i: retained(i))
         plan.step(f"F{i}", [f"R{i}"] + ([f"F{i - 1}"] if i else []), lambda i=i: fed(i))
-    plan.step("H", [], lambda: beside("H", core_half(line, inputs)))
-    plan.step("G", ["H"], lambda: partner_rows(line, plan["H"], gain1, bias1))
+    plan.step("G", ["P1"], lambda: partner_rows(line, plan["P1"][7], gain1, bias1))
 
     def first(n):
         return plan["P1"][n]
@@ -1041,38 +1070,38 @@
 
     def middle_back(i):
         before = plan["M1"] if i == 0 else None
-        return second_norm_back(line, i, rows, *plan[f"B{i}"], plan[f"F{last}"][4], gain2, cotangent, before)
+        return second_norm_back(line, 2 * i, *plan[f"B{i}"], plan[f"F{last}"][4], gain2, cotangent, before)
 
     def first_sum(i):
-        dq, dk, dv, _ = plan["AB"]
+        dq, dk, dv = plan["AB"][:3]
         return summed(f"C{i}", [dq, dk, dv, plan["GB"][1]], [w_query, w_key, w_value, w_swish], True, i)
 
     def inputs_back(i):
         before = plan["I1"] if i == 0 else None
-        return first_norm_back(line, i, rows, *plan[f"C{i}"], inputs, gain1, plan["M0"][1], before)
+        return first_norm_back(line, 2 * i, *plan[f"C{i}"], inputs, gain1, plan["M0"][1], before)
 
     def feed_sum():
         return summed("D", [plan[f"F{last}"][0]], [w_down], False, 0, SEQ_LEN)
 
-    def output_rows_all():
-        return output_rows(line, 0, SEQ_LEN, *plan["D"], plan[f"F{last}"][4], None)
-
     def retention_grads():
-        _, q, k, v, _, cos, sin = plan["P1"]
+        _, q, k, v, _, cos, sin = plan["P1"][:7]
         weights = [plan[f"R{i}"][3] for i in range(CHUNKS)]
-        return retention_back(line, q, k, v, plan["GB"][0], seg_row, logs, cos, sin, weights)
+        result = retention_back(line, where, q, k, v, plan["GB"][0], seg_row, logs, cos, sin, weights)
+        return result[:4] + (beside("Tq", result[4]), beside("Tv", result[5]))
+
+    def gate_grads():
+        result = gate_back(line, where, plan["M0"][0], w_out, plan[f"R{last}"][2], first(4))
+        return result[:2] + (beside("Ts", result[2]),)
 
     for i in reversed(pair):
-        after = [] if i else ["M1"]
         plan.step(f"B{i}", [f"F{last}"], lambda i=i: second_sum(i))
-        plan.step(f"M{i}", [f"B{i}"] + after, lambda i=i: middle_back(i))
-    plan.step("D", [f"F{last}"], feed_sum)
-    plan.step("O", ["D"], output_rows_all)
-    plan.step("GB", ["M0"], lambda: gate_back(line, plan["M0"][0], w_out, plan[f"R{last}"][2], first(4)))
-    plan.step("AB", ["GB"], retention_grads)
-    for i in reversed(pair):
+        plan.step(f"M{i}", [f"B{i}"] + ([] if i else ["M1"]), lambda i=i: middle_back(i))
         plan.step(f"C{i}", ["AB"], lambda i=i: first_sum(i))
         plan.step(f"I{i}", [f"C{i}", "M0"] + ([] if i else ["I1"]), lambda i=i: inputs_back(i))
+    plan.step("GB", ["M0"], gate_grads)
+    plan.step("AB", ["GB"], retention_grads)
+    plan.step("D", [f"F{last}"], feed_sum)
+    plan.step("O", ["D"], lambda: output_rows(line, *plan["D"], plan[f"F{last}"][4]))
     plan.step("CI", ["I0"], lambda: own_copy(line, plan["I0"][0]))
     plan.step("CO", ["O"], lambda: own_copy(line, plan["O"]))
 
@@ -1086,7 +1115,7 @@
         plan.sent["L"] = lax.ppermute(own, "tensor", [(i, i ^ 1) for i in range(tensor)])
         return own, plan.sent["L"]
 
-    plan.step("L", ["I0", "M0"], small_sums)
+    plan.step("L", ["I0", "I1", "M0", "M1"], small_sums)
 
 
     def products(name, needs, operands, by_rows, extra=tuple, skip=0):
@@ -1132,11 +1161,11 @@
         return lambda: plan[f"E{name}"]
 
 
-    def shares(name, needs, operand, count):
+    def shares(name, needs, operand, far, count):
         def ring(j):
             travelling = plan[f"J{name}{j - 1}"] if j else None
             right = operand()
-            pairs = [(first(0), right), (plan["G"], plan[f"T{name}"])]
+            pairs = [(first(0), right), (plan["G"], far())]
             block = wide_block(
                 line, where, pairs, groups, j, travelling, j == groups - 1, right.shape[1] // 2, True
             )
@@ -1144,9 +1173,8 @@
                 return onward(f"J{name}{j}", block)
             return block[1], beside(f"J{name}{j}", block[0])
 
-        plan.step(f"T{name}", needs, lambda: beside(f"T{name}", neighbour_half(line, where, operand())))
         for j in range(groups):
-            plan.step(f"J{name}{j}", [f"T{name}", "G"] + ([f"J{name}{j - 1}"] if j else []), lambda j=j: ring(j))
+            plan.step(f"J{name}{j}", ["G", f"J{name}{j - 1}"] if j else ["G", *needs], lambda j=j: ring(j))
         plan.step(f"E{name}", [f"J{name}{groups - 1}"], lambda: join_halves(line, where, *plan[f"J{name}{groups - 1}"], count))
         return lambda: plan[f"E{name}"]
 
@@ -1159,16 +1187,16 @@
     more_up = products("w", [f"F{last}"], lambda: (normed2(), fed_all(2)), True, skip=half_ff)
     out = products("o", ["M0", "L"], lambda: (plan[f"R{last}"][1], plan["M0"][0]), False, lambda: plan["L"])
     plan.step("U", ["Eu", f"Kw{groups - 1}"], lambda: side_by_side(line, up(), more_up()))
-    swish = shares("s", ["GB"], lambda: plan["GB"][1], 1)
-    vgrad = shares("v", ["AB"], lambda: plan["AB"][2], 1)
-    both = shares("q", ["AB"], lambda: plan["AB"][3], 2)
+    swish = shares("s", ["GB"], lambda: plan["GB"][1], lambda: plan["GB"][2], 1)
+    vgrad = shares("v", ["AB"], lambda: plan["AB"][2], lambda: plan["AB"][5], 1)
+    both = shares("q", ["AB"], lambda: plan["AB"][3], lambda: plan["AB"][4], 2)
 
     plan.run(
-        "P0", "R0", "P1", "R1", "H", "R2", "F0", "~R1", "R3", "F1", "F2", "F3", "B1", "SwA", "Ku0", "SgA", "SwB",
-        "B0", "Kw0", "Ku1", "G", "Kw1", "~B1", "SdA", "M1", "Ku2", "~Kw1", "Kg0", "M0", "GB", "Ts", "~Ku2", "Kd0",
-        "AB", "Kg1", "C1", "Kd1", "Tq", "Ku3", "~Kg1", "Tv", "Js0", "C0", "~Kd1", "Kw2", "I1", "Js1", "Kw3", "Jv0",
-        "Js2", "I0", "L", "SgB", "SoA", "Jq0", "Jv1", "D", "CI", "SdB", "Js3", "Jq1", "Jv2", "Ko0", "Jq2", "SoB",
-        "Eu", "Kg2", "Ko1", "Jv3", "O", "U", "CO", "Ko2", "Jq3", "Kd2", "Eq", "Kg3", "Ko3", "Es", "Ev", "Kd3",
+        "P0", "R0", "P1", "R1", "F0", "R2", "R3", "F1", "F2", "F3", "SgA", "Ku0", "B1", "SdA", "SwA", "Ku1", "B0",
+        "Kg0", "SgB", "G", "Ku2", "Kg1", "M1", "SwB", "Kd0", "~Ku2", "M0", "Kw0", "GB", "AB", "Kd1", "Kg2", "Kw1",
+        "C1", "Kg3", "Jq0", "~Kd1", "C0", "Jq1", "I1", "~Kw1", "Js0", "D", "Jq2", "Kw2", "I0", "Js1", "SoA", "Jq3",
+        "SdB", "SoB", "Jv0", "Js2", "Kw3", "Ku3", "Ko0", "Jv1", "Kd2", "Ko1", "Js3", "O", "Jv2", "Eu", "CO", "Ko2",
+        "U", "Jv3", "Eq", "Ko3", "Ev", "Es", "CI", "Kd3",
     )
     plan.run(*plan.steps)
     query, key = both()

time: 696 us -> 685 us (0.984)
  Pallas kernels: 506 us -> 469 us
  waiting for transfers between devices: 115 us -> 150 us
    ppermute x16, waiting for transfers between devices: 25.8 us -> 65.8 us  [beside(): lax.ppermute(values, 'dp', [(i, i ^ 1) for i in range(dp)])]
    pallas_call x74 -> x70, Pallas kernels: 506 us -> 469 us  [call(): pl.pallas_call(body, out_shape=tuple(outs), grid_spec=pltpu.PrefetchScala...]
    ppermute x24, waiting for transfers between devices: 86.5 us -> 66.9 us  [onward(): lax.ppermute(values, 'dp', [(i, (i + 2) % dp) for i in range(dp)])]
    ppermute x9, waiting for transfers between devices: 2.89 us -> 17.8 us  [across(): lax.ppermute(values, 'tensor', [(i, i ^ 2) for i in range(tensor)])]
  transfers between devices with their start and end apart: 50 -> 50, of which waited for: 17 -> 23; matrix products, arithmetic and copies ran while one was open for 0% -> 0% of each run, Pallas kernels for 70% -> 66%
where the time goes in v4:
time: 685 us; the launch traced here: 676 us
  Pallas kernels  469 us (68%)
  waiting for transfers between devices  150 us (22%)
  starting transfers between devices  47.2 us (7%)
    pallas_call x70, Pallas kernels, call(): pl.pallas_call(body, out_shape=tuple(outs), grid_spec=pltpu.PrefetchScala...  469 us
    ppermute x24, waiting for transfers between devices, onward(): lax.ppermute(values, 'dp', [(i, (i + 2) % dp) for i in range(dp)])  66.9 us
    ppermute x16, waiting for transfers between devices, beside(): lax.ppermute(values, 'dp', [(i, i ^ 1) for i in range(dp)])  65.8 us
    ppermute x24, starting transfers between devices, onward(): lax.ppermute(values, 'dp', [(i, (i + 2) % dp) for i in range(dp)])  23.2 us
    ppermute x9, waiting for transfers between devices, across(): lax.ppermute(values, 'tensor', [(i, i ^ 2) for i in range(tensor)])  17.8 us
    ppermute x16, starting transfers between devices, beside(): lax.ppermute(values, 'dp', [(i, i ^ 1) for i in range(dp)])  14.2 us
  transfers between devices with their start and end apart: 50, of which 23 were waited for; matrix products, arithmetic and copies ran while one was open for 0% of the time, Pallas kernels for 66%

profile of v4, /device:TPU:0, one launch (start us, length us, event | category | flops | bytes accessed | tf_op | source)
XLA Modules:
  0.0 675.9 jit_solution(13262153233327759355)
XLA Ops:
  4.4 8.5 %shard_map.263 = (bf16[1024,2048]{1,0:T(8,128)(2,1)}, bf16[1024,512]{1,0:T(8,128)(2,1)}, bf16[1024,512]{1,0:T(8,128)(2,1)}, bf16[1024,1024]{1,0:T(8,128)(2,1)}, ...) custom-call(bf16[1024,2048]{1,0:T(8,128)(2,1)} %refs_2_.26, ...), custom_call_target="tpu_custom_call" | custom-call | flops 1 | bytes 1 | tf_op jit(solution)/shard_map/pallas_call | solution.py:108
  12.9 8.8 %shard_map.264 = (f32[128,2048]{1,0:T(8,128)}, bf16[1024,1024]{1,0:T(8,128)(2,1)}, f32[1024,1024]{1,0:T(8,128)}, bf16[2,256,256]{2,1,0:T(8,128)(2,1)}) custom-call(bf16[1024,512]{1,0:T(8,128)(2,1)} %get-tuple-element.102.refs_0_.refs_12_, bf16[1024,512]{1,0:T(8,128)(2,1)} %get-tuple-element.103.refs_1_.refs_13_, ...), custom_call_target="tpu_custom_call" | custom-call | flops 1 | bytes 1 | tf_op jit(solution)/shard_map/pallas_call | solution.py:108
  24.5 19.2 %shard_map.265 = (bf16[1024,2048]{1,0:T(8,128)(2,1)}, bf16[1024,512]{1,0:T(8,128)(2,1)}, bf16[1024,512]{1,0:T(8,128)(2,1)}, bf16[1024,1024]{1,0:T(8,128)(2,1)}, ...) custom-call(bf16[1024,2048]{1,0:T(8,128)(2,1)} %refs_2_.26, ...), custom_call_target="tpu_custom_call", output_to_operand_aliasing={{0}: (11, {}), {1}: (12, {}), {2}: (13, {}), {3}: (14, {}),... | custom-call | flops 1 | bytes 1 | tf_op jit(solution)/shard_map/pallas_call | solution.py:108
  45.3 8.8 %shard_map.266 = (f32[128,2048]{1,0:T(8,128)}, bf16[1024,1024]{1,0:T(8,128)(2,1)}, f32[1024,1024]{1,0:T(8,128)}, bf16[2,256,512]{2,1,0:T(8,128)(2,1)}) custom-call(bf16[1024,512]{1,0:T(8,128)(2,1)} %get-tuple-element.110.refs_0_.refs_1_, bf16[1024,512]{1,0:T(8,128)(2,1)} %get-tuple-element.111.refs_1_.refs_2_, ...), custom_call_target="tpu_custom_call", output_to_operand_aliasing={{1}: (7, {}), {2}: (8, {})} | custom-call | flops 1 | bytes 1 | tf_op jit(solution)/shard_map/pallas_call | solution.py:108
  54.6 10.7 %shard_map.267 = (bf16[1024,1024]{1,0:T(8,128)(2,1)}, bf16[1024,1024]{1,0:T(8,128)(2,1)}, bf16[1024,1024]{1,0:T(8,128)(2,1)}, bf16[1024,2048]{1,0:T(8,128)(2,1)}, f32[512,2048]{1,0:T(8,128)}) custom-call(f32[128,2048]{1,0:T(8,128)} %get-tuple-element.109.refs_19_.refs_0_, f32[128,2048]{1,0:T(8,128)} %collective-permute-done.refs_1_, ...), custom_call_target="tpu_custom_call" | custom-call | flops 1 | bytes 1 | tf_op jit(solution)/shard_map/pallas_call | solution.py:108
  65.3 9.3 %shard_map.268 = (f32[128,2048]{1,0:T(8,128)}, bf16[1024,1024]{1,0:T(8,128)(2,1)}, f32[1024,1024]{1,0:T(8,128)}, bf16[2,256,768]{2,1,0:T(8,128)(2,1)}) custom-call(bf16[1024,512]{1,0:T(8,128)(2,1)} %get-tuple-element.110.refs_0_.refs_1_, bf16[1024,512]{1,0:T(8,128)(2,1)} %get-tuple-element.111.refs_1_.refs_2_, ...), custom_call_target="tpu_custom_call", output_to_operand_aliasing={{1}: (7, {}), {2}: (8, {})} | custom-call | flops 1 | bytes 1 | tf_op jit(solution)/shard_map/pallas_call | solution.py:108
  76.2 9.6 %shard_map.269 = (f32[128,2048]{1,0:T(8,128)}, bf16[1024,1024]{1,0:T(8,128)(2,1)}, f32[1024,1024]{1,0:T(8,128)}, bf16[2,256,768]{2,1,0:T(8,128)(2,1)}) custom-call(bf16[1024,512]{1,0:T(8,128)(2,1)} %get-tuple-element.110.refs_0_.refs_1_, bf16[1024,512]{1,0:T(8,128)(2,1)} %get-tuple-element.111.refs_1_.refs_2_, ...), custom_call_target="tpu_custom_call", output_to_operand_aliasing={{1}: (7, {}), {2}: (8, {})} | custom-call | flops 1 | bytes 1 | tf_op jit(solution)/shard_map/pallas_call | solution.py:108
  87.1 10.7 %shard_map.270 = (bf16[1024,1024]{1,0:T(8,128)(2,1)}, bf16[1024,1024]{1,0:T(8,128)(2,1)}, bf16[1024,1024]{1,0:T(8,128)(2,1)}, bf16[1024,2048]{1,0:T(8,128)(2,1)}, f32[512,2048]{1,0:T(8,128)}) custom-call(f32[128,2048]{1,0:T(8,128)} %get-tuple-element.119.refs_9_.refs_0_, ...), custom_call_target="tpu_custom_call", output_to_operand_aliasing={{0}: (9, {}), {1}: (10, {}), {2}: (11, {}), {3}: (12, {}), ... | custom-call | flops 1 | bytes 1 | tf_op jit(solution)/shard_map/pallas_call | solution.py:108
  102.9 10.7 %shard_map.271 = (bf16[1024,1024]{1,0:T(8,128)(2,1)}, bf16[1024,1024]{1,0:T(8,128)(2,1)}, bf16[1024,1024]{1,0:T(8,128)(2,1)}, bf16[1024,2048]{1,0:T(8,128)(2,1)}, f32[512,2048]{1,0:T(8,128)}) custom-call(f32[128,2048]{1,0:T(8,128)} %get-tuple-element.123.refs_9_.refs_0_, ...), custom_call_target="tpu_custom_call", output_to_operand_aliasing={{0}: (9, {}), {1}: (10, {}), {2}: (11, {}), {3}: (12, {}), ... | custom-call | flops 1 | bytes 1 | tf_op jit(solution)/shard_map/pallas_call | solution.py:108
  113.6 11.2 %collective-permute-done.1.refs_1_ = f32[128,2048]{1,0:T(8,128)} collective-permute-done((f32[128,2048]{1,0:T(8,128)}, f32[128,2048]{1,0:T(8,128)}, u32[]{:S(2)}, u32[]{:S(2)}) %collective-permute-start.1) | collective-permute-done | bytes 1048608 | tf_op jit(solution)/shard_map/ppermute | solution.py:1028
  124.8 10.9 %shard_map.272 = (bf16[1024,1024]{1,0:T(8,128)(2,1)}, bf16[1024,1024]{1,0:T(8,128)(2,1)}, bf16[1024,1024]{1,0:T(8,128)(2,1)}, bf16[1024,2048]{1,0:T(8,128)(2,1)}, f32[512,2048]{1,0:T(8,128)}) custom-call(f32[128,2048]{1,0:T(8,128)} %get-tuple-element.124.refs_14_.refs_0_, ...), custom_call_target="tpu_custom_call", output_to_operand_aliasing={{0}: (9, {}), {1}: (10, {}), {2}: (11, {}), {3}: (12, {}), ... | custom-call | flops 1 | bytes 1 | tf_op jit(solution)/shard_map/pallas_call | solution.py:108
  146.7 11.2 %shard_map.275.refs_3_.refs_0_ = f32[256,2048]{1,0:T(8,128)} custom-call(bf16[1024,1024]{1,0:T(8,128)(2,1)} %get-tuple-element.140.refs_2_.refs_0_, bf16[1024,1024]{1,0:T(8,128)(2,1)} %get-tuple-element.141.refs_2_.refs_1_, bf16[2048,1024]{1,0:T(8,128)(2,1)} %refs_2_.21, bf16[2048,1024]{1,0:T(8,128)(2,1)} %refs_3_.3, f32[512,512]{1,0:T(8,128)} %shard_map.274.refs_4_), custom_call_target="tpu_custom_call" | custom-call | flops 1 | bytes 1 | tf_op jit(solution)/shard_map/pallas_call | solution.py:108
  175.6 11.1 %shard_map.279.refs_4_.refs_0_ = f32[256,2048]{1,0:T(8,128)} custom-call(bf16[1024,1024]{1,0:T(8,128)(2,1)} %get-tuple-element.140.refs_2_.refs_0_, bf16[1024,1024]{1,0:T(8,128)(2,1)} %get-tuple-element.141.refs_2_.refs_1_, bf16[2048,1024]{1,0:T(8,128)(2,1)} %refs_2_.21, bf16[2048,1024]{1,0:T(8,128)(2,1)} %refs_3_.3, f32[512,512]{1,0:T(8,128)} %shard_map.278.refs_4_), custom_call_target="tpu_custom_call" | custom-call | flops 1 | bytes 1 | tf_op jit(solution)/shard_map/pallas_call | solution.py:108
  200.6 10.0 %shard_map.282.refs_4_.refs_3_ = bf16[1024,2048]{1,0:T(8,128)(2,1)} custom-call(f32[512,2048]{1,0:T(8,128)} %collective-permute-done.10.refs_0_, f32[1,2048]{1,0:T(1,128)} %bitcast.19, f32[1,2048]{1,0:T(1,128)} %bitcast.28, f32[2,256,1024]{2,1,0:T(8,128)} %shard_map.281.refs_3_), custom_call_target="tpu_custom_call" | custom-call | flops 1 | bytes 1 | tf_op jit(solution)/shard_map/pallas_call | solution.py:108
  216.8 9.5 %collective-permute-done.8.refs_4_ = f32[256,1024]{1,0:T(8,128)} collective-permute-done((f32[256,1024]{1,0:T(8,128)}, f32[256,1024]{1,0:T(8,128)}, u32[]{:S(2)}, u32[]{:S(2)}) %collective-permute-start.8) | collective-permute-done | bytes 1048608 | tf_op jit(solution)/shard_map/ppermute | solution.py:1024
  232.1 9.2 %shard_map.285 = (bf16[1024,2048]{1,0:T(8,128)(2,1)}, f32[512,2048]{1,0:T(8,128)}, f32[1,2048]{1,0:T(1,128)}, f32[1,2048]{1,0:T(1,128)}) custom-call(f32[256,2048]{1,0:T(8,128)} %shard_map.275.refs_3_.refs_0_, f32[256,2048]{1,0:T(8,128)} %collective-permute-done.6.refs_1_, f32[512,2048]{1,0:T(8,128)} %get-tuple-element.143.refs_2_, f32[1,2048]{1,0:T(1,128)} %bitcast.15, ...), custom_call_target="tpu_custom_call" | custom-call | flops 1 | bytes 1 | tf_op jit(solution)/shard_map/pallas_call | solution.py:108
  251.1 9.3 %shard_map.288 = (bf16[1024,2048]{1,0:T(8,128)(2,1)}, f32[512,2048]{1,0:T(8,128)}, f32[1,2048]{1,0:T(1,128)}, f32[1,2048]{1,0:T(1,128)}) custom-call(f32[256,2048]{1,0:T(8,128)} %shard_map.279.refs_4_.refs_0_, f32[256,2048]{1,0:T(8,128)} %collective-permute-done.5.refs_1_, ...), custom_call_target="tpu_custom_call", output_to_operand_aliasing={{0}: (5, {}), {1}: (6, {})} | custom-call | flops 1 | bytes 1 | tf_op jit(solution)/shard_map/pallas_call | solution.py:108
  263.8 14.3 %shard_map.290 = (bf16[1024,1024]{1,0:T(8,128)(2,1)}, bf16[1024,1024]{1,0:T(8,128)(2,1)}, f32[1024,512]{1,0:T(8,128)}) custom-call(s32[3]{0:T(128)} %pad_add_fusion.refs_0_, bf16[1024,2048]{1,0:T(8,128)(2,1)} %get-tuple-element.147.refs_4_.refs_1_.refs_2_, bf16[1024,2048]{1,0:T(8,128)(2,1)} %refs_2_.23, f32[1024,1024]{1,0:T(8,128)} %get-tuple-element.148.refs_3_, ...), custom_call_target="tpu_custom_call" | custom-call | flops 1 | bytes 1 | tf_op jit(solution)/shard_map/pallas_call | solution.py:108
  278.1 14.7 %shard_map.291 = (bf16[1024,512]{1,0:T(8,128)(2,1)}, bf16[1024,512]{1,0:T(8,128)(2,1)}, bf16[1024,1024]{1,0:T(8,128)(2,1)}, bf16[1024,1024]{1,0:T(8,128)(2,1)}, ...) custom-call(s32[3]{0:T(128)} %pad_add_fusion.refs_0_, bf16[1024,512]{1,0:T(8,128)(2,1)} %get-tuple-element.110.refs_0_.refs_1_, ...), custom_call_target="tpu_custom_call" | custom-call | flops 1 | bytes 1 | tf_op jit(solution)/shard_map/pallas_call | solution.py:108
  314.6 13.8 %shard_map.295.refs_5_.refs_0_ = f32[256,2048]{1,0:T(8,128)} custom-call(bf16[1024,512]{1,0:T(8,128)(2,1)} %get-tuple-element.158.refs_5_.refs_0_, bf16[1024,512]{1,0:T(8,128)(2,1)} %get-tuple-element.159.refs_1_, bf16[1024,1024]{1,0:T(8,128)(2,1)} %get-tuple-element.160.refs_2_, bf16[1024,1024]{1,0:T(8,128)(2,1)} %get-tuple-element.149.refs_3_.refs_2_, ...), custom_call_target="tpu_custom_call" | custom-call | flops 1 | bytes 1 | tf_op jit(solution)/shard_map/pallas_call | solution.py:108
  336.8 10.0 %collective-permute-done.20.refs_4_ = f32[1024,512]{1,0:T(8,128)} collective-permute-done((f32[1024,512]{1,0:T(8,128)}, f32[1024,512]{1,0:T(8,128)}, u32[]{:S(2)}, u32[]{:S(2)}) %collective-permute-start.20) | collective-permute-done | bytes 2097184 | tf_op jit(solution)/shard_map/ppermute | solution.py:1020
  357.1 13.8 %shard_map.298.refs_6_.refs_0_ = f32[256,2048]{1,0:T(8,128)} custom-call(bf16[1024,512]{1,0:T(8,128)(2,1)} %get-tuple-element.158.refs_5_.refs_0_, bf16[1024,512]{1,0:T(8,128)(2,1)} %get-tuple-element.159.refs_1_, bf16[1024,1024]{1,0:T(8,128)(2,1)} %get-tuple-element.160.refs_2_, bf16[1024,1024]{1,0:T(8,128)(2,1)} %get-tuple-element.149.refs_3_.refs_2_, ...), custom_call_target="tpu_custom_call" | custom-call | flops 1 | bytes 1 | tf_op jit(solution)/shard_map/pallas_call | solution.py:108
  372.5 7.3 %collective-permute-done.22.refs_5_ = f32[512,512]{1,0:T(8,128)} collective-permute-done((f32[512,512]{1,0:T(8,128)}, f32[512,512]{1,0:T(8,128)}, u32[]{:S(2)}, u32[]{:S(2)}) %collective-permute-start.22) | collective-permute-done | bytes 1048608 | tf_op jit(solution)/shard_map/ppermute | solution.py:1024
  385.9 9.1 %shard_map.300 = (f32[1024,2048]{1,0:T(8,128)}, f32[1,2048]{1,0:T(1,128)}, f32[1,2048]{1,0:T(1,128)}) custom-call(f32[256,2048]{1,0:T(8,128)} %shard_map.295.refs_5_.refs_0_, f32[256,2048]{1,0:T(8,128)} %collective-permute-done.19.refs_1_, bf16[1024,2048]{1,0:T(8,128)(2,1)} %refs_2_.26, f32[1,2048]{1,0:T(1,128)} %bitcast.20, ...), custom_call_target="tpu_custom_call" | custom-call | flops 1 | bytes 1 | tf_op jit(solution)/shard_map/pallas_call | solution.py:108
  404.0 12.7 %shard_map.302.refs_6_.refs_0_ = f32[512,2048]{1,0:T(8,128)} custom-call(bf16[1024,1024]{1,0:T(8,128)(2,1)} %get-tuple-element.139.refs_3_.refs_1_.refs_0_, bf16[1024,2048]{1,0:T(8,128)(2,1)} %refs_1_.1, f32[512,512]{1,0:T(8,128)} %shard_map.301.refs_2_), custom_call_target="tpu_custom_call" | custom-call | flops 1 | bytes 1 | tf_op jit(solution)/shard_map/pallas_call | solution.py:108
  416.8 5.7 shard_map.303.refs_5_
  428.1 9.3 %shard_map.305 = (f32[1024,2048]{1,0:T(8,128)}, f32[1,2048]{1,0:T(1,128)}, f32[1,2048]{1,0:T(1,128)}) custom-call(f32[256,2048]{1,0:T(8,128)} %shard_map.298.refs_6_.refs_0_, f32[256,2048]{1,0:T(8,128)} %collective-permute-done.27.refs_1_, bf16[1024,2048]{1,0:T(8,128)(2,1)} %refs_2_.26, f32[1,2048]{1,0:T(1,128)} %bitcast.21, ...), custom_call_target="tpu_custom_call", output_to_operand_aliasing={{0}: (5, {})} | custom-call | flops 1 | bytes 1 | tf_op jit(solution)/shard_map/pallas_call | solution.py:108
  519.7 29.8 %collective-permute-done.38.refs_3_ = f32[2,1024,256]{2,1,0:T(8,128)} collective-permute-done((f32[2,1024,256]{2,1,0:T(8,128)}, f32[2,1024,256]{2,1,0:T(8,128)}, u32[]{:S(2)}, u32[]{:S(2)}) %collective-permute-start.38) | collective-permute-done | bytes 2097184 | tf_op jit(solution)/shard_map/ppermute | solution.py:1020
  568.1 10.7 %shard_map.320.refs_6_.refs_0_ = bf16[1024,2048]{1,0:T(8,128)(2,1)} custom-call(f32[512,2048]{1,0:T(8,128)} %shard_map.302.refs_6_.refs_0_, f32[512,2048]{1,0:T(8,128)} %collective-permute-done.25.refs_1_, f32[512,2048]{1,0:T(8,128)} %get-tuple-element.143.refs_2_, f32[256,512]{1,0:T(8,128)} %get-tuple-element.178.refs_3_), custom_call_target="tpu_custom_call" | custom-call | flops 1 | bytes 1 | tf_op jit(solution)/shard_map/pallas_call | solution.py:108
  588.0 16.4 %collective-permute-done.40.refs_0_ = f32[256,512]{1,0:T(8,128)} collective-permute-done((f32[256,512]{1,0:T(8,128)S(1)}, f32[256,512]{1,0:T(8,128)}, u32[]{:S(2)}, u32[]{:S(2)}) %collective-permute-start.40) | collective-permute-done | bytes 524320 | tf_op jit(solution)/shard_map/ppermute | solution.py:1020
  637.9 12.1 %collective-permute-done.47.refs_6_ = f32[1032,256]{1,0:T(8,128)} collective-permute-done((f32[1032,256]{1,0:T(8,128)}, f32[1032,256]{1,0:T(8,128)}, u32[]{:S(2)}, u32[]{:S(2)}) %collective-permute-start.47) | collective-permute-done | bytes 1056800 | tf_op jit(solution)/shard_map/ppermute | solution.py:1024
  660.6 7.1 %shard_map.331.refs_5_ = f32[1024,2048]{1,0:T(8,128)} custom-call(f32[1024,2048]{1,0:T(8,128)} %get-tuple-element.165.refs_6_.refs_0_, f32[256,1024]{1,0:T(8,128)} %shard_map.330.refs_1_), custom_call_target="tpu_custom_call" | custom-call | flops 1 | bytes 1 | tf_op jit(solution)/shard_map/pallas_call | solution.py:108
  (180 shorter events, 308.7 us)
Async XLA Ops:
  43.7 150.3 %collective-permute-start.10 = (f32[512,2048]{1,0:T(8,128)}, f32[512,2048]{1,0:T(8,128)}, u32[]{:S(2)}, u32[]{:S(2)}) collective-permute-start(f32[512,2048]{1,0:T(8,128)} %get-tuple-element.144), channel_id=1, source_target_pairs={{0,4},{4,0},{8,12},{12,8},{16,20},{20,16},{24,28},{28,24},{1,5},{5... | collective-permute-start | bytes 12582920 | tf_op jit(solution)/shard_map/ppermute | solution.py:1020
  85.9 38.9 %collective-permute-start.1 = (f32[128,2048]{1,0:T(8,128)}, f32[128,2048]{1,0:T(8,128)}, u32[]{:S(2)}, u32[]{:S(2)}) collective-permute-start(f32[128,2048]{1,0:T(8,128)} %get-tuple-element.124.refs_14_.refs_0_), channel_id=1, source_target_pairs={{0,2},{1,3},{2,0},{3,1},{4,6},{5,7},{6,4},{7,5},{8,10},{9,11},{10,... | collective-permute-start | bytes 3145736 | tf_op jit(solution)/shard_map/ppermute | solution.py:1028
  140.7 48.9 %collective-permute-start.7 = (f32[2,256,1024]{2,1,0:T(8,128)}, f32[2,256,1024]{2,1,0:T(8,128)}, u32[]{:S(2)}, u32[]{:S(2)}) collective-permute-start(f32[2,256,1024]{2,1,0:T(8,128)} %shard_map.273.refs_3_), channel_id=1, source_target_pairs={{0,4},{4,0},{8,12},{12,8},{16,20},{20,16},{24,28},{28,24},{1,5},{5... | collective-permute-start | bytes 6291464 | tf_op jit(solution)/shard_map/ppermute | solution.py:1020
  157.8 58.4 %collective-permute-start.6 = (f32[256,2048]{1,0:T(8,128)}, f32[256,2048]{1,0:T(8,128)}, u32[]{:S(2)}, u32[]{:S(2)}) collective-permute-start(f32[256,2048]{1,0:T(8,128)} %shard_map.275.refs_3_.refs_0_), channel_id=1, source_target_pairs={{0,2},{1,3},{2,0},{3,1},{4,6},{5,7},{6,4},{7,5},{8,10},{9,11},{10,... | collective-permute-start | bytes 6291464 | tf_op jit(solution)/shard_map/ppermute | solution.py:1028
  167.3 77.9 %collective-permute-start.11 = (f32[2,1024,256]{2,1,0:T(8,128)}, f32[2,1024,256]{2,1,0:T(8,128)}, u32[]{:S(2)}, u32[]{:S(2)}) collective-permute-start(f32[2,1024,256]{2,1,0:T(8,128)} %shard_map.276.refs_3_), channel_id=1, source_target_pairs={{0,4},{4,0},{8,12},{12,8},{16,20},{20,16},{24,28},{28,24},{1,5},{5... | collective-permute-start | bytes 6291464 | tf_op jit(solution)/shard_map/ppermute | solution.py:1020
  175.6 35.0 %collective-permute-start.9 = (f32[512,512]{1,0:T(8,128)}, f32[512,512]{1,0:T(8,128)}, u32[]{:S(2)}, u32[]{:S(2)}) collective-permute-start(f32[512,512]{1,0:T(8,128)} %shard_map.278.refs_4_), channel_id=1, source_target_pairs={{0,8},{4,12},{8,16},{12,20},{16,24},{20,28},{24,0},{28,4},{1,9},{5... | collective-permute-start | bytes 3145736 | tf_op jit(solution)/shard_map/ppermute | solution.py:1024
  189.5 61.5 %collective-permute-start.5 = (f32[256,2048]{1,0:T(8,128)}, f32[256,2048]{1,0:T(8,128)}, u32[]{:S(2)}, u32[]{:S(2)}) collective-permute-start(f32[256,2048]{1,0:T(8,128)} %shard_map.279.refs_4_.refs_0_), channel_id=1, source_target_pairs={{0,2},{1,3},{2,0},{3,1},{4,6},{5,7},{6,4},{7,5},{8,10},{9,11},{10,... | collective-permute-start | bytes 6291464 | tf_op jit(solution)/shard_map/ppermute | solution.py:1028
  214.6 35.0 %collective-permute-start.12 = (f32[512,512]{1,0:T(8,128)}, f32[512,512]{1,0:T(8,128)}, u32[]{:S(2)}, u32[]{:S(2)}) collective-permute-start(f32[512,512]{1,0:T(8,128)} %shard_map.283.refs_5_), channel_id=1, source_target_pairs={{0,8},{4,12},{8,16},{12,20},{16,24},{20,28},{24,0},{28,4},{1,9},{5... | collective-permute-start | bytes 3145736 | tf_op jit(solution)/shard_map/ppermute | solution.py:1024
  216.2 44.1 %collective-permute-start.13 = (f32[2,256,512]{2,1,0:T(8,128)}, f32[2,256,512]{2,1,0:T(8,128)}, u32[]{:S(2)}, u32[]{:S(2)}) collective-permute-start(f32[2,256,512]{2,1,0:T(8,128)} %shard_map.277.refs_4_), channel_id=1, source_target_pairs={{0,4},{4,0},{8,12},{12,8},{16,20},{20,16},{24,28},{28,24},{1,5},{5... | collective-permute-start | bytes 3145736 | tf_op jit(solution)/shard_map/ppermute | solution.py:1020
  226.3 75.6 %collective-permute-start.16 = (f32[2,256,1024]{2,1,0:T(8,128)}, f32[2,256,1024]{2,1,0:T(8,128)}, u32[]{:S(2)}, u32[]{:S(2)}) collective-permute-start(f32[2,256,1024]{2,1,0:T(8,128)} %shard_map.281.refs_3_), channel_id=1, source_target_pairs={{0,4},{4,0},{8,12},{12,8},{16,20},{20,16},{24,28},{28,24},{1,5},{5... | collective-permute-start | bytes 6291464 | tf_op jit(solution)/shard_map/ppermute | solution.py:1020
  245.2 56.7 %collective-permute-start.17 = (f32[256,1024]{1,0:T(8,128)}, f32[256,1024]{1,0:T(8,128)}, u32[]{:S(2)}, u32[]{:S(2)}) collective-permute-start(f32[256,1024]{1,0:T(8,128)} %shard_map.284.refs_5_), channel_id=1, source_target_pairs={{0,8},{4,12},{8,16},{12,20},{16,24},{20,28},{24,0},{28,4},{1,9},{5... | collective-permute-start | bytes 3145736 | tf_op jit(solution)/shard_map/ppermute | solution.py:1024
  249.6 46.3 %collective-permute-start.18 = (f32[1024,256]{1,0:T(8,128)}, f32[1024,256]{1,0:T(8,128)}, u32[]{:S(2)}, u32[]{:S(2)}) collective-permute-start(f32[1024,256]{1,0:T(8,128)} %shard_map.287.refs_7_), channel_id=1, source_target_pairs={{0,8},{4,12},{8,16},{12,20},{16,24},{20,28},{24,0},{28,4},{1,9},{5... | collective-permute-start | bytes 3145736 | tf_op jit(solution)/shard_map/ppermute | solution.py:1024
  292.8 54.0 %collective-permute-start.20 = (f32[1024,512]{1,0:T(8,128)}, f32[1024,512]{1,0:T(8,128)}, u32[]{:S(2)}, u32[]{:S(2)}) collective-permute-start(f32[1024,512]{1,0:T(8,128)} %get-tuple-element.163), channel_id=1, source_target_pairs={{0,4},{4,0},{8,12},{12,8},{16,20},{20,16},{24,28},{28,24},{1,5},{5... | collective-permute-start | bytes 6291464 | tf_op jit(solution)/shard_map/ppermute | solution.py:1020
  328.4 57.0 %collective-permute-start.19 = (f32[256,2048]{1,0:T(8,128)}, f32[256,2048]{1,0:T(8,128)}, u32[]{:S(2)}, u32[]{:S(2)}) collective-permute-start(f32[256,2048]{1,0:T(8,128)} %shard_map.295.refs_5_.refs_0_), channel_id=1, source_target_pairs={{0,2},{1,3},{2,0},{3,1},{4,6},{5,7},{6,4},{7,5},{8,10},{9,11},{10,... | collective-permute-start | bytes 6291464 | tf_op jit(solution)/shard_map/ppermute | solution.py:1028
  329.0 66.1 %collective-permute-start.14 = (f32[1024,512]{1,0:T(8,128)}, f32[1024,512]{1,0:T(8,128)}, u32[]{:S(2)}, u32[]{:S(2)}) collective-permute-start(f32[1024,512]{1,0:T(8,128)} %get-tuple-element.150), channel_id=1, source_target_pairs={{0,4},{4,0},{8,12},{12,8},{16,20},{20,16},{24,28},{28,24},{1,5},{5... | collective-permute-start | bytes 6291464 | tf_op jit(solution)/shard_map/ppermute | solution.py:1020
  370.9 57.1 %collective-permute-start.27 = (f32[256,2048]{1,0:T(8,128)}, f32[256,2048]{1,0:T(8,128)}, u32[]{:S(2)}, u32[]{:S(2)}) collective-permute-start(f32[256,2048]{1,0:T(8,128)} %shard_map.298.refs_6_.refs_0_), channel_id=1, source_target_pairs={{0,2},{1,3},{2,0},{3,1},{4,6},{5,7},{6,4},{7,5},{8,10},{9,11},{10,... | collective-permute-start | bytes 6291464 | tf_op jit(solution)/shard_map/ppermute | solution.py:1028
  385.4 38.1 %collective-permute-start.28 = (f32[2,256,512]{2,1,0:T(8,128)}, f32[2,256,512]{2,1,0:T(8,128)}, u32[]{:S(2)}, u32[]{:S(2)}) collective-permute-start(f32[2,256,512]{2,1,0:T(8,128)} %shard_map.286.refs_4_), channel_id=1, source_target_pairs={{0,4},{4,0},{8,12},{12,8},{16,20},{20,16},{24,28},{28,24},{1,5},{5... | collective-permute-start | bytes 3145736 | tf_op jit(solution)/shard_map/ppermute | solution.py:1020
  400.9 38.3 %collective-permute-start.26 = (f32[512,512]{1,0:T(8,128)}, f32[512,512]{1,0:T(8,128)}, u32[]{:S(2)}, u32[]{:S(2)}) collective-permute-start(f32[512,512]{1,0:T(8,128)} %shard_map.301.refs_2_), channel_id=1, source_target_pairs={{0,8},{4,12},{8,16},{12,20},{16,24},{20,28},{24,0},{28,4},{1,9},{5... | collective-permute-start | bytes 3145736 | tf_op jit(solution)/shard_map/ppermute | solution.py:1024
  402.5 66.2 %collective-permute-start.31 = (f32[1024,512]{1,0:T(8,128)}, f32[1024,512]{1,0:T(8,128)}, u32[]{:S(2)}, u32[]{:S(2)}) collective-permute-start(f32[1024,512]{1,0:T(8,128)} %get-tuple-element.166), channel_id=1, source_target_pairs={{0,4},{4,0},{8,12},{12,8},{16,20},{20,16},{24,28},{28,24},{1,5},{5... | collective-permute-start | bytes 6291464 | tf_op jit(solution)/shard_map/ppermute | solution.py:1020
  422.5 35.4 %collective-permute-start.33 = (f32[512,512]{1,0:T(8,128)}, f32[512,512]{1,0:T(8,128)}, u32[]{:S(2)}, u32[]{:S(2)}) collective-permute-start(f32[512,512]{1,0:T(8,128)} %shard_map.303.refs_5_), channel_id=1, source_target_pairs={{0,8},{4,12},{8,16},{12,20},{16,24},{20,28},{24,0},{28,4},{1,9},{5... | collective-permute-start | bytes 3145736 | tf_op jit(solution)/shard_map/ppermute | solution.py:1024
  423.5 144.6 %collective-permute-start.25 = (f32[512,2048]{1,0:T(8,128)}, f32[512,2048]{1,0:T(8,128)}, u32[]{:S(2)}, u32[]{:S(2)}) collective-permute-start(f32[512,2048]{1,0:T(8,128)} %shard_map.302.refs_6_.refs_0_), channel_id=1, source_target_pairs={{0,2},{1,3},{2,0},{3,1},{4,6},{5,7},{6,4},{7,5},{8,10},{9,11},{10,... | collective-permute-start | bytes 12582920 | tf_op jit(solution)/shard_map/ppermute | solution.py:1028
  450.5 54.0 %collective-permute-start.35 = (f32[2,1032,256]{2,1,0:T(8,128)}, f32[2,1032,256]{2,1,0:T(8,128)}, u32[]{:S(2)}, u32[]{:S(2)}) collective-permute-start(f32[2,1032,256]{2,1,0:T(8,128)} %shard_map.307.refs_6_), channel_id=1, source_target_pairs={{0,4},{4,0},{8,12},{12,8},{16,20},{20,16},{24,28},{28,24},{1,5},{5... | collective-permute-start | bytes 6340616 | tf_op jit(solution)/shard_map/ppermute | solution.py:1020
  468.8 80.7 %collective-permute-start.38 = (f32[2,1024,256]{2,1,0:T(8,128)}, f32[2,1024,256]{2,1,0:T(8,128)}, u32[]{:S(2)}, u32[]{:S(2)}) collective-permute-start(f32[2,1024,256]{2,1,0:T(8,128)} %shard_map.309.refs_5_), channel_id=1, source_target_pairs={{0,4},{4,0},{8,12},{12,8},{16,20},{20,16},{24,28},{28,24},{1,5},{5... | collective-permute-start | bytes 6291464 | tf_op jit(solution)/shard_map/ppermute | solution.py:1020
  480.4 33.7 %collective-permute-start.39 = (f32[512,512]{1,0:T(8,128)}, f32[512,512]{1,0:T(8,128)}, u32[]{:S(2)}, u32[]{:S(2)}) collective-permute-start(f32[512,512]{1,0:T(8,128)} %shard_map.311.refs_6_), channel_id=1, source_target_pairs={{0,8},{4,12},{8,16},{12,20},{16,24},{20,28},{24,0},{28,4},{1,9},{5... | collective-permute-start | bytes 3145736 | tf_op jit(solution)/shard_map/ppermute | solution.py:1024
  508.9 46.4 %collective-permute-start.37 = (f32[1032,256]{1,0:T(8,128)}, f32[1032,256]{1,0:T(8,128)}, u32[]{:S(2)}, u32[]{:S(2)}) collective-permute-start(f32[1032,256]{1,0:T(8,128)} %shard_map.315.refs_6_), channel_id=1, source_target_pairs={{0,8},{4,12},{8,16},{12,20},{16,24},{20,28},{24,0},{28,4},{1,9},{5... | collective-permute-start | bytes 3170312 | tf_op jit(solution)/shard_map/ppermute | solution.py:1024
  510.5 100.7 %collective-permute-start.44 = (f32[2,1032,256]{2,1,0:T(8,128)}, f32[2,1032,256]{2,1,0:T(8,128)}, u32[]{:S(2)}, u32[]{:S(2)}) collective-permute-start(f32[2,1032,256]{2,1,0:T(8,128)} %shard_map.310.refs_5_), channel_id=1, source_target_pairs={{0,4},{4,0},{8,12},{12,8},{16,20},{20,16},{24,28},{28,24},{1,5},{5... | collective-permute-start | bytes 6340616 | tf_op jit(solution)/shard_map/ppermute | solution.py:1020
  514.1 47.8 %collective-permute-start.34 = (f32[512,512]{1,0:T(8,128)}, f32[512,512]{1,0:T(8,128)}, u32[]{:S(2)}, u32[]{:S(2)}) collective-permute-start(f32[512,512]{1,0:T(8,128)} %shard_map.312.refs_5_), channel_id=1, source_target_pairs={{0,8},{4,12},{8,16},{12,20},{16,24},{20,28},{24,0},{28,4},{1,9},{5... | collective-permute-start | bytes 3145736 | tf_op jit(solution)/shard_map/ppermute | solution.py:1024
  560.3 51.0 %collective-permute-start.45 = (f32[1032,256]{1,0:T(8,128)}, f32[1032,256]{1,0:T(8,128)}, u32[]{:S(2)}, u32[]{:S(2)}) collective-permute-start(f32[1032,256]{1,0:T(8,128)} %shard_map.318.refs_6_), channel_id=1, source_target_pairs={{0,8},{4,12},{8,16},{12,20},{16,24},{20,28},{24,0},{28,4},{1,9},{5... | collective-permute-start | bytes 3170312 | tf_op jit(solution)/shard_map/ppermute | solution.py:1024
  561.9 42.6 %collective-permute-start.40 = (f32[256,512]{1,0:T(8,128)S(1)}, f32[256,512]{1,0:T(8,128)}, u32[]{:S(2)}, u32[]{:S(2)}) collective-permute-start(f32[256,512]{1,0:T(8,128)S(1)} %copy-done.6), channel_id=1, source_target_pairs={{0,4},{4,0},{8,12},{12,8},{16,20},{20,16},{24,28},{28,24},{1,5},{5... | collective-permute-start | bytes 1572872 | tf_op jit(solution)/shard_map/ppermute | solution.py:1020
  587.8 39.6 %collective-permute-start.43 = (f32[512,512]{1,0:T(8,128)}, f32[512,512]{1,0:T(8,128)}, u32[]{:S(2)}, u32[]{:S(2)}) collective-permute-start(f32[512,512]{1,0:T(8,128)} %shard_map.321.refs_2_), channel_id=1, source_target_pairs={{0,8},{4,12},{8,16},{12,20},{16,24},{20,28},{24,0},{28,4},{1,9},{5... | collective-permute-start | bytes 3145736 | tf_op jit(solution)/shard_map/ppermute | solution.py:1024
  616.2 33.8 %collective-permute-start.47 = (f32[1032,256]{1,0:T(8,128)}, f32[1032,256]{1,0:T(8,128)}, u32[]{:S(2)}, u32[]{:S(2)}) collective-permute-start(f32[1032,256]{1,0:T(8,128)} %shard_map.324.refs_2_), channel_id=1, source_target_pairs={{0,8},{4,12},{8,16},{12,20},{16,24},{20,28},{24,0},{28,4},{1,9},{5... | collective-permute-start | bytes 3170312 | tf_op jit(solution)/shard_map/ppermute | solution.py:1024
  617.8 53.3 %collective-permute-start.49 = (f32[1024,256]{1,0:T(8,128)}, f32[1024,256]{1,0:T(8,128)}, u32[]{:S(2)}, u32[]{:S(2)}) collective-permute-start(f32[1024,256]{1,0:T(8,128)} %shard_map.317.refs_7_), channel_id=1, source_target_pairs={{0,8},{4,12},{8,16},{12,20},{16,24},{20,28},{24,0},{28,4},{1,9},{5... | collective-permute-start | bytes 3145736 | tf_op jit(solution)/shard_map/ppermute | solution.py:1024
  (32 other events, 558.2 us)

commit v5 on v4

--- a/solution.py
+++ b/solution.py
@@ -2,6 +2,7 @@
 
 import jax
 import jax.numpy as jnp
+import numpy as np
 from jax import lax
 from jax.experimental import pallas as pl
 from jax.experimental.pallas import tpu as pltpu
@@ -32,12 +33,12 @@
 
 
 def angle_tables(length):
-    half_width = KEY // 2
-    column = jnp.arange(KEY, dtype=jnp.int32) // 2
-    frequency = jnp.power(10000.0, -column.astype(F32) / (half_width - 1))
-    inside = jnp.arange(BLOCK, dtype=jnp.int32).astype(F32)[:, None] * frequency[None, :]
-    starts = jnp.arange(0, length, BLOCK, dtype=jnp.int32).astype(F32)[:, None] * frequency[None, :]
-    return jnp.cos(inside), jnp.sin(inside), jnp.cos(starts), jnp.sin(starts)
+    column = np.arange(KEY) // 2
+    frequency = 10000.0 ** (-column / (KEY // 2 - 1))
+    inside = np.arange(BLOCK)[:, None] * frequency[None, :]
+    starts = np.arange(0, length, BLOCK)[:, None] * frequency[None, :]
+    tables = (np.cos(inside), np.sin(inside), np.cos(starts), np.sin(starts))
+    return tuple(jnp.asarray(table.astype(np.float32)) for table in tables)
 
 
 def rotate(values, cosines, sines, sign):

time: 685 us -> 682 us (level)
  no operation moved by 1% of the time
where the time goes in v5:
time: 682 us; the launch traced here: 673 us
  Pallas kernels  469 us (69%)
  waiting for transfers between devices  151 us (22%)
  starting transfers between devices  46.8 us (7%)
    pallas_call x70, Pallas kernels, call(): pl.pallas_call(body, out_shape=tuple(outs), grid_spec=pltpu.PrefetchScala...  469 us
    ppermute x24, waiting for transfers between devices, onward(): lax.ppermute(values, 'dp', [(i, (i + 2) % dp) for i in range(dp)])  67.3 us
    ppermute x16, waiting for transfers between devices, beside(): lax.ppermute(values, 'dp', [(i, i ^ 1) for i in range(dp)])  65.9 us
    ppermute x24, starting transfers between devices, onward(): lax.ppermute(values, 'dp', [(i, (i + 2) % dp) for i in range(dp)])  22.9 us
    ppermute x9, waiting for transfers between devices, across(): lax.ppermute(values, 'tensor', [(i, i ^ 2) for i in range(tensor)])  17.9 us
    ppermute x16, starting transfers between devices, beside(): lax.ppermute(values, 'dp', [(i, i ^ 1) for i in range(dp)])  14.1 us
  transfers between devices with their start and end apart: 50, of which 23 were waited for; matrix products, arithmetic and copies ran while one was open for 0% of the time, Pallas kernels for 66%

profile of v5, /device:TPU:0, one launch (start us, length us, event | category | flops | bytes accessed | tf_op | source)
XLA Modules:
  0.0 673.3 jit_solution(15418269323574533388)
XLA Ops:
  1.8 8.5 %shard_map.299 = (bf16[1024,2048]{1,0:T(8,128)(2,1)}, bf16[1024,512]{1,0:T(8,128)(2,1)}, bf16[1024,512]{1,0:T(8,128)(2,1)}, bf16[1024,1024]{1,0:T(8,128)(2,1)}, ...) custom-call(bf16[1024,2048]{1,0:T(8,128)(2,1)} %refs_2_.26, ...), custom_call_target="tpu_custom_call" | custom-call | flops 1 | bytes 1 | tf_op jit(solution)/shard_map/pallas_call | solution.py:109
  10.3 8.8 %shard_map.300 = (f32[128,2048]{1,0:T(8,128)}, bf16[1024,1024]{1,0:T(8,128)(2,1)}, f32[1024,1024]{1,0:T(8,128)}, bf16[2,256,256]{2,1,0:T(8,128)(2,1)}) custom-call(bf16[1024,512]{1,0:T(8,128)(2,1)} %get-tuple-element.102.refs_0_.refs_12_, bf16[1024,512]{1,0:T(8,128)(2,1)} %get-tuple-element.103.refs_1_.refs_13_, ...), custom_call_target="tpu_custom_call" | custom-call | flops 1 | bytes 1 | tf_op jit(solution)/shard_map/pallas_call | solution.py:109
  22.0 19.2 %shard_map.301 = (bf16[1024,2048]{1,0:T(8,128)(2,1)}, bf16[1024,512]{1,0:T(8,128)(2,1)}, bf16[1024,512]{1,0:T(8,128)(2,1)}, bf16[1024,1024]{1,0:T(8,128)(2,1)}, ...) custom-call(bf16[1024,2048]{1,0:T(8,128)(2,1)} %refs_2_.26, ...), custom_call_target="tpu_custom_call", output_to_operand_aliasing={{0}: (11, {}), {1}: (12, {}), {2}: (13, {}), {3}: (14, {}),... | custom-call | flops 1 | bytes 1 | tf_op jit(solution)/shard_map/pallas_call | solution.py:109
  42.7 8.8 %shard_map.302 = (f32[128,2048]{1,0:T(8,128)}, bf16[1024,1024]{1,0:T(8,128)(2,1)}, f32[1024,1024]{1,0:T(8,128)}, bf16[2,256,512]{2,1,0:T(8,128)(2,1)}) custom-call(bf16[1024,512]{1,0:T(8,128)(2,1)} %get-tuple-element.110.refs_0_.refs_1_, bf16[1024,512]{1,0:T(8,128)(2,1)} %get-tuple-element.111.refs_1_.refs_2_, ...), custom_call_target="tpu_custom_call", output_to_operand_aliasing={{1}: (7, {}), {2}: (8, {})} | custom-call | flops 1 | bytes 1 | tf_op jit(solution)/shard_map/pallas_call | solution.py:109
  52.1 10.7 %shard_map.303 = (bf16[1024,1024]{1,0:T(8,128)(2,1)}, bf16[1024,1024]{1,0:T(8,128)(2,1)}, bf16[1024,1024]{1,0:T(8,128)(2,1)}, bf16[1024,2048]{1,0:T(8,128)(2,1)}, f32[512,2048]{1,0:T(8,128)}) custom-call(f32[128,2048]{1,0:T(8,128)} %get-tuple-element.109.refs_19_.refs_0_, f32[128,2048]{1,0:T(8,128)} %collective-permute-done.refs_1_, ...), custom_call_target="tpu_custom_call" | custom-call | flops 1 | bytes 1 | tf_op jit(solution)/shard_map/pallas_call | solution.py:109
  62.8 9.3 %shard_map.304 = (f32[128,2048]{1,0:T(8,128)}, bf16[1024,1024]{1,0:T(8,128)(2,1)}, f32[1024,1024]{1,0:T(8,128)}, bf16[2,256,768]{2,1,0:T(8,128)(2,1)}) custom-call(bf16[1024,512]{1,0:T(8,128)(2,1)} %get-tuple-element.110.refs_0_.refs_1_, bf16[1024,512]{1,0:T(8,128)(2,1)} %get-tuple-element.111.refs_1_.refs_2_, ...), custom_call_target="tpu_custom_call", output_to_operand_aliasing={{1}: (7, {}), {2}: (8, {})} | custom-call | flops 1 | bytes 1 | tf_op jit(solution)/shard_map/pallas_call | solution.py:109
  73.6 9.6 %shard_map.305 = (f32[128,2048]{1,0:T(8,128)}, bf16[1024,1024]{1,0:T(8,128)(2,1)}, f32[1024,1024]{1,0:T(8,128)}, bf16[2,256,768]{2,1,0:T(8,128)(2,1)}) custom-call(bf16[1024,512]{1,0:T(8,128)(2,1)} %get-tuple-element.110.refs_0_.refs_1_, bf16[1024,512]{1,0:T(8,128)(2,1)} %get-tuple-element.111.refs_1_.refs_2_, ...), custom_call_target="tpu_custom_call", output_to_operand_aliasing={{1}: (7, {}), {2}: (8, {})} | custom-call | flops 1 | bytes 1 | tf_op jit(solution)/shard_map/pallas_call | solution.py:109
  84.4 10.7 %shard_map.306 = (bf16[1024,1024]{1,0:T(8,128)(2,1)}, bf16[1024,1024]{1,0:T(8,128)(2,1)}, bf16[1024,1024]{1,0:T(8,128)(2,1)}, bf16[1024,2048]{1,0:T(8,128)(2,1)}, f32[512,2048]{1,0:T(8,128)}) custom-call(f32[128,2048]{1,0:T(8,128)} %get-tuple-element.119.refs_9_.refs_0_, ...), custom_call_target="tpu_custom_call", output_to_operand_aliasing={{0}: (9, {}), {1}: (10, {}), {2}: (11, {}), {3}: (12, {}), ... | custom-call | flops 1 | bytes 1 | tf_op jit(solution)/shard_map/pallas_call | solution.py:109
  100.3 10.7 %shard_map.307 = (bf16[1024,1024]{1,0:T(8,128)(2,1)}, bf16[1024,1024]{1,0:T(8,128)(2,1)}, bf16[1024,1024]{1,0:T(8,128)(2,1)}, bf16[1024,2048]{1,0:T(8,128)(2,1)}, f32[512,2048]{1,0:T(8,128)}) custom-call(f32[128,2048]{1,0:T(8,128)} %get-tuple-element.123.refs_9_.refs_0_, ...), custom_call_target="tpu_custom_call", output_to_operand_aliasing={{0}: (9, {}), {1}: (10, {}), {2}: (11, {}), {3}: (12, {}), ... | custom-call | flops 1 | bytes 1 | tf_op jit(solution)/shard_map/pallas_call | solution.py:109
  111.0 11.2 %collective-permute-done.1.refs_1_ = f32[128,2048]{1,0:T(8,128)} collective-permute-done((f32[128,2048]{1,0:T(8,128)}, f32[128,2048]{1,0:T(8,128)}, u32[]{:S(2)}, u32[]{:S(2)}) %collective-permute-start.1) | collective-permute-done | bytes 1048608 | tf_op jit(solution)/shard_map/ppermute | solution.py:1029
  122.3 10.9 %shard_map.308 = (bf16[1024,1024]{1,0:T(8,128)(2,1)}, bf16[1024,1024]{1,0:T(8,128)(2,1)}, bf16[1024,1024]{1,0:T(8,128)(2,1)}, bf16[1024,2048]{1,0:T(8,128)(2,1)}, f32[512,2048]{1,0:T(8,128)}) custom-call(f32[128,2048]{1,0:T(8,128)} %get-tuple-element.124.refs_14_.refs_0_, ...), custom_call_target="tpu_custom_call", output_to_operand_aliasing={{0}: (9, {}), {1}: (10, {}), {2}: (11, {}), {3}: (12, {}), ... | custom-call | flops 1 | bytes 1 | tf_op jit(solution)/shard_map/pallas_call | solution.py:109
  144.1 11.1 %shard_map.311.refs_3_.refs_0_ = f32[256,2048]{1,0:T(8,128)} custom-call(bf16[1024,1024]{1,0:T(8,128)(2,1)} %get-tuple-element.140.refs_2_.refs_0_, bf16[1024,1024]{1,0:T(8,128)(2,1)} %get-tuple-element.141.refs_2_.refs_1_, bf16[2048,1024]{1,0:T(8,128)(2,1)} %refs_2_.21, bf16[2048,1024]{1,0:T(8,128)(2,1)} %refs_3_.5, f32[512,512]{1,0:T(8,128)} %shard_map.310.refs_4_), custom_call_target="tpu_custom_call" | custom-call | flops 1 | bytes 1 | tf_op jit(solution)/shard_map/pallas_call | solution.py:109
  173.1 11.2 %shard_map.315.refs_4_.refs_0_ = f32[256,2048]{1,0:T(8,128)} custom-call(bf16[1024,1024]{1,0:T(8,128)(2,1)} %get-tuple-element.140.refs_2_.refs_0_, bf16[1024,1024]{1,0:T(8,128)(2,1)} %get-tuple-element.141.refs_2_.refs_1_, bf16[2048,1024]{1,0:T(8,128)(2,1)} %refs_2_.21, bf16[2048,1024]{1,0:T(8,128)(2,1)} %refs_3_.5, f32[512,512]{1,0:T(8,128)} %shard_map.314.refs_4_), custom_call_target="tpu_custom_call" | custom-call | flops 1 | bytes 1 | tf_op jit(solution)/shard_map/pallas_call | solution.py:109
  198.0 10.0 %shard_map.318.refs_4_.refs_3_ = bf16[1024,2048]{1,0:T(8,128)(2,1)} custom-call(f32[512,2048]{1,0:T(8,128)} %collective-permute-done.10.refs_0_, f32[1,2048]{1,0:T(1,128)} %bitcast.19, f32[1,2048]{1,0:T(1,128)} %bitcast.28, f32[2,256,1024]{2,1,0:T(8,128)} %shard_map.317.refs_3_), custom_call_target="tpu_custom_call" | custom-call | flops 1 | bytes 1 | tf_op jit(solution)/shard_map/pallas_call | solution.py:109
  214.2 9.6 %collective-permute-done.8.refs_4_ = f32[256,1024]{1,0:T(8,128)} collective-permute-done((f32[256,1024]{1,0:T(8,128)}, f32[256,1024]{1,0:T(8,128)}, u32[]{:S(2)}, u32[]{:S(2)}) %collective-permute-start.8) | collective-permute-done | bytes 1048608 | tf_op jit(solution)/shard_map/ppermute | solution.py:1025
  229.6 9.2 %shard_map.321 = (bf16[1024,2048]{1,0:T(8,128)(2,1)}, f32[512,2048]{1,0:T(8,128)}, f32[1,2048]{1,0:T(1,128)}, f32[1,2048]{1,0:T(1,128)}) custom-call(f32[256,2048]{1,0:T(8,128)} %shard_map.311.refs_3_.refs_0_, f32[256,2048]{1,0:T(8,128)} %collective-permute-done.6.refs_1_, f32[512,2048]{1,0:T(8,128)} %get-tuple-element.143.refs_2_, f32[1,2048]{1,0:T(1,128)} %bitcast.15, ...), custom_call_target="tpu_custom_call" | custom-call | flops 1 | bytes 1 | tf_op jit(solution)/shard_map/pallas_call | solution.py:109
  248.5 9.2 %shard_map.324 = (bf16[1024,2048]{1,0:T(8,128)(2,1)}, f32[512,2048]{1,0:T(8,128)}, f32[1,2048]{1,0:T(1,128)}, f32[1,2048]{1,0:T(1,128)}) custom-call(f32[256,2048]{1,0:T(8,128)} %shard_map.315.refs_4_.refs_0_, f32[256,2048]{1,0:T(8,128)} %collective-permute-done.5.refs_1_, ...), custom_call_target="tpu_custom_call", output_to_operand_aliasing={{0}: (5, {}), {1}: (6, {})} | custom-call | flops 1 | bytes 1 | tf_op jit(solution)/shard_map/pallas_call | solution.py:109
  261.1 14.3 %shard_map.326 = (bf16[1024,1024]{1,0:T(8,128)(2,1)}, bf16[1024,1024]{1,0:T(8,128)(2,1)}, f32[1024,512]{1,0:T(8,128)}) custom-call(s32[3]{0:T(128)} %pad_add_fusion.refs_0_, bf16[1024,2048]{1,0:T(8,128)(2,1)} %get-tuple-element.147.refs_4_.refs_1_.refs_2_, bf16[1024,2048]{1,0:T(8,128)(2,1)} %refs_2_.23, f32[1024,1024]{1,0:T(8,128)} %get-tuple-element.148.refs_3_, ...), custom_call_target="tpu_custom_call" | custom-call | flops 1 | bytes 1 | tf_op jit(solution)/shard_map/pallas_call | solution.py:109
  275.4 14.7 %shard_map.327 = (bf16[1024,512]{1,0:T(8,128)(2,1)}, bf16[1024,512]{1,0:T(8,128)(2,1)}, bf16[1024,1024]{1,0:T(8,128)(2,1)}, bf16[1024,1024]{1,0:T(8,128)(2,1)}, ...) custom-call(s32[3]{0:T(128)} %pad_add_fusion.refs_0_, bf16[1024,512]{1,0:T(8,128)(2,1)} %get-tuple-element.110.refs_0_.refs_1_, ...), custom_call_target="tpu_custom_call" | custom-call | flops 1 | bytes 1 | tf_op jit(solution)/shard_map/pallas_call | solution.py:109
  312.0 13.8 %shard_map.331.refs_5_.refs_0_ = f32[256,2048]{1,0:T(8,128)} custom-call(bf16[1024,512]{1,0:T(8,128)(2,1)} %get-tuple-element.158.refs_5_.refs_0_, bf16[1024,512]{1,0:T(8,128)(2,1)} %get-tuple-element.159.refs_1_, bf16[1024,1024]{1,0:T(8,128)(2,1)} %get-tuple-element.160.refs_2_, bf16[1024,1024]{1,0:T(8,128)(2,1)} %get-tuple-element.149.refs_3_.refs_2_, ...), custom_call_target="tpu_custom_call" | custom-call | flops 1 | bytes 1 | tf_op jit(solution)/shard_map/pallas_call | solution.py:109
  334.2 10.1 %collective-permute-done.20.refs_4_ = f32[1024,512]{1,0:T(8,128)} collective-permute-done((f32[1024,512]{1,0:T(8,128)}, f32[1024,512]{1,0:T(8,128)}, u32[]{:S(2)}, u32[]{:S(2)}) %collective-permute-start.20) | collective-permute-done | bytes 2097184 | tf_op jit(solution)/shard_map/ppermute | solution.py:1021
  354.6 13.8 %shard_map.334.refs_6_.refs_0_ = f32[256,2048]{1,0:T(8,128)} custom-call(bf16[1024,512]{1,0:T(8,128)(2,1)} %get-tuple-element.158.refs_5_.refs_0_, bf16[1024,512]{1,0:T(8,128)(2,1)} %get-tuple-element.159.refs_1_, bf16[1024,1024]{1,0:T(8,128)(2,1)} %get-tuple-element.160.refs_2_, bf16[1024,1024]{1,0:T(8,128)(2,1)} %get-tuple-element.149.refs_3_.refs_2_, ...), custom_call_target="tpu_custom_call" | custom-call | flops 1 | bytes 1 | tf_op jit(solution)/shard_map/pallas_call | solution.py:109
  370.0 7.3 %collective-permute-done.22.refs_5_ = f32[512,512]{1,0:T(8,128)} collective-permute-done((f32[512,512]{1,0:T(8,128)}, f32[512,512]{1,0:T(8,128)}, u32[]{:S(2)}, u32[]{:S(2)}) %collective-permute-start.22) | collective-permute-done | bytes 1048608 | tf_op jit(solution)/shard_map/ppermute | solution.py:1025
  383.2 9.1 %shard_map.336 = (f32[1024,2048]{1,0:T(8,128)}, f32[1,2048]{1,0:T(1,128)}, f32[1,2048]{1,0:T(1,128)}) custom-call(f32[256,2048]{1,0:T(8,128)} %shard_map.331.refs_5_.refs_0_, f32[256,2048]{1,0:T(8,128)} %collective-permute-done.19.refs_1_, bf16[1024,2048]{1,0:T(8,128)(2,1)} %refs_2_.26, f32[1,2048]{1,0:T(1,128)} %bitcast.20, ...), custom_call_target="tpu_custom_call" | custom-call | flops 1 | bytes 1 | tf_op jit(solution)/shard_map/pallas_call | solution.py:109
  401.4 12.8 %shard_map.338.refs_6_.refs_0_ = f32[512,2048]{1,0:T(8,128)} custom-call(bf16[1024,1024]{1,0:T(8,128)(2,1)} %get-tuple-element.139.refs_3_.refs_1_.refs_0_, bf16[1024,2048]{1,0:T(8,128)(2,1)} %refs_1_.1, f32[512,512]{1,0:T(8,128)} %shard_map.337.refs_2_), custom_call_target="tpu_custom_call" | custom-call | flops 1 | bytes 1 | tf_op jit(solution)/shard_map/pallas_call | solution.py:109
  414.2 5.7 shard_map.339.refs_5_
  425.3 9.3 %shard_map.341 = (f32[1024,2048]{1,0:T(8,128)}, f32[1,2048]{1,0:T(1,128)}, f32[1,2048]{1,0:T(1,128)}) custom-call(f32[256,2048]{1,0:T(8,128)} %shard_map.334.refs_6_.refs_0_, f32[256,2048]{1,0:T(8,128)} %collective-permute-done.27.refs_1_, bf16[1024,2048]{1,0:T(8,128)(2,1)} %refs_2_.26, f32[1,2048]{1,0:T(1,128)} %bitcast.21, ...), custom_call_target="tpu_custom_call", output_to_operand_aliasing={{0}: (5, {})} | custom-call | flops 1 | bytes 1 | tf_op jit(solution)/shard_map/pallas_call | solution.py:109
  517.1 29.7 %collective-permute-done.38.refs_3_ = f32[2,1024,256]{2,1,0:T(8,128)} collective-permute-done((f32[2,1024,256]{2,1,0:T(8,128)}, f32[2,1024,256]{2,1,0:T(8,128)}, u32[]{:S(2)}, u32[]{:S(2)}) %collective-permute-start.38) | collective-permute-done | bytes 2097184 | tf_op jit(solution)/shard_map/ppermute | solution.py:1021
  565.5 10.7 %shard_map.356.refs_6_.refs_0_ = bf16[1024,2048]{1,0:T(8,128)(2,1)} custom-call(f32[512,2048]{1,0:T(8,128)} %shard_map.338.refs_6_.refs_0_, f32[512,2048]{1,0:T(8,128)} %collective-permute-done.25.refs_1_, f32[512,2048]{1,0:T(8,128)} %get-tuple-element.143.refs_2_, f32[256,512]{1,0:T(8,128)} %get-tuple-element.178.refs_3_), custom_call_target="tpu_custom_call" | custom-call | flops 1 | bytes 1 | tf_op jit(solution)/shard_map/pallas_call | solution.py:109
  585.5 16.4 %collective-permute-done.40.refs_0_ = f32[256,512]{1,0:T(8,128)} collective-permute-done((f32[256,512]{1,0:T(8,128)S(1)}, f32[256,512]{1,0:T(8,128)}, u32[]{:S(2)}, u32[]{:S(2)}) %collective-permute-start.40) | collective-permute-done | bytes 524320 | tf_op jit(solution)/shard_map/ppermute | solution.py:1021
  635.4 12.1 %collective-permute-done.47.refs_6_ = f32[1032,256]{1,0:T(8,128)} collective-permute-done((f32[1032,256]{1,0:T(8,128)}, f32[1032,256]{1,0:T(8,128)}, u32[]{:S(2)}, u32[]{:S(2)}) %collective-permute-start.47) | collective-permute-done | bytes 1056800 | tf_op jit(solution)/shard_map/ppermute | solution.py:1025
  658.1 7.1 %shard_map.367.refs_5_ = f32[1024,2048]{1,0:T(8,128)} custom-call(f32[1024,2048]{1,0:T(8,128)} %get-tuple-element.165.refs_6_.refs_0_, f32[256,1024]{1,0:T(8,128)} %shard_map.366.refs_1_), custom_call_target="tpu_custom_call" | custom-call | flops 1 | bytes 1 | tf_op jit(solution)/shard_map/pallas_call | solution.py:109
  (175 shorter events, 306.3 us)
Async XLA Ops:
  41.1 150.4 %collective-permute-start.10 = (f32[512,2048]{1,0:T(8,128)}, f32[512,2048]{1,0:T(8,128)}, u32[]{:S(2)}, u32[]{:S(2)}) collective-permute-start(f32[512,2048]{1,0:T(8,128)} %get-tuple-element.144), channel_id=1, source_target_pairs={{0,4},{4,0},{8,12},{12,8},{16,20},{20,16},{24,28},{28,24},{1,5},{5... | collective-permute-start | bytes 12582920 | tf_op jit(solution)/shard_map/ppermute | solution.py:1021
  83.2 39.0 %collective-permute-start.1 = (f32[128,2048]{1,0:T(8,128)}, f32[128,2048]{1,0:T(8,128)}, u32[]{:S(2)}, u32[]{:S(2)}) collective-permute-start(f32[128,2048]{1,0:T(8,128)} %get-tuple-element.124.refs_14_.refs_0_), channel_id=1, source_target_pairs={{0,2},{1,3},{2,0},{3,1},{4,6},{5,7},{6,4},{7,5},{8,10},{9,11},{10,... | collective-permute-start | bytes 3145736 | tf_op jit(solution)/shard_map/ppermute | solution.py:1029
  138.1 48.9 %collective-permute-start.7 = (f32[2,256,1024]{2,1,0:T(8,128)}, f32[2,256,1024]{2,1,0:T(8,128)}, u32[]{:S(2)}, u32[]{:S(2)}) collective-permute-start(f32[2,256,1024]{2,1,0:T(8,128)} %shard_map.309.refs_3_), channel_id=1, source_target_pairs={{0,4},{4,0},{8,12},{12,8},{16,20},{20,16},{24,28},{28,24},{1,5},{5... | collective-permute-start | bytes 6291464 | tf_op jit(solution)/shard_map/ppermute | solution.py:1021
  155.3 58.4 %collective-permute-start.6 = (f32[256,2048]{1,0:T(8,128)}, f32[256,2048]{1,0:T(8,128)}, u32[]{:S(2)}, u32[]{:S(2)}) collective-permute-start(f32[256,2048]{1,0:T(8,128)} %shard_map.311.refs_3_.refs_0_), channel_id=1, source_target_pairs={{0,2},{1,3},{2,0},{3,1},{4,6},{5,7},{6,4},{7,5},{8,10},{9,11},{10,... | collective-permute-start | bytes 6291464 | tf_op jit(solution)/shard_map/ppermute | solution.py:1029
  164.7 77.9 %collective-permute-start.11 = (f32[2,1024,256]{2,1,0:T(8,128)}, f32[2,1024,256]{2,1,0:T(8,128)}, u32[]{:S(2)}, u32[]{:S(2)}) collective-permute-start(f32[2,1024,256]{2,1,0:T(8,128)} %shard_map.312.refs_3_), channel_id=1, source_target_pairs={{0,4},{4,0},{8,12},{12,8},{16,20},{20,16},{24,28},{28,24},{1,5},{5... | collective-permute-start | bytes 6291464 | tf_op jit(solution)/shard_map/ppermute | solution.py:1021
  173.1 35.0 %collective-permute-start.9 = (f32[512,512]{1,0:T(8,128)}, f32[512,512]{1,0:T(8,128)}, u32[]{:S(2)}, u32[]{:S(2)}) collective-permute-start(f32[512,512]{1,0:T(8,128)} %shard_map.314.refs_4_), channel_id=1, source_target_pairs={{0,8},{4,12},{8,16},{12,20},{16,24},{20,28},{24,0},{28,4},{1,9},{5... | collective-permute-start | bytes 3145736 | tf_op jit(solution)/shard_map/ppermute | solution.py:1025
  187.0 61.5 %collective-permute-start.5 = (f32[256,2048]{1,0:T(8,128)}, f32[256,2048]{1,0:T(8,128)}, u32[]{:S(2)}, u32[]{:S(2)}) collective-permute-start(f32[256,2048]{1,0:T(8,128)} %shard_map.315.refs_4_.refs_0_), channel_id=1, source_target_pairs={{0,2},{1,3},{2,0},{3,1},{4,6},{5,7},{6,4},{7,5},{8,10},{9,11},{10,... | collective-permute-start | bytes 6291464 | tf_op jit(solution)/shard_map/ppermute | solution.py:1029
  212.1 34.9 %collective-permute-start.12 = (f32[512,512]{1,0:T(8,128)}, f32[512,512]{1,0:T(8,128)}, u32[]{:S(2)}, u32[]{:S(2)}) collective-permute-start(f32[512,512]{1,0:T(8,128)} %shard_map.319.refs_5_), channel_id=1, source_target_pairs={{0,8},{4,12},{8,16},{12,20},{16,24},{20,28},{24,0},{28,4},{1,9},{5... | collective-permute-start | bytes 3145736 | tf_op jit(solution)/shard_map/ppermute | solution.py:1025
  213.6 44.1 %collective-permute-start.13 = (f32[2,256,512]{2,1,0:T(8,128)}, f32[2,256,512]{2,1,0:T(8,128)}, u32[]{:S(2)}, u32[]{:S(2)}) collective-permute-start(f32[2,256,512]{2,1,0:T(8,128)} %shard_map.313.refs_4_), channel_id=1, source_target_pairs={{0,4},{4,0},{8,12},{12,8},{16,20},{20,16},{24,28},{28,24},{1,5},{5... | collective-permute-start | bytes 3145736 | tf_op jit(solution)/shard_map/ppermute | solution.py:1021
  223.7 75.6 %collective-permute-start.16 = (f32[2,256,1024]{2,1,0:T(8,128)}, f32[2,256,1024]{2,1,0:T(8,128)}, u32[]{:S(2)}, u32[]{:S(2)}) collective-permute-start(f32[2,256,1024]{2,1,0:T(8,128)} %shard_map.317.refs_3_), channel_id=1, source_target_pairs={{0,4},{4,0},{8,12},{12,8},{16,20},{20,16},{24,28},{28,24},{1,5},{5... | collective-permute-start | bytes 6291464 | tf_op jit(solution)/shard_map/ppermute | solution.py:1021
  242.6 56.7 %collective-permute-start.17 = (f32[256,1024]{1,0:T(8,128)}, f32[256,1024]{1,0:T(8,128)}, u32[]{:S(2)}, u32[]{:S(2)}) collective-permute-start(f32[256,1024]{1,0:T(8,128)} %shard_map.320.refs_5_), channel_id=1, source_target_pairs={{0,8},{4,12},{8,16},{12,20},{16,24},{20,28},{24,0},{28,4},{1,9},{5... | collective-permute-start | bytes 3145736 | tf_op jit(solution)/shard_map/ppermute | solution.py:1025
  247.0 46.3 %collective-permute-start.18 = (f32[1024,256]{1,0:T(8,128)}, f32[1024,256]{1,0:T(8,128)}, u32[]{:S(2)}, u32[]{:S(2)}) collective-permute-start(f32[1024,256]{1,0:T(8,128)} %shard_map.323.refs_7_), channel_id=1, source_target_pairs={{0,8},{4,12},{8,16},{12,20},{16,24},{20,28},{24,0},{28,4},{1,9},{5... | collective-permute-start | bytes 3145736 | tf_op jit(solution)/shard_map/ppermute | solution.py:1025
  290.2 54.1 %collective-permute-start.20 = (f32[1024,512]{1,0:T(8,128)}, f32[1024,512]{1,0:T(8,128)}, u32[]{:S(2)}, u32[]{:S(2)}) collective-permute-start(f32[1024,512]{1,0:T(8,128)} %get-tuple-element.163), channel_id=1, source_target_pairs={{0,4},{4,0},{8,12},{12,8},{16,20},{20,16},{24,28},{28,24},{1,5},{5... | collective-permute-start | bytes 6291464 | tf_op jit(solution)/shard_map/ppermute | solution.py:1021
  325.8 57.0 %collective-permute-start.19 = (f32[256,2048]{1,0:T(8,128)}, f32[256,2048]{1,0:T(8,128)}, u32[]{:S(2)}, u32[]{:S(2)}) collective-permute-start(f32[256,2048]{1,0:T(8,128)} %shard_map.331.refs_5_.refs_0_), channel_id=1, source_target_pairs={{0,2},{1,3},{2,0},{3,1},{4,6},{5,7},{6,4},{7,5},{8,10},{9,11},{10,... | collective-permute-start | bytes 6291464 | tf_op jit(solution)/shard_map/ppermute | solution.py:1029
  326.4 65.9 %collective-permute-start.14 = (f32[1024,512]{1,0:T(8,128)}, f32[1024,512]{1,0:T(8,128)}, u32[]{:S(2)}, u32[]{:S(2)}) collective-permute-start(f32[1024,512]{1,0:T(8,128)} %get-tuple-element.150), channel_id=1, source_target_pairs={{0,4},{4,0},{8,12},{12,8},{16,20},{20,16},{24,28},{28,24},{1,5},{5... | collective-permute-start | bytes 6291464 | tf_op jit(solution)/shard_map/ppermute | solution.py:1021
  368.4 56.9 %collective-permute-start.27 = (f32[256,2048]{1,0:T(8,128)}, f32[256,2048]{1,0:T(8,128)}, u32[]{:S(2)}, u32[]{:S(2)}) collective-permute-start(f32[256,2048]{1,0:T(8,128)} %shard_map.334.refs_6_.refs_0_), channel_id=1, source_target_pairs={{0,2},{1,3},{2,0},{3,1},{4,6},{5,7},{6,4},{7,5},{8,10},{9,11},{10,... | collective-permute-start | bytes 6291464 | tf_op jit(solution)/shard_map/ppermute | solution.py:1029
  382.8 38.0 %collective-permute-start.28 = (f32[2,256,512]{2,1,0:T(8,128)}, f32[2,256,512]{2,1,0:T(8,128)}, u32[]{:S(2)}, u32[]{:S(2)}) collective-permute-start(f32[2,256,512]{2,1,0:T(8,128)} %shard_map.322.refs_4_), channel_id=1, source_target_pairs={{0,4},{4,0},{8,12},{12,8},{16,20},{20,16},{24,28},{28,24},{1,5},{5... | collective-permute-start | bytes 3145736 | tf_op jit(solution)/shard_map/ppermute | solution.py:1021
  398.2 38.2 %collective-permute-start.26 = (f32[512,512]{1,0:T(8,128)}, f32[512,512]{1,0:T(8,128)}, u32[]{:S(2)}, u32[]{:S(2)}) collective-permute-start(f32[512,512]{1,0:T(8,128)} %shard_map.337.refs_2_), channel_id=1, source_target_pairs={{0,8},{4,12},{8,16},{12,20},{16,24},{20,28},{24,0},{28,4},{1,9},{5... | collective-permute-start | bytes 3145736 | tf_op jit(solution)/shard_map/ppermute | solution.py:1025
  400.0 66.3 %collective-permute-start.31 = (f32[1024,512]{1,0:T(8,128)}, f32[1024,512]{1,0:T(8,128)}, u32[]{:S(2)}, u32[]{:S(2)}) collective-permute-start(f32[1024,512]{1,0:T(8,128)} %get-tuple-element.166), channel_id=1, source_target_pairs={{0,4},{4,0},{8,12},{12,8},{16,20},{20,16},{24,28},{28,24},{1,5},{5... | collective-permute-start | bytes 6291464 | tf_op jit(solution)/shard_map/ppermute | solution.py:1021
  419.9 35.5 %collective-permute-start.33 = (f32[512,512]{1,0:T(8,128)}, f32[512,512]{1,0:T(8,128)}, u32[]{:S(2)}, u32[]{:S(2)}) collective-permute-start(f32[512,512]{1,0:T(8,128)} %shard_map.339.refs_5_), channel_id=1, source_target_pairs={{0,8},{4,12},{8,16},{12,20},{16,24},{20,28},{24,0},{28,4},{1,9},{5... | collective-permute-start | bytes 3145736 | tf_op jit(solution)/shard_map/ppermute | solution.py:1025
  420.8 144.7 %collective-permute-start.25 = (f32[512,2048]{1,0:T(8,128)}, f32[512,2048]{1,0:T(8,128)}, u32[]{:S(2)}, u32[]{:S(2)}) collective-permute-start(f32[512,2048]{1,0:T(8,128)} %shard_map.338.refs_6_.refs_0_), channel_id=1, source_target_pairs={{0,2},{1,3},{2,0},{3,1},{4,6},{5,7},{6,4},{7,5},{8,10},{9,11},{10,... | collective-permute-start | bytes 12582920 | tf_op jit(solution)/shard_map/ppermute | solution.py:1029
  447.7 54.2 %collective-permute-start.35 = (f32[2,1032,256]{2,1,0:T(8,128)}, f32[2,1032,256]{2,1,0:T(8,128)}, u32[]{:S(2)}, u32[]{:S(2)}) collective-permute-start(f32[2,1032,256]{2,1,0:T(8,128)} %shard_map.343.refs_6_), channel_id=1, source_target_pairs={{0,4},{4,0},{8,12},{12,8},{16,20},{20,16},{24,28},{28,24},{1,5},{5... | collective-permute-start | bytes 6340616 | tf_op jit(solution)/shard_map/ppermute | solution.py:1021
  466.2 80.6 %collective-permute-start.38 = (f32[2,1024,256]{2,1,0:T(8,128)}, f32[2,1024,256]{2,1,0:T(8,128)}, u32[]{:S(2)}, u32[]{:S(2)}) collective-permute-start(f32[2,1024,256]{2,1,0:T(8,128)} %shard_map.345.refs_5_), channel_id=1, source_target_pairs={{0,4},{4,0},{8,12},{12,8},{16,20},{20,16},{24,28},{28,24},{1,5},{5... | collective-permute-start | bytes 6291464 | tf_op jit(solution)/shard_map/ppermute | solution.py:1021
  477.9 33.7 %collective-permute-start.39 = (f32[512,512]{1,0:T(8,128)}, f32[512,512]{1,0:T(8,128)}, u32[]{:S(2)}, u32[]{:S(2)}) collective-permute-start(f32[512,512]{1,0:T(8,128)} %shard_map.347.refs_6_), channel_id=1, source_target_pairs={{0,8},{4,12},{8,16},{12,20},{16,24},{20,28},{24,0},{28,4},{1,9},{5... | collective-permute-start | bytes 3145736 | tf_op jit(solution)/shard_map/ppermute | solution.py:1025
  506.4 46.4 %collective-permute-start.37 = (f32[1032,256]{1,0:T(8,128)}, f32[1032,256]{1,0:T(8,128)}, u32[]{:S(2)}, u32[]{:S(2)}) collective-permute-start(f32[1032,256]{1,0:T(8,128)} %shard_map.351.refs_6_), channel_id=1, source_target_pairs={{0,8},{4,12},{8,16},{12,20},{16,24},{20,28},{24,0},{28,4},{1,9},{5... | collective-permute-start | bytes 3170312 | tf_op jit(solution)/shard_map/ppermute | solution.py:1025
  507.9 100.8 %collective-permute-start.44 = (f32[2,1032,256]{2,1,0:T(8,128)}, f32[2,1032,256]{2,1,0:T(8,128)}, u32[]{:S(2)}, u32[]{:S(2)}) collective-permute-start(f32[2,1032,256]{2,1,0:T(8,128)} %shard_map.346.refs_5_), channel_id=1, source_target_pairs={{0,4},{4,0},{8,12},{12,8},{16,20},{20,16},{24,28},{28,24},{1,5},{5... | collective-permute-start | bytes 6340616 | tf_op jit(solution)/shard_map/ppermute | solution.py:1021
  511.6 47.7 %collective-permute-start.34 = (f32[512,512]{1,0:T(8,128)}, f32[512,512]{1,0:T(8,128)}, u32[]{:S(2)}, u32[]{:S(2)}) collective-permute-start(f32[512,512]{1,0:T(8,128)} %shard_map.348.refs_5_), channel_id=1, source_target_pairs={{0,8},{4,12},{8,16},{12,20},{16,24},{20,28},{24,0},{28,4},{1,9},{5... | collective-permute-start | bytes 3145736 | tf_op jit(solution)/shard_map/ppermute | solution.py:1025
  557.7 51.0 %collective-permute-start.45 = (f32[1032,256]{1,0:T(8,128)}, f32[1032,256]{1,0:T(8,128)}, u32[]{:S(2)}, u32[]{:S(2)}) collective-permute-start(f32[1032,256]{1,0:T(8,128)} %shard_map.354.refs_6_), channel_id=1, source_target_pairs={{0,8},{4,12},{8,16},{12,20},{16,24},{20,28},{24,0},{28,4},{1,9},{5... | collective-permute-start | bytes 3170312 | tf_op jit(solution)/shard_map/ppermute | solution.py:1025
  559.3 42.6 %collective-permute-start.40 = (f32[256,512]{1,0:T(8,128)S(1)}, f32[256,512]{1,0:T(8,128)}, u32[]{:S(2)}, u32[]{:S(2)}) collective-permute-start(f32[256,512]{1,0:T(8,128)S(1)} %copy-done.6), channel_id=1, source_target_pairs={{0,4},{4,0},{8,12},{12,8},{16,20},{20,16},{24,28},{28,24},{1,5},{5... | collective-permute-start | bytes 1572872 | tf_op jit(solution)/shard_map/ppermute | solution.py:1021
  585.3 39.6 %collective-permute-start.43 = (f32[512,512]{1,0:T(8,128)}, f32[512,512]{1,0:T(8,128)}, u32[]{:S(2)}, u32[]{:S(2)}) collective-permute-start(f32[512,512]{1,0:T(8,128)} %shard_map.357.refs_2_), channel_id=1, source_target_pairs={{0,8},{4,12},{8,16},{12,20},{16,24},{20,28},{24,0},{28,4},{1,9},{5... | collective-permute-start | bytes 3145736 | tf_op jit(solution)/shard_map/ppermute | solution.py:1025
  613.6 33.8 %collective-permute-start.47 = (f32[1032,256]{1,0:T(8,128)}, f32[1032,256]{1,0:T(8,128)}, u32[]{:S(2)}, u32[]{:S(2)}) collective-permute-start(f32[1032,256]{1,0:T(8,128)} %shard_map.360.refs_2_), channel_id=1, source_target_pairs={{0,8},{4,12},{8,16},{12,20},{16,24},{20,28},{24,0},{28,4},{1,9},{5... | collective-permute-start | bytes 3170312 | tf_op jit(solution)/shard_map/ppermute | solution.py:1025
  615.2 53.3 %collective-permute-start.49 = (f32[1024,256]{1,0:T(8,128)}, f32[1024,256]{1,0:T(8,128)}, u32[]{:S(2)}, u32[]{:S(2)}) collective-permute-start(f32[1024,256]{1,0:T(8,128)} %shard_map.353.refs_7_), channel_id=1, source_target_pairs={{0,8},{4,12},{8,16},{12,20},{16,24},{20,28},{24,0},{28,4},{1,9},{5... | collective-permute-start | bytes 3145736 | tf_op jit(solution)/shard_map/ppermute | solution.py:1025
  (32 other events, 557.5 us)
